TPU v7x, 32 devices: a whole 2x2x4 slice. The times are simulated.
32 devices in a mesh: node: 8 (over y, x, core), col: 4 (over z).
Axes of the slice: x: 2, y: 2, z: 4, core: 2. Of those that a mesh axis runs over, the one named last changes fastest.
Arguments:
- features: float32 [128, 8192], P('col', 'node'), may hold values from -6 to 6
- tiles: float32 [64, 64, 128, 128], P('node'), may hold values from -0.0625 to 0.0625
- tile_column: int32 [64, 64], P('node'), may hold values from 0 to 63, as said below
- tile_count: int32 [64], P('node'), may hold values from 1 to 64
- labels: int32 [8192], P('node'), may hold values from 0 to 171
- train_mask: int32 [8192], P('node'), may hold values from 0 to 1
- weight_in: float32 [128, 256], P('col'), may hold values from -0.5 to 0.5
- bias_in: float32 [256], P('col'), may hold values from -3 to 3
- weight_out: float32 [256, 172], P('col'), may hold values from -0.75 to 0.75
- bias_out: float32 [172], replicated, may hold values from -4 to 304
Outputs:
- logits: float32 [172, 8192], P(None, 'node')
- mean_loss: float32 [], replicated
- grad_weight_in: float32 [128, 256], P('col')
- grad_bias_in: float32 [256], P('col')
- grad_weight_out: float32 [256, 172], P('col')
- grad_bias_out: float32 [172], replicated
Inputs may be any that keep to these rules, and one draw needn't show every extreme that they name: `tile_column`: slot 0 of block row r names block column r; live slots mostly name block columns of the same 1024 nodes or of nearby ones, a few name any block column.
All inputs are finite; a program needn't handle non-finite values.
Results may differ from a plain program's by a relative error of at most 0.0003.
Values sent between devices are 32-bit elements; how exact they have to be, the bound alone decides.
No kernel may reach another device: no remote copies, remote signals or barrier semaphores. Data moves between devices by JAX's collectives and lax.ppermute only.
A program may use at most 128 MiB of HBM per device.

v0:
```python
import jax
import jax.numpy as jnp
from jax import lax
from jax.sharding import PartitionSpec as P

BLOCK = 128


precise = lax.Precision.HIGHEST


def dot_first(left, right):
    return lax.dot_general(
        left, right, (((0,), (0,)), ((), ())), precision=precise, preferred_element_type=jnp.float32
    )


def dot_last(left, right):
    return lax.dot_general(
        left, right, (((1,), (1,)), ((), ())), precision=precise, preferred_element_type=jnp.float32
    )


def on_device(
    features,
    tiles,
    tile_column,
    tile_count,
    labels,
    train_mask,
    weight_in,
    bias_in,
    weight_out,
    bias_out,
):
    local_rows = labels.shape[0]
    slot_total = tile_column.shape[1]
    live_slots = (jnp.arange(slot_total, dtype=jnp.int32)[None, :] < tile_count[:, None]).astype(
        jnp.float32
    )
    block_total = lax.axis_size("node") * tile_column.shape[0]
    flat_columns = tile_column.reshape(-1)

    def gather_blocks(values):
        channel_count = values.shape[0]
        block_view = values.reshape(channel_count, -1, BLOCK)
        picked = block_view[:, tile_column] * live_slots[None, :, :, None]
        mixed = jnp.einsum("frkj,rkij->fri", picked, tiles, precision=precise)
        return mixed.reshape(channel_count, local_rows)

    feature_all = lax.all_gather(features, "node", axis=1, tiled=True)
    mixed_in = gather_blocks(feature_all)
    inner_act = (
        lax.psum_scatter(dot_first(weight_in, mixed_in), "col", scatter_dimension=0, tiled=True)
        + bias_in[:, None]
    )
    hidden, activation_back = jax.vjp(
        lambda values: jax.nn.gelu(values, approximate=True), inner_act
    )
    class_total = weight_out.shape[1]
    hidden_all = lax.all_gather(hidden, "node", axis=1, tiled=True)
    mixed_out = gather_blocks(hidden_all)
    logits = lax.psum(dot_first(weight_out, mixed_out), "col") + bias_out[:, None]
    log_total = jax.nn.logsumexp(logits, axis=0)
    label_table = (jnp.arange(class_total, dtype=jnp.int32)[:, None] == labels[None, :]).astype(
        jnp.float32
    )
    train_weight = train_mask.astype(jnp.float32)
    cross_entropy = log_total - jnp.sum(label_table * logits, axis=0)
    loss_total, train_count = lax.psum(
        (jnp.sum(train_weight * cross_entropy), jnp.sum(train_weight)), "node"
    )
    mean_loss = loss_total / jnp.maximum(train_count, 1.0)
    logit_grad = train_weight[None, :] * (jnp.exp(logits - log_total[None, :]) - label_table)
    out_bias_part = jnp.sum(logit_grad, axis=1)
    out_weight_part = dot_last(mixed_out, logit_grad)
    local_grad = jnp.dot(
        weight_out, logit_grad, precision=precise, preferred_element_type=jnp.float32
    )
    channel_count = local_grad.shape[0]
    grad_blocks = local_grad.reshape(channel_count, -1, BLOCK)
    term_blocks = (
        jnp.einsum("fri,rkij->frkj", grad_blocks, tiles, precision=precise)
        * live_slots[None, :, :, None]
    )
    summed = jnp.zeros((channel_count, block_total, BLOCK), jnp.float32)
    summed = summed.at[:, flat_columns].add(term_blocks.reshape(channel_count, -1, BLOCK))
    hidden_grad = lax.psum_scatter(
        summed.reshape(channel_count, block_total * BLOCK), "node", scatter_dimension=1, tiled=True
    )
    out_weight, out_bias = lax.psum((out_weight_part, out_bias_part), "node")
    inner_grad = activation_back(hidden_grad)[0]
    in_bias_part = jnp.sum(inner_grad, axis=1)
    inner_all = lax.all_gather(inner_grad, "col", axis=0, tiled=True)
    in_weight_part = dot_last(mixed_in, inner_all)
    in_weight, in_bias = lax.psum((in_weight_part, in_bias_part), "node")
    return (logits, mean_loss, in_weight, in_bias, out_weight, out_bias)


def solution(mesh):
    in_specs = (
        P("col", "node"),
        P("node", None, None, None),
        P("node", None),
        P("node"),
        P("node"),
        P("node"),
        P("col", None),
        P("col"),
        P("col", None),
        P(),
    )
    out_specs = (P(None, "node"), P(), P("col", None), P("col"), P("col", None), P())
    return jax.shard_map(
        on_device, mesh=mesh, in_specs=in_specs, out_specs=out_specs, check_vma=False
    )
```

profile of v0, /device:TPU:0, one launch (start us, length us, event | category | flops | bytes accessed | tf_op | source)
XLA Modules:
  0.0 421.7 jit_solution(17403649763500536862)
XLA Ops:
  7.2 0.0 copy-start
  7.2 0.0 all-gather.4.cloned.1.call-start
  7.2 0.7 all-gather.4.cloned.1.call-update
  7.9 0.0 reduce-scatter.7.cloned.1.call-start
  8.0 0.7 compare_select_fusion.1
  8.7 0.1 reshape.111
  8.7 0.7 fusion.32
  9.5 26.7 %all-gather.4.cloned.1.call-done = f32[32,8192]{1,0:T(8,128)} async-done(((f32[32,1024]{1,0:T(8,128)}), f32[32,8192]{1,0:T(8,128)}) %all-gather.4.cloned.1.call-update) | async-done | bytes 1048592 | tf_op jit(solution)/shard_map/all_gather | solution.py:51
  36.1 1.4 copy_bitcast_fusion.2
  37.5 4.4 %gather_fusion = f32[512,32,128]{2,1,0:T(8,128)} fusion(f32[32,64,128]{2,0,1:T(8,128)S(1)} %copy_bitcast_fusion.2, s32[1024]{0:T(1024)S(1)} %pad_clamp_fusion), kind=kCustom, calls=%fused_computation | custom fusion | bytes 16779264 | tf_op jit(solution)/shard_map/gather | solution.py:47
  41.9 0.0 copy-start.4
  41.9 0.0 copy-start.7
  41.9 38.2 %fusion.11 = f32[8,4,8,128]{3,2,1,0:T(8,128)S(1)} fusion(f32[8,64,128,128]{3,2,1,0:T(8,128)} %param.11, f32[8,64,32,128]{3,2,1,0:T(8,128)} %bitcast.75, f32[8,64]{1,0:T(8,128)S(1)} %fusion.32), kind=kOutput, calls=%fused_computation.18 | convolution fusion | flops 3223322624 | bytes 42076160 | tf_op jit(solution)/shard_map/frkj,rkij->fri/dot_general | solution.py:48
  80.1 0.0 copy-done.4
  80.1 1.0 convolution_bitcast_fusion
  81.1 1.3 copy.62
  82.5 0.0 reduce-scatter.7.cloned.1.call-update
  82.5 0.0 all-gather.6.cloned.1.call-start
  82.5 27.2 %reduce-scatter.7.cloned.1.call-done = f32[64,1024]{1,0:T(8,128)} async-done(((f32[256,1024]{1,0:T(8,128)}), f32[64,1024]{1,0:T(8,128)}) %reduce-scatter.7.cloned.1.call-update) | async-done | bytes 262160 | tf_op jit(solution)/shard_map/reduce_scatter | solution.py:54
  109.8 0.0 copy-done.7
  109.8 1.8 multiply_multiply_fusion.2
  111.6 0.0 all-gather.6.cloned.1.call-update
  111.6 0.2 all-reduce.4.cloned.1.call-start
  111.9 27.2 %all-gather.6.cloned.1.call-done = f32[64,8192]{1,0:T(8,128)} async-done(((f32[64,1024]{1,0:T(8,128)}), f32[64,8192]{1,0:T(8,128)}) %all-gather.6.cloned.1.call-update) | async-done | bytes 2097168 | tf_op jit(solution)/shard_map/all_gather | solution.py:61
  139.0 1.9 copy_bitcast_fusion.1
  140.9 7.0 %gather_fusion.1 = f32[512,64,128]{2,1,0:T(8,128)} fusion(f32[64,64,128]{2,0,1:T(8,128)S(1)} %copy_bitcast_fusion.1, s32[1024]{0:T(1024)S(1)} %pad_clamp_fusion), kind=kCustom, calls=%fused_computation.1 | custom fusion | bytes 33556480 | tf_op jit(solution)/shard_map/gather | solution.py:47
  147.8 0.0 copy-start.5
  147.8 0.0 copy-start.6
  147.9 40.5 %fusion.8 = f32[8,8,8,128]{3,2,1,0:T(8,128)S(1)} fusion(f32[8,64,128,128]{3,2,1,0:T(8,128)} %param.11, f32[8,64,64,128]{3,2,1,0:T(8,128)} %bitcast.74, f32[8,64]{1,0:T(8,128)S(1)} %fusion.32), kind=kOutput, calls=%fused_computation.17 | convolution fusion | flops 6446645248 | bytes 50595840 | tf_op jit(solution)/shard_map/frkj,rkij->fri/dot_general | solution.py:48
  188.3 0.0 copy-done
  188.3 1.6 convolution_bitcast_fusion.1
  190.0 0.0 all-reduce.4.cloned.1.call-update
  190.0 0.3 reduce-scatter.5.cloned.1.call-start
  190.3 0.0 copy-done.5
  190.3 0.1 reshape.105
  190.3 0.0 copy-done.6
  190.3 0.6 compare_select_fusion
  190.9 41.2 %all-reduce.4.cloned.1.call-done = f32[172,1024]{1,0:T(8,128)} async-done(((f32[172,1024]{1,0:T(8,128)}), f32[172,1024]{1,0:T(8,128)}) %all-reduce.4.cloned.1.call-update) | async-done | bytes 704528 | tf_op jit(solution)/shard_map/psum | solution.py:63
  232.1 0.0 copy-done.9
  232.1 1.2 fusion.35
  233.4 0.0 copy-start.1
  233.4 0.1 exponential_reduce_fusion
  233.6 0.0 copy-done.3
  233.6 0.8 convolution_bitcast_fusion.2
  234.4 24.9 %convolution_multiply_fusion = f32[8,64,64,128]{3,1,2,0:T(8,128)} fusion(f32[8,64,128,128]{3,2,1,0:T(8,128)} %param.11, f32[8,64]{1,0:T(8,128)S(1)} %fusion.32, f32[64,8,128,1]{2,1,0,3:T(8,128)S(1)} %bitcast.76), kind=kOutput, calls=%fused_computation.6 | convolution fusion | flops 6446645248 | bytes 50595840 | tf_op jit(solution)/shard_map/fri,rkij->frkj/dot_general | solution.py:83
  259.3 0.2 broadcast_in_dim.8
  259.6 0.0 copy-start.2
  259.6 0.0 copy-start.8
  259.6 52.2 %scatter_fusion = f32[64,64,128]{2,0,1:T(8,128)S(1)} fusion(f32[64,64,128]{2,0,1:T(8,128)S(1)} %broadcast_in_dim.8, s32[512]{0:T(512)} %bitcast.77, f32[512,64,128]{2,1,0:T(8,128)} %bitcast.73), kind=kCustom, calls=%fused_computation.2 | custom fusion | flops 4194304 | bytes 50333696 | tf_op jit(solution)/shard_map/scatter-add | solution.py:87
  311.8 1.5 copy_bitcast_fusion
  313.3 0.0 reduce-scatter.5.cloned.1.call-update
  313.3 0.0 all-gather.8.cloned.1.call-start
  313.3 40.9 %reduce-scatter.5.cloned.1.call-done = f32[64,1024]{1,0:T(8,128)} async-done(((f32[64,8192]{1,0:T(8,128)}), f32[64,1024]{1,0:T(8,128)}) %reduce-scatter.5.cloned.1.call-update) | async-done | bytes 262160 | tf_op jit(solution)/shard_map/reduce_scatter | solution.py:88
  354.2 0.0 copy-done.2
  354.2 0.0 copy-done.8
  354.2 2.0 fusion.33
  356.3 0.0 all-gather.8.cloned.1.call-update
  356.3 0.4 fusion.14
  356.7 1.3 convert_reduce_fusion
  358.0 0.0 copy-done.1
  358.0 0.9 fusion.15
  358.9 25.5 %all-gather.8.cloned.1.call-done = f32[256,1024]{1,0:T(8,128)} async-done(((f32[64,1024]{1,0:T(8,128)}), f32[256,1024]{1,0:T(8,128)}) %all-gather.8.cloned.1.call-update) | async-done | bytes 1048592 | tf_op jit(solution)/shard_map/all_gather | solution.py:94
  384.4 2.2 fusion.27
  386.6 25.8 %all-reduce.5 = (f32[]{:T(128)}, f32[]{:T(128)}, f32[32,256]{1,0:T(8,128)}, f32[64]{0:T(128)}, f32[64,172]{1,0:T(8,128)}, /*index=5*/f32[172]{0:T(256)}) all-reduce(f32[]{:T(128)} %get-tuple-element.9, f32[]{:T(128)} %get-tuple-element.8, f32[32,256]{1,0:T(8,128)S(1)} %fusion.27, ...), channel_id=1, replica_groups=mesh['node'=8,'col'=4] {'node'}, use_global_device_ids=true, to_apply=%region_6.0 | all-reduce | flops 19438 | bytes 155504 | tf_op jit(solution)/shard_map/psum | solution.py:70
  (7 shorter events, 0.1 us)
Async XLA Ops:
  7.2 181.2 %copy-start = (f32[64,172]{1,0:T(8,128)S(1)}, f32[64,172]{1,0:T(8,128)}, u32[]{:S(2)}) copy-start(f32[64,172]{1,0:T(8,128)} %param.18) | copy-start | bytes 132100
  7.2 29.0 %all-gather.4.cloned.1.call-start = ((), (), s32[]{:S(2)}) async-start(), calls=%async_computation.2 | async-start | bytes 1179648 | tf_op jit(solution)/shard_map/all_gather | solution.py:51
  7.9 101.9 %reduce-scatter.7.cloned.1.call-start = ((), (), s32[]{:S(2)}) async-start(), calls=%async_computation.7 | async-start | bytes 1310720 | tf_op jit(solution)/shard_map/reduce_scatter | solution.py:54
  41.9 38.2 %copy-start.4 = (f32[32,256]{1,0:T(8,128)S(1)}, f32[32,256]{1,0:T(8,128)}, u32[]{:S(2)}) copy-start(f32[32,256]{1,0:T(8,128)} %param.16) | copy-start | bytes 98308
  41.9 67.9 %copy-start.7 = (f32[64]{0:T(128)S(1)}, f32[64]{0:T(128)}, u32[]{:S(2)}) copy-start(f32[64]{0:T(128)} %param.17) | copy-start | bytes 772
  82.5 56.5 %all-gather.6.cloned.1.call-start = ((), (), s32[]{:S(2)}) async-start(), calls=%async_computation.3 | async-start | bytes 2359296 | tf_op jit(solution)/shard_map/all_gather | solution.py:61
  111.6 120.5 %all-reduce.4.cloned.1.call-start = ((), (), s32[]{:S(2)}) async-start(), calls=%async_computation.4 | async-start | bytes 1441792 | tf_op jit(solution)/shard_map/psum | solution.py:63
  147.8 42.4 %copy-start.5 = (s32[8,64]{1,0:T(8,128)S(1)}, s32[8,64]{1,0:T(8,128)}, u32[]{:S(2)}) copy-start(s32[8,64]{1,0:T(8,128)} %param.12) | copy-start | bytes 6148
  147.8 42.5 %copy-start.6 = (s32[1024]{0:T(1024)S(1)}, s32[1024]{0:T(1024)}, u32[]{:S(2)}) copy-start(s32[1024]{0:T(1024)} %param.15) | copy-start | bytes 12292
  147.8 84.3 %copy-start.9 = (f32[172]{0:T(256)S(1)}, f32[172]{0:T(256)}, u32[]{:S(2)}) copy-start(f32[172]{0:T(256)} %param.19) | copy-start | bytes 2068
  147.8 85.7 %copy-start.3 = (s32[1024]{0:T(1024)S(1)}, s32[1024]{0:T(1024)}, u32[]{:S(2)}) copy-start(s32[1024]{0:T(1024)} %param.14) | copy-start | bytes 12292
  190.0 164.2 %reduce-scatter.5.cloned.1.call-start = ((), (), s32[]{:S(2)}) async-start(), calls=%async_computation.5 | async-start | bytes 2359296 | tf_op jit(solution)/shard_map/reduce_scatter | solution.py:88
  233.4 124.6 %copy-start.1 = (f32[172,1024]{1,0:T(8,128)}, f32[172,1024]{1,0:T(8,128)S(1)}, u32[]{:S(2)}) copy-start(f32[172,1024]{1,0:T(8,128)S(1)} %get-tuple-element.19) | copy-start | bytes 2113540
  259.6 94.7 %copy-start.2 = (f32[64,1024]{1,0:T(8,128)S(1)}, f32[64,1024]{1,0:T(8,128)}, u32[]{:S(2)}) copy-start(f32[64,1024]{1,0:T(8,128)} %reduce-scatter.7.cloned.1.call-done) | copy-start | bytes 786436
  259.6 94.7 %copy-start.8 = (f32[64]{0:T(128)S(1)}, f32[64]{0:T(128)}, u32[]{:S(2)}) copy-start(f32[64]{0:T(128)} %param.17) | copy-start | bytes 772
  313.3 71.1 %all-gather.8.cloned.1.call-start = ((), (), s32[]{:S(2)}) async-start(), calls=%async_computation.6 | async-start | bytes 1310720 | tf_op jit(solution)/shard_map/all_gather | solution.py:94
Sparse Core Ops, SparseCore 0:
  9.9 26.1 all-gather.3
  82.6 27.1 reduce-scatter.6
  112.4 26.5 all-gather.5
  190.1 41.9 all-reduce.3
  313.4 40.7 reduce-scatter.4
  356.4 27.9 all-gather.7
where the time goes:
time: 424 us; the launch traced here: 422 us
  waiting for transfers between devices  189 us (45%)
  matrix products  110 us (26%)
  other arithmetic  61.1 us (14%)
  blocking collectives  25.8 us (6%)
  local copies, waits for them, and re-layouts  17.9 us (4%)
  between operations  16.8 us (4%)
    dot_general x2, matrix products, gather_blocks(): mixed = jnp.einsum('frkj,rkij->fri', picked, tiles, precision=precise)  78.6 us
    scatter-add x1, other arithmetic, on_device(): summed.at[:, flat_columns]  52.2 us
    psum x1, waiting for transfers between devices, on_device(): lax.psum(dot_first(weight_out, mixed_out), 'col') + bias_out[:, None]  41.2 us
    reduce_scatter x1, waiting for transfers between devices, on_device(): lax.psum_scatter(summed.reshape(channel_count, block_total * BLOCK), 'nod...  40.9 us
    reduce_scatter x1, waiting for transfers between devices, on_device(): lax.psum_scatter(dot_first(weight_in, mixed_in), 'col', scatter_dimension...  27.2 us
    all_gather x1, waiting for transfers between devices, on_device(): hidden_all = lax.all_gather(hidden, 'node', axis=1, tiled=True)  27.2 us
    all_gather x1, waiting for transfers between devices, on_device(): feature_all = lax.all_gather(features, 'node', axis=1, tiled=True)  26.7 us
    psum x1, blocking collectives, on_device(): lax.psum((jnp.sum(train_weight * cross_entropy), jnp.sum(train_weight)),...  25.8 us
  transfers between devices with their start and end apart: 6, of which 6 were waited for; matrix products, arithmetic and copies ran while one was open for 1% of the time, Pallas kernels for 0%

commit v1 on v0

v1 whole, which is shorter than its diff:
```python
import functools

import jax
import jax.numpy as jnp
from jax import lax
from jax.experimental import pallas as pl
from jax.experimental.pallas import tpu as pltpu
from jax.sharding import PartitionSpec as P

BLOCK = 128
CHUNK = 4
UNROLL = 2
FETCH = 4
PAD = 48

f32 = jnp.float32
bf16 = jnp.bfloat16
VMEM = pl.BlockSpec(memory_space=pltpu.VMEM)
SMEM = pl.BlockSpec(memory_space=pltpu.SMEM)
MIB = 1 << 20

CURVE = 0.7978845608028654
CUBIC = 0.044715


def exchange(value, axis, offset):
    total = lax.axis_size(axis)
    return lax.ppermute(value, axis, [(i, i ^ offset) for i in range(total)])


def split(value):
    high = value.astype(bf16)
    low = (value - high.astype(f32)).astype(bf16)
    return high, low


def product(left, right, dims):
    lh, ll = split(left)
    rh, rl = split(right)

    def one(a, b):
        return lax.dot_general(a, b, (dims, ((), ())), preferred_element_type=f32)

    return one(lh, rh) + (one(lh, rl) + one(ll, rh))


def call(body, outs, scratch, *args, specs=None, out_specs=None, limit=12, flops=0, moved=0):
    return pl.pallas_call(
        body,
        out_shape=outs,
        in_specs=specs or [VMEM] * len(args),
        out_specs=out_specs or [VMEM] * len(outs),
        scratch_shapes=scratch,
        compiler_params=pltpu.CompilerParams(vmem_limit_bytes=limit * MIB),
        cost_estimate=pl.CostEstimate(flops=flops, bytes_accessed=moved, transcendentals=0),
    )(*args)


def pack_body(count_ref, column_ref, tiles_ref, pack_ref, list_ref, row_ref, total_ref, land, store, place, owner, sem, out_sem):
    rows, slots = column_ref.shape

    def copies(row, act):
        buffer = lax.rem(row, 2)

        def one(group, _):
            part = pl.ds(group * FETCH, FETCH)
            copy = pltpu.make_async_copy(
                tiles_ref.at[row, part], land.at[buffer, part], sem.at[buffer, group]
            )
            act(copy)
            return 0

        lax.fori_loop(0, (count_ref[row] + FETCH - 1) // FETCH, one, 0)

    def leave(item):
        return pltpu.make_async_copy(store.at[item], pack_ref.at[item], out_sem.at[item])

    def start(copy):
        copy.start()

    def wait(copy):
        copy.wait()

    def blank_item(item):
        for q in range(CHUNK):
            list_ref[item * CHUNK + q] = 0

    copies(0, start)

    def one_row(row, begin):
        buffer = lax.rem(row, 2)
        live = count_ref[row]

        @pl.when(row + 1 < rows)
        def _():
            copies(row + 1, start)

        def clear(slot, _):
            place[column_ref[row, slot]] = -1
            return 0

        lax.fori_loop(0, live, clear, 0)
        copies(row, wait)

        def scan(slot, found):
            column = column_ref[row, slot]
            at = place[column]
            fresh = at < 0

            @pl.when(fresh)
            def _():
                place[column] = slot
                owner[found] = slot
                list_ref[begin * CHUNK + found] = column

            @pl.when(jnp.logical_not(fresh))
            def _():
                land[buffer, at] = land[buffer, at] + land[buffer, slot]

            return found + fresh.astype(jnp.int32)

        found = lax.fori_loop(0, live, scan, 0)
        steps = (found + CHUNK - 1) // CHUNK

        def blank(index, _):
            list_ref[begin * CHUNK + index] = 0
            return 0

        lax.fori_loop(found, steps * CHUNK, blank, 0)

        def convert(step, _):
            item = begin + step
            row_ref[item] = row
            for q in range(CHUNK):
                index = step * CHUNK + q
                at = slice(q * BLOCK, (q + 1) * BLOCK)

                @pl.when(index < found)
                def _():
                    high, low = split(land[buffer, owner[index]])
                    store[item, :BLOCK, at] = high
                    store[item, BLOCK:, at] = low

                @pl.when(index >= found)
                def _():
                    store[item, :, at] = jnp.zeros((2 * BLOCK, BLOCK), bf16)

            leave(item).start()
            return 0

        lax.fori_loop(0, steps, convert, 0)
        return begin + steps

    used = lax.fori_loop(0, rows, one_row, 0)
    total = (used + UNROLL - 1) // UNROLL * UNROLL

    def fill(item, _):
        row_ref[item] = 0
        blank_item(item)
        store[item] = jnp.zeros(store.shape[1:], bf16)
        leave(item).start()
        return 0

    lax.fori_loop(used, total, fill, 0)
    total_ref[0] = total // UNROLL

    def last(item, _):
        leave(item).wait()
        return 0

    lax.fori_loop(0, total, last, 0)


def pack(tiles, tile_column, tile_count, block_total):
    rows, slots = tile_column.shape
    items = -(-rows * slots // (CHUNK * UNROLL)) * UNROLL
    shape = jax.ShapeDtypeStruct
    return call(
        pack_body,
        [
            pltpu.HBM((items, 2 * BLOCK, CHUNK * BLOCK), bf16),
            shape((items * CHUNK,), jnp.int32),
            shape((items,), jnp.int32),
            shape((1,), jnp.int32),
        ],
        [
            pltpu.VMEM((2, slots, BLOCK, BLOCK), f32),
            pltpu.VMEM((items, 2 * BLOCK, CHUNK * BLOCK), bf16),
            pltpu.SMEM((block_total,), jnp.int32),
            pltpu.SMEM((slots,), jnp.int32),
            pltpu.SemaphoreType.DMA((2, slots // FETCH)),
            pltpu.SemaphoreType.DMA((items,)),
        ],
        tile_count,
        tile_column,
        tiles,
        specs=[SMEM, SMEM, pl.BlockSpec(memory_space=pl.ANY)],
        out_specs=[pl.BlockSpec(memory_space=pltpu.HBM), SMEM, SMEM, SMEM],
        limit=48,
        flops=10**8,
        moved=40 * MIB,
    )


def bring(total_ref, pack_ref, store, sem):
    def one(group):
        part = pl.ds(group * UNROLL, UNROLL)
        return pltpu.make_async_copy(pack_ref.at[part], store.at[part], sem.at[group])

    def start(group, _):
        one(group).start()
        return 0

    lax.fori_loop(0, total_ref[0], start, 0)
    return one


def store_block(values, at, value):
    channels = value.shape[0]
    high, low = split(value)
    values[at, :channels] = high
    values[at, channels:] = low


def mix_rows(total_ref, list_ref, row_ref, one, store, values, sums):
    sums[...] = jnp.zeros_like(sums)

    def step(group, _):
        one(group).wait()
        for part in range(UNROLL):
            item = group * UNROLL + part
            left = jnp.concatenate([values[list_ref[item * CHUNK + q]] for q in range(CHUNK)], axis=1)
            row = row_ref[item]
            sums[row] = sums[row] + lax.dot_general(
                left, store[item], (((1,), (1,)), ((), ())), preferred_element_type=f32
            )
        return 0

    lax.fori_loop(0, total_ref[0], step, 0)


def mixed_row(sums, row):
    total = sums[row]
    channels = total.shape[0] // 2
    total = total[:, :BLOCK] + total[:, BLOCK:]
    return total[:channels] + total[channels:]


def mix_in_body(nodes, cols, ids_ref, total_ref, list_ref, row_ref, pack_ref, *refs):
    pieces, outs = refs[:nodes], refs[nodes : nodes + cols]
    values, sums, store, sem = refs[nodes + cols :]
    one = bring(total_ref, pack_ref, store, sem)
    rows = sums.shape[0]
    node, col = ids_ref[0], ids_ref[1]
    for offset in range(nodes):
        base = (node ^ offset) * rows
        for part in range(rows):
            store_block(values, base + part, pieces[offset][:, part * BLOCK : (part + 1) * BLOCK])
    mix_rows(total_ref, list_ref, row_ref, one, store, values, sums)
    slice_rows = rows // cols
    for offset in range(cols):
        for part in range(slice_rows):
            row = (col ^ offset) * slice_rows + part
            outs[offset][:, part * BLOCK : (part + 1) * BLOCK] = mixed_row(sums, row)


def dense_body(cols, per, ids_ref, *refs):
    pieces, weights = refs[:cols], refs[cols : 2 * cols]
    mixed_ref, hidden_ref, slope_ref, weight_out_ref = refs[2 * cols : 2 * cols + 4]
    outs = refs[2 * cols + 4 : 3 * cols + 4]
    held, held_weights, scores = refs[-3:]
    col = ids_ref[1]
    for offset in range(cols):
        held[col ^ offset] = pieces[offset][...]
        held_weights[col ^ offset] = weights[offset][...]
    feats = held.shape[1]
    units, classes = weight_out_ref.shape
    mixed = held[...].reshape(mixed_ref.shape)
    mixed_ref[...] = mixed
    weight_in = held_weights[:, :feats].reshape(feats * cols, units)
    weight_tail = held_weights[:, feats:].reshape(units, units)
    weight_out_ref[...] = weight_tail[:, :classes]
    inner = product(weight_in, mixed, ((0,), (0,))) + weight_tail[:, classes : classes + 1]
    bend = jnp.tanh(CURVE * (inner + CUBIC * inner * inner * inner))
    hidden = 0.5 * inner * (1.0 + bend)
    hidden_ref[...] = hidden
    slope_ref[...] = 0.5 * (1.0 + bend) + (0.5 * inner) * (1.0 - bend * bend) * (
        CURVE * (1.0 + 3.0 * CUBIC * inner * inner)
    )
    value = product(weight_out_ref[...], hidden, ((0,), (0,)))
    scores[...] = jnp.zeros_like(scores)
    for group in range(cols):
        scores[group, :per] = value[group * per : (group + 1) * per]
    for offset in range(cols):
        outs[offset][...] = scores[col ^ offset]


def stack_body(*refs):
    for index, ref in enumerate(refs[:-1]):
        refs[-1][index] = ref[...]


def mix_out_body(nodes, cols, per, ids_ref, total_ref, list_ref, row_ref, pack_ref, bias_ref, labels_ref, *refs):
    pieces = refs[:nodes]
    logits_ref, stats_ref, values, sums, store, sem = refs[nodes:]
    one = bring(total_ref, pack_ref, store, sem)
    rows = sums.shape[0]
    node, col = ids_ref[0], ids_ref[1]
    slice_rows = rows // cols
    for offset in range(nodes):
        base = (node ^ offset) * rows
        for group in range(cols):
            for part in range(slice_rows):
                store_block(
                    values,
                    base + (col ^ group) * slice_rows + part,
                    pieces[offset][group, :, part * BLOCK : (part + 1) * BLOCK],
                )
    mix_rows(total_ref, list_ref, row_ref, one, store, values, sums)
    for row in range(rows):
        logits_ref[:, row * BLOCK : (row + 1) * BLOCK] = mixed_row(sums, row) + bias_ref[col]
    logits = logits_ref[...]
    place = lax.broadcasted_iota(jnp.int32, logits.shape, 0)
    inside = place < per
    top = jnp.max(jnp.where(inside, logits, -jnp.inf), axis=0, keepdims=True)
    total = jnp.sum(jnp.where(inside, jnp.exp(logits - top), 0.0), axis=0, keepdims=True)
    hit = inside & (place + col * per == labels_ref[...])
    chosen = jnp.sum(jnp.where(hit, logits, 0.0), axis=0, keepdims=True)
    stats_ref[...] = jnp.zeros_like(stats_ref)
    stats_ref[0:1] = top
    stats_ref[1:2] = total
    stats_ref[2:3] = chosen


def mix_back_body(nodes, cols, per, ids_ref, total_ref, list_ref, row_ref, pack_ref, logits_ref, labels_ref, mask_ref, *refs):
    stats, outs = refs[:cols], refs[cols : cols + nodes]
    extra_ref, sums, grads, store, sem = refs[cols + nodes :]
    one = bring(total_ref, pack_ref, store, sem)
    rows = grads.shape[0]
    node, col = ids_ref[0], ids_ref[1]
    tops = [ref[0:1] for ref in stats]
    top = functools.reduce(jnp.maximum, tops)
    total = sum(ref[1:2] * jnp.exp(at - top) for ref, at in zip(stats, tops))
    chosen = sum(ref[2:3] for ref in stats)
    mask = mask_ref[...].astype(f32)
    logits = logits_ref[...]
    place = lax.broadcasted_iota(jnp.int32, logits.shape, 0)
    inside = place < per
    hit = place + col * per == labels_ref[...]
    chance = jnp.exp(logits - top) * (1.0 / total)
    grad = jnp.where(inside, mask * (chance - hit.astype(f32)), 0.0)
    high, low = split(grad)
    ones = jnp.ones((8, grad.shape[1]), bf16)
    bias_row = lax.dot_general(
        ones, high, (((1,), (1,)), ((), ())), preferred_element_type=f32
    ) + lax.dot_general(ones, low, (((1,), (1,)), ((), ())), preferred_element_type=f32)
    loss = jnp.sum(mask * (top + jnp.log(total) - chosen), axis=1, keepdims=True)
    number = jnp.sum(mask, axis=1, keepdims=True)
    first = (col == 0).astype(f32)
    extra_ref[...] = jnp.zeros_like(extra_ref)
    line = lax.broadcasted_iota(jnp.int32, bias_row.shape, 0)
    extra_ref[:, : high.shape[0]] = jnp.where(line == col, bias_row, 0.0)
    extra_ref[cols : cols + 1, 0:1] = loss * first
    extra_ref[cols : cols + 1, 1:2] = number * first

    for row in range(rows):
        at = slice(row * BLOCK, (row + 1) * BLOCK)
        grads[row] = jnp.concatenate(
            [
                jnp.concatenate([high[:, at], high[:, at]], axis=1),
                jnp.concatenate([low[:, at], low[:, at]], axis=1),
            ],
            axis=0,
        )
    sums[...] = jnp.zeros_like(sums)

    def step(group, _):
        one(group).wait()
        for part in range(UNROLL):
            item = group * UNROLL + part
            terms = jnp.dot(grads[row_ref[item]], store[item], preferred_element_type=f32)
            half = terms.shape[0] // 2
            terms = terms[:half] + terms[half:]
            for q in range(CHUNK):
                to = list_ref[item * CHUNK + q]
                sums[to] = sums[to] + terms[:, q * BLOCK : (q + 1) * BLOCK]
        return 0

    lax.fori_loop(0, total_ref[0], step, 0)
    for offset in range(nodes):
        base = (node ^ offset) * rows
        for part in range(rows):
            outs[offset][:, part * BLOCK : (part + 1) * BLOCK] = sums[base + part]


def grads_body(cols, per, ids_ref, mixed_ref, hidden_ref, slope_ref, weight_out_ref, extra_ref, *refs):
    pieces = refs[:cols]
    keep_ref, send_ref, held, packed = refs[cols:]
    core, col = ids_ref[0] & 1, ids_ref[1]
    for offset in range(cols):
        held[col ^ offset] = pieces[offset][...]
    spread = jnp.concatenate([held[group, :per] for group in range(cols)], axis=0)
    classes = spread.shape[0]
    hidden_grad = product(weight_out_ref[...], spread, ((1,), (0,)))
    inner_grad = hidden_grad * slope_ref[...]
    weight_in = product(mixed_ref[...], inner_grad, ((1,), (1,)))
    weight_out = product(hidden_ref[...], spread, ((1,), (1,)))
    bias_in = jnp.sum(inner_grad, axis=1, keepdims=True)
    feats, units = weight_in.shape[0] // cols, weight_out.shape[0] // cols
    packed[...] = jnp.zeros_like(packed)
    for group in range(cols):
        packed[group, :feats] = weight_in[group * feats : (group + 1) * feats]
        rows = slice(group * units, (group + 1) * units)
        packed[group, feats : feats + units, :classes] = weight_out[rows]
        packed[group, feats : feats + units, classes : classes + 1] = bias_in[rows]
        packed[group, feats + units : feats + units + 8] = extra_ref[...]
    half = packed.shape[1] // 2
    for offset in range(cols):
        keep_ref[offset] = packed[col ^ offset, pl.ds(pl.multiple_of(core * half, 8), half)]
        send_ref[offset] = packed[col ^ offset, pl.ds(pl.multiple_of((1 - core) * half, 8), half)]


def finish_body(cols, per, ids_ref, mine_ref, other_ref, weight_in_ref, bias_in_ref, weight_out_ref, bias_out_ref, loss_ref, whole):
    core = ids_ref[0] & 1
    half = mine_ref.shape[0]
    whole[core] = mine_ref[...]
    whole[1 - core] = other_ref[...]
    value = whole[...].reshape(2 * half, mine_ref.shape[1])
    feats, (units, classes) = weight_in_ref.shape[0], weight_out_ref.shape
    weight_in_ref[...] = value[:feats]
    weight_out_ref[...] = value[feats : feats + units, :classes]
    bias_in_ref[...] = value[feats : feats + units, classes : classes + 1]
    extra = value[feats + units : feats + units + 8]
    bias_out_ref[...] = jnp.concatenate([extra[group : group + 1, :per] for group in range(cols)], axis=1)
    loss_ref[...] = extra[cols : cols + 1, 0:1] / jnp.maximum(extra[cols : cols + 1, 1:2], 1.0)


def logits_body(cols, per, ids_ref, *refs):
    pieces, out_ref, held = refs[:cols], refs[cols], refs[-1]
    col = ids_ref[1]
    for offset in range(cols):
        held[col ^ offset] = pieces[offset][...]
    out_ref[...] = jnp.concatenate([held[group, :per] for group in range(cols)], axis=0)


def gather_chips(value, nodes):
    return [value] + [exchange(value, "node", offset) for offset in range(2, nodes, 2)]


def gather_cores(even):
    odd = [exchange(piece, "node", 1) for piece in even]
    return [piece for pair in zip(even, odd) for piece in pair]


def on_device(
    features,
    tiles,
    tile_column,
    tile_count,
    labels,
    train_mask,
    weight_in,
    bias_in,
    weight_out,
    bias_out,
):
    nodes, cols = lax.axis_size("node"), lax.axis_size("col")
    rows = tile_column.shape[0]
    local = labels.shape[0]
    slice_nodes = local // cols
    block_total = nodes * rows
    feats = features.shape[0]
    classes = weight_out.shape[1]
    per = classes // cols
    units = weight_out.shape[0] * cols
    shape = jax.ShapeDtypeStruct
    ids = jnp.stack([lax.axis_index("node"), lax.axis_index("col")]).astype(jnp.int32)

    tail = jnp.concatenate(
        [weight_out, bias_in[:, None], jnp.zeros((units // cols, units - classes - 1), f32)], axis=1
    )
    weights = jnp.concatenate([weight_in, tail], axis=0)
    bias_groups = jnp.pad(bias_out.reshape(cols, per, 1), ((0, 0), (0, PAD - per), (0, 0)))
    labels = labels[None, :]
    train_mask = train_mask[None, :]
    tile_count, ids, bias_groups, labels, train_mask, weights = lax.optimization_barrier(
        (tile_count, ids, bias_groups, labels, train_mask, weights)
    )

    even = gather_chips(features, nodes)
    weight_pieces = [weights] + [exchange(weights, "col", k) for k in range(1, cols)]
    packed, listed, placed, steps = pack(tiles, tile_column, tile_count, block_total)
    steps, *even = lax.optimization_barrier((steps, *even))
    feature_pieces = gather_cores(even)
    sparse = (ids, steps, listed, placed, packed)
    sparse_specs = [SMEM] * 4 + [pl.BlockSpec(memory_space=pltpu.HBM)]
    held = [pltpu.VMEM(packed.shape, bf16), pltpu.SemaphoreType.DMA((packed.shape[0] // UNROLL,))]

    mixed_parts = call(
        functools.partial(mix_in_body, nodes, cols),
        [shape((feats, slice_nodes), f32)] * cols,
        [pltpu.VMEM((block_total, 2 * feats, BLOCK), bf16), pltpu.VMEM((rows, 2 * feats, 2 * BLOCK), f32), *held],
        *sparse,
        *feature_pieces,
        specs=sparse_specs + [VMEM] * nodes,
        limit=44,
        flops=10**9,
        moved=16 * MIB,
    )
    mixed_pieces = [mixed_parts[0]] + [exchange(mixed_parts[k], "col", k) for k in range(1, cols)]
    mixed, hidden, slope, weight_out_all, *score_parts = call(
        functools.partial(dense_body, cols, per),
        [shape((feats * cols, slice_nodes), f32)]
        + [shape((units, slice_nodes), f32)] * 2
        + [shape((units, classes), f32)]
        + [shape((PAD, slice_nodes), f32)] * cols,
        [
            pltpu.VMEM((cols, feats, slice_nodes), f32),
            pltpu.VMEM((cols, *weights.shape), f32),
            pltpu.VMEM((cols, PAD, slice_nodes), f32),
        ],
        ids,
        *mixed_pieces,
        *weight_pieces,
        specs=[SMEM] + [VMEM] * (2 * cols),
        flops=10**8,
        moved=2 * MIB,
    )
    score_pieces = [score_parts[0]] + [exchange(score_parts[k], "col", k) for k in range(1, cols)]
    (stacked,) = call(
        stack_body,
        [shape((cols, PAD, slice_nodes), f32)],
        [],
        *score_pieces,
        limit=4,
        moved=MIB,
    )
    scores = gather_cores(gather_chips(stacked, nodes))
    logits_part, stats = call(
        functools.partial(mix_out_body, nodes, cols, per),
        [shape((PAD, local), f32), shape((8, local), f32)],
        [pltpu.VMEM((block_total, 2 * PAD, BLOCK), bf16), pltpu.VMEM((rows, 2 * PAD, 2 * BLOCK), f32), *held],
        *sparse,
        bias_groups,
        labels,
        *scores,
        specs=sparse_specs + [VMEM] * (2 + nodes),
        limit=44,
        flops=10**9,
        moved=16 * MIB,
    )
    stats_pieces = [stats] + [exchange(stats, "col", k) for k in range(1, cols)]
    *spread_parts, extra = call(
        functools.partial(mix_back_body, nodes, cols, per),
        [shape((PAD, local), f32)] * nodes + [shape((8, 2 * BLOCK), f32)],
        [
            pltpu.VMEM((block_total, PAD, BLOCK), f32),
            pltpu.VMEM((rows, 2 * PAD, 2 * BLOCK), bf16),
            *held,
        ],
        *sparse,
        logits_part,
        labels,
        train_mask,
        *stats_pieces,
        specs=sparse_specs + [VMEM] * (3 + cols),
        limit=44,
        flops=10**9,
        moved=16 * MIB,
    )
    logit_pieces = [logits_part] + [exchange(logits_part, "col", k) for k in range(1, cols)]
    (logits,) = call(
        functools.partial(logits_body, cols, per),
        [shape((classes, local), f32)],
        [pltpu.VMEM((cols, PAD, local), f32)],
        ids,
        *logit_pieces,
        specs=[SMEM] + [VMEM] * cols,
        moved=2 * MIB,
    )

    paired = [
        spread_parts[k] + exchange(spread_parts[k + 1], "node", 1) for k in range(0, nodes, 2)
    ]
    spread = paired[0]
    for index in range(1, nodes // 2):
        spread = spread + exchange(paired[index], "node", 2 * index)
    col = ids[1]
    spread_slices = [
        lax.dynamic_slice_in_dim(spread, (col ^ k) * slice_nodes, slice_nodes, axis=1) for k in range(cols)
    ]
    spread_pieces = [spread_slices[0]] + [exchange(spread_slices[k], "col", k) for k in range(1, cols)]
    logits, *spread_pieces = lax.optimization_barrier((logits, *spread_pieces))

    height = -(-(feats + units // cols + 8) // 16) * 16
    keep, send = call(
        functools.partial(grads_body, cols, per),
        [shape((cols, height // 2, units), f32)] * 2,
        [pltpu.VMEM((cols, PAD, slice_nodes), f32), pltpu.VMEM((cols, height, units), f32)],
        ids,
        mixed,
        hidden,
        slope,
        weight_out_all,
        extra,
        *spread_pieces,
        specs=[SMEM] + [VMEM] * (5 + cols),
        flops=10**8,
        moved=2 * MIB,
    )
    halves = keep + exchange(send, "node", 1)
    total = halves[0]
    for k in range(1, cols):
        total = total + exchange(halves[k], "col", k)
    grand = total
    for k in range(2, nodes, 2):
        grand = grand + exchange(total, "node", k)
    other = exchange(grand, "node", 1)
    grad_in, grad_bias_in, grad_out, grad_bias_out, mean_loss = call(
        functools.partial(finish_body, cols, per),
        [
            shape((feats, units), f32),
            shape((units // cols, 1), f32),
            shape((units // cols, classes), f32),
            shape((1, classes), f32),
            shape((1, 1), f32),
        ],
        [pltpu.VMEM((2, height // 2, units), f32)],
        ids,
        grand,
        other,
        specs=[SMEM, VMEM, VMEM],
    )
    return (logits, mean_loss[0, 0], grad_in, grad_bias_in[:, 0], grad_out, grad_bias_out[0])


def solution(mesh):
    in_specs = (
        P("col", "node"),
        P("node", None, None, None),
        P("node", None),
        P("node"),
        P("node"),
        P("node"),
        P("col", None),
        P("col"),
        P("col", None),
        P(),
    )
    out_specs = (P(None, "node"), P(), P("col", None), P("col"), P("col", None), P())
    return jax.shard_map(
        on_device, mesh=mesh, in_specs=in_specs, out_specs=out_specs, check_vma=False
    )
```

time: 424 us -> 159 us (0.38)
  waiting for transfers between devices: 189 us -> 48.4 us
  matrix products: 110 us -> 0 us
  other arithmetic: 61.1 us -> 1.84 us
  starting transfers between devices: 0.64 us -> 58.8 us
  Pallas kernels: 0 us -> 44.6 us
  blocking collectives: 25.8 us -> 0 us
  local copies, waits for them, and re-layouts: 17.9 us -> 3.61 us
  between operations: 16.8 us -> 3.52 us
    dot_general x8 -> x0, matrix products: 110 us -> none  [the longest x2 78.6 us: gather_blocks(): mixed = jnp.einsum('frkj,rkij->fri', picked, tiles, precision=precise)]
    all_gather x3 -> x0, waiting for transfers between devices: 79.3 us -> none  [the longest x1 27.2 us: on_device(): hidden_all = lax.all_gather(hidden, 'node', axis=1, tiled=True)]
    reduce_scatter x2 -> x0, waiting for transfers between devices: 68.1 us -> none  [the longest x1 40.9 us: on_device(): lax.psum_scatter(summed.reshape(channel_count, block_total * BLOCK), 'nod...]
    ppermute x0 -> x47, starting transfers between devices: none -> 58.8 us  [exchange(): return lax.ppermute(value, axis, [(i, i ^ offset) for i in range(total)])]
    scatter-add x1 -> x0, other arithmetic: 52.2 us -> none  [on_device(): summed.at[:, flat_columns]]
    ppermute x0 -> x47, waiting for transfers between devices: none -> 48.4 us  [exchange(): return lax.ppermute(value, axis, [(i, i ^ offset) for i in range(total)])]
    pallas_call x0 -> x9, Pallas kernels: none -> 44.6 us  [call(): pl.pallas_call(body, out_shape=outs, in_specs=specs or [VMEM] * len(args)...]
    psum x1 -> x0, waiting for transfers between devices: 41.2 us -> none  [on_device(): lax.psum(dot_first(weight_out, mixed_out), 'col') + bias_out[:, None]]
  transfers between devices with their start and end apart: 6 -> 47, of which waited for: 6 -> 22; matrix products, arithmetic and copies ran while one was open for 1% -> 2% of each run, Pallas kernels for 0% -> 16%
where the time goes in v1:
time: 159 us; the launch traced here: 161 us
  starting transfers between devices  58.8 us (37%)
  waiting for transfers between devices  48.4 us (30%)
  Pallas kernels  44.6 us (28%)
  local copies, waits for them, and re-layouts  3.61 us (2%)
  between operations  3.52 us (2%)
  other arithmetic  1.84 us (1%)
    ppermute x47, starting transfers between devices, exchange(): return lax.ppermute(value, axis, [(i, i ^ offset) for i in range(total)])  58.8 us
    ppermute x47, waiting for transfers between devices, exchange(): return lax.ppermute(value, axis, [(i, i ^ offset) for i in range(total)])  48.4 us
    pallas_call x9, Pallas kernels, call(): pl.pallas_call(body, out_shape=outs, in_specs=specs or [VMEM] * len(args)...  44.6 us
  transfers between devices with their start and end apart: 47, of which 22 were waited for; matrix products, arithmetic and copies ran while one was open for 2% of the time, Pallas kernels for 16%

profile of v1, /device:TPU:0, one launch (start us, length us, event | category | flops | bytes accessed | tf_op | source)
XLA Modules:
  0.0 160.9 jit_solution(9782878682225471023)
XLA Ops:
  0.6 3.0 %collective-permute-start = (f32[32,1024]{1,0:T(8,128)}, f32[32,1024]{1,0:T(8,128)S(1)}, u32[]{:S(2)}, u32[]{:S(2)}) collective-permute-start(f32[32,1024]{1,0:T(8,128)} %refs_0_), channel_id=1, source_target_pairs={{0,8},{4,12},{8,0},{12,4},{16,24},{20,28},{24,16},{28,20},{1,9},{5... | collective-permute-start | bytes 393224 | tf_op jit(solution)/shard_map/ppermute | solution.py:28
  3.6 1.5 collective-permute-start.1
  5.3 0.9 reshape.30
  6.1 0.7 copy.18
  6.9 0.9 maximum_maximum_fusion.refs_4_
  7.9 0.7 copy-done.2
  8.5 0.7 copy-done.4
  9.2 17.1 %shard_map.145 = (bf16[128,256,512]{2,1,0:T(8,128)(2,1)}, s32[512]{0:T(512)S(1)}, s32[128]{0:T(128)S(1)}, s32[1]{0:T(128)}) custom-call(s32[8]{0:T(128)S(1)} %copy-done.4, s32[8,64]{1,0:T(8,128)S(1)} %copy-done.2, f32[8,64,128,128]{3,2,1,0:T(8,128)} %tiles_ref.1), custom_call_target="tpu_custom_call" | custom-call | flops 100000000 | bytes 41943040 | tf_op jit(solution)/shard_map/pallas_call | solution.py:48
  26.4 0.5 collective-permute-start.4
  27.0 0.4 collective-permute-start.6
  27.4 2.0 %collective-permute-start.10 = (f32[96,256]{1,0:T(8,128)S(1)}, f32[96,256]{1,0:T(8,128)S(1)}, u32[]{:S(2)}, u32[]{:S(2)}) collective-permute-start(f32[96,256]{1,0:T(8,128)S(1)} %maximum_maximum_fusion.refs_4_), channel_id=1, source_target_pairs={{0,1},{1,0},{2,3},{3,2},{4,5},{5,4},{6,7},{7,6},{8,9},{9,8},{10,11... | collective-permute-start | bytes 294920 | tf_op jit(solution)/shard_map/ppermute | solution.py:28
  29.5 2.6 %collective-permute-start.11 = (f32[96,256]{1,0:T(8,128)S(1)}, f32[96,256]{1,0:T(8,128)S(1)}, u32[]{:S(2)}, u32[]{:S(2)}) collective-permute-start(f32[96,256]{1,0:T(8,128)S(1)} %maximum_maximum_fusion.refs_4_), channel_id=1, source_target_pairs={{0,2},{1,3},{2,0},{3,1},{4,6},{5,7},{6,4},{7,5},{8,10},{9,11},{10,... | collective-permute-start | bytes 294920 | tf_op jit(solution)/shard_map/ppermute | solution.py:28
  32.2 7.6 %shard_map.146 = (f32[32,256]{1,0:T(8,128)S(1)}, f32[32,256]{1,0:T(8,128)S(1)}, f32[32,256]{1,0:T(8,128)S(1)}, f32[32,256]{1,0:T(8,128)S(1)}) custom-call(s32[2]{0:T(128)S(1)} %pad_add_fusion.ids_ref, s32[1]{0:T(128)} %get-tuple-element.59.total_ref, s32[512]{0:T(512)S(1)} %get-tuple-element.60.list_ref, s32[128]{0:T(128)S(1)} %get-tuple-element.61.row_ref, ...), custom_call_target="tpu_custom_call" | custom-call | flops 1000000000 | bytes 16777216 | tf_op jit(solution)/shard_map/pallas_call | solution.py:48
  39.8 0.9 collective-permute-start.7
  40.7 3.5 %collective-permute-start.8 = (f32[32,256]{1,0:T(8,128)S(1)}, f32[32,256]{1,0:T(8,128)S(1)}, u32[]{:S(2)}, u32[]{:S(2)}) collective-permute-start(f32[32,256]{1,0:T(8,128)S(1)} %get-tuple-element.71), channel_id=1, source_target_pairs={{0,2},{1,3},{2,0},{3,1},{4,6},{5,7},{6,4},{7,5},{8,10},{9,11},{10,... | collective-permute-start | bytes 98312 | tf_op jit(solution)/shard_map/ppermute | solution.py:28
  44.3 2.1 %collective-permute-done.8.refs_2_ = f32[32,256]{1,0:T(8,128)S(1)} collective-permute-done((f32[32,256]{1,0:T(8,128)S(1)}, f32[32,256]{1,0:T(8,128)S(1)}, u32[]{:S(2)}, u32[]{:S(2)}) %collective-permute-start.8) | collective-permute-done | bytes 32800 | tf_op jit(solution)/shard_map/ppermute | solution.py:28
  46.4 3.5 %collective-permute-done.9.refs_3_ = f32[32,256]{1,0:T(8,128)S(1)} collective-permute-done((f32[32,256]{1,0:T(8,128)S(1)}, f32[32,256]{1,0:T(8,128)S(1)}, u32[]{:S(2)}, u32[]{:S(2)}) %collective-permute-start.9) | collective-permute-done | bytes 32800 | tf_op jit(solution)/shard_map/ppermute | solution.py:28
  49.9 1.3 shard_map.147
  51.3 0.9 collective-permute-start.14
  52.2 3.5 %collective-permute-start.15 = (f32[48,256]{1,0:T(8,128)S(1)}, f32[48,256]{1,0:T(8,128)S(1)}, u32[]{:S(2)}, u32[]{:S(2)}) collective-permute-start(f32[48,256]{1,0:T(8,128)S(1)} %get-tuple-element.77), channel_id=1, source_target_pairs={{0,3},{1,2},{2,1},{3,0},{4,7},{5,6},{6,5},{7,4},{8,11},{9,10},{10,... | collective-permute-start | bytes 147464 | tf_op jit(solution)/shard_map/ppermute | solution.py:28
  55.6 0.7 collective-permute-done.14.refs_2_
  56.3 1.9 %collective-permute-done.15.refs_3_ = f32[48,256]{1,0:T(8,128)S(1)} collective-permute-done((f32[48,256]{1,0:T(8,128)S(1)}, f32[48,256]{1,0:T(8,128)S(1)}, u32[]{:S(2)}, u32[]{:S(2)}) %collective-permute-start.15) | collective-permute-done | bytes 49184 | tf_op jit(solution)/shard_map/ppermute | solution.py:28
  58.4 11.5 %collective-permute-start.19 = (f32[4,48,256]{2,1,0:T(8,128)S(1)}, f32[4,48,256]{2,1,0:T(8,128)S(1)}, u32[]{:S(2)}, u32[]{:S(2)}) collective-permute-start(f32[4,48,256]{2,1,0:T(8,128)S(1)} %shard_map.148.refs_0_), channel_id=1, source_target_pairs={{0,16},{4,20},{8,24},{12,28},{16,0},{20,4},{24,8},{28,12},{1,17},{... | collective-permute-start | bytes 589832 | tf_op jit(solution)/shard_map/ppermute | solution.py:28
  69.9 0.5 collective-permute-start.18
  70.4 4.8 %collective-permute-done.19.refs_4_ = f32[4,48,256]{2,1,0:T(8,128)S(1)} collective-permute-done((f32[4,48,256]{2,1,0:T(8,128)S(1)}, f32[4,48,256]{2,1,0:T(8,128)S(1)}, u32[]{:S(2)}, u32[]{:S(2)}) %collective-permute-start.19) | collective-permute-done | bytes 196640 | tf_op jit(solution)/shard_map/ppermute | solution.py:28
  75.2 1.3 collective-permute-done.21.refs_6_
  76.5 0.2 collective-permute-done.20.refs_5_
  76.6 1.3 collective-permute-done.22.refs_7_
  77.9 7.9 %shard_map.149 = (f32[48,1024]{1,0:T(8,128)S(1)}, f32[8,1024]{1,0:T(8,128)S(1)}) custom-call(s32[2]{0:T(128)S(1)} %pad_add_fusion.ids_ref, s32[1]{0:T(128)} %get-tuple-element.59.total_ref, s32[512]{0:T(512)S(1)} %get-tuple-element.60.list_ref, s32[128]{0:T(128)S(1)} %get-tuple-element.61.row_ref, bf16[128,256,512]{2,1,0:T(8,128)(2,1)} %get-tuple-element.62.pack_ref, ...), custom_call_target="tpu_custom_call" | custom-call | flops 1000000000 | bytes 16777216 | tf_op jit(solution)/shard_map/pallas_call | solution.py:48
  85.9 3.8 %collective-permute-start.27 = (f32[8,1024]{1,0:T(8,128)S(1)}, f32[8,1024]{1,0:T(8,128)S(1)}, u32[]{:S(2)}, u32[]{:S(2)}) collective-permute-start(f32[8,1024]{1,0:T(8,128)S(1)} %get-tuple-element.80.refs_0_), channel_id=1, source_target_pairs={{0,2},{1,3},{2,0},{3,1},{4,6},{5,7},{6,4},{7,5},{8,10},{9,11},{10,... | collective-permute-start | bytes 98312 | tf_op jit(solution)/shard_map/ppermute | solution.py:28
  89.7 0.5 collective-permute-start.28
  90.3 1.4 collective-permute-done.27.refs_2_
  91.7 3.8 %collective-permute-done.28.refs_3_ = f32[8,1024]{1,0:T(8,128)S(1)} collective-permute-done((f32[8,1024]{1,0:T(8,128)S(1)}, f32[8,1024]{1,0:T(8,128)S(1)}, u32[]{:S(2)}, u32[]{:S(2)}) %collective-permute-start.28) | collective-permute-done | bytes 32800 | tf_op jit(solution)/shard_map/ppermute | solution.py:28
  95.4 6.7 %shard_map.151 = (f32[48,1024]{1,0:T(8,128)S(1)}, f32[48,1024]{1,0:T(8,128)S(1)}, f32[48,1024]{1,0:T(8,128)S(1)}, f32[48,1024]{1,0:T(8,128)S(1)}, f32[48,1024]{1...) custom-call(s32[2]{0:T(128)S(1)} %pad_add_fusion.ids_ref, ...), custom_call_target="tpu_custom_call" | custom-call | flops 1000000000 | bytes 16777216 | tf_op jit(solution)/shard_map/pallas_call | solution.py:48
  102.3 0.5 collective-permute-start.32
  102.8 0.4 collective-permute-start.29
  103.3 0.4 collective-permute-done.30
  103.7 0.2 collective-permute-start.31
  104.0 6.3 %collective-permute-start.33 = (f32[48,1024]{1,0:T(8,128)S(1)}, f32[48,1024]{1,0:T(8,128)S(1)}, u32[]{:S(2)}, u32[]{:S(2)}) collective-permute-start(f32[48,1024]{1,0:T(8,128)S(1)} %add.59), channel_id=1, source_target_pairs={{0,16},{4,20},{8,24},{12,28},{16,0},{20,4},{24,8},{28,12},{1,17},{... | collective-permute-start | bytes 589832 | tf_op jit(solution)/shard_map/ppermute | solution.py:28
  110.4 0.6 slice.15
  113.7 1.1 collective-permute-start.24
  114.8 3.3 %collective-permute-start.25 = (f32[48,1024]{1,0:T(8,128)S(1)}, f32[48,1024]{1,0:T(8,128)S(1)}, u32[]{:S(2)}, u32[]{:S(2)}) collective-permute-start(f32[48,1024]{1,0:T(8,128)S(1)} %get-tuple-element.78.refs_0_.logits_ref), channel_id=1, source_target_pairs={{0,3},{1,2},{2,1},{3,0},{4,7},{5,6},{6,5},{7,4},{8,11},{9,10},{10,... | collective-permute-start | bytes 589832 | tf_op jit(solution)/shard_map/ppermute | solution.py:28
  118.1 1.4 collective-permute-done.33
  119.6 1.1 collective-permute-start.37
  120.7 2.4 %collective-permute-done.23.refs_1_ = f32[48,1024]{1,0:T(8,128)S(1)} collective-permute-done((f32[48,1024]{1,0:T(8,128)S(1)}, f32[48,1024]{1,0:T(8,128)S(1)}, u32[]{:S(2)}, u32[]{:S(2)}) %collective-permute-start.23) | collective-permute-done | bytes 196640 | tf_op jit(solution)/shard_map/ppermute | solution.py:28
  123.1 1.6 %collective-permute-start.38 = (f32[48,256]{1,0:T(8,128)S(1)}, f32[48,256]{1,0:T(8,128)S(1)}, u32[]{:S(2)}, u32[]{:S(2)}) collective-permute-start(f32[48,256]{1,0:T(8,128)S(1)} %get-tuple-element.109), channel_id=1, source_target_pairs={{0,3},{1,2},{2,1},{3,0},{4,7},{5,6},{6,5},{7,4},{8,11},{9,10},{10,... | collective-permute-start | bytes 147464 | tf_op jit(solution)/shard_map/ppermute | solution.py:28
  124.8 8.2 %collective-permute-done.24.refs_2_ = f32[48,1024]{1,0:T(8,128)S(1)} collective-permute-done((f32[48,1024]{1,0:T(8,128)S(1)}, f32[48,1024]{1,0:T(8,128)S(1)}, u32[]{:S(2)}, u32[]{:S(2)}) %collective-permute-start.24) | collective-permute-done | bytes 196640 | tf_op jit(solution)/shard_map/ppermute | solution.py:28
  133.0 1.5 shard_map.150
  134.5 3.1 %collective-permute-done.37.refs_2_ = f32[48,256]{1,0:T(8,128)S(1)} collective-permute-done((f32[48,256]{1,0:T(8,128)S(1)}, f32[48,256]{1,0:T(8,128)S(1)}, u32[]{:S(2)}, u32[]{:S(2)}) %collective-permute-start.37) | collective-permute-done | bytes 49184 | tf_op jit(solution)/shard_map/ppermute | solution.py:28
  137.6 1.2 shard_map.152
  138.9 1.5 collective-permute-done.39
  140.4 1.6 %collective-permute-start.40 = (f32[56,256]{1,0:T(8,128)S(1)}, f32[56,256]{1,0:T(8,128)S(1)}, u32[]{:S(2)}, u32[]{:S(2)}) collective-permute-start(f32[56,256]{1,0:T(8,128)S(1)} %get-tuple-element.106), channel_id=1, source_target_pairs={{0,1},{1,0},{2,3},{3,2},{4,5},{5,4},{6,7},{7,6},{8,9},{9,8},{10,11... | collective-permute-start | bytes 172040 | tf_op jit(solution)/shard_map/ppermute | solution.py:28
  142.1 0.4 collective-permute-start.41
  142.4 2.4 %collective-permute-start.42 = (f32[56,256]{1,0:T(8,128)S(1)}, f32[56,256]{1,0:T(8,128)S(1)}, u32[]{:S(2)}, u32[]{:S(2)}) collective-permute-start(f32[56,256]{1,0:T(8,128)S(1)} %get-tuple-element.107), channel_id=1, source_target_pairs={{0,3},{1,2},{2,1},{3,0},{4,7},{5,6},{6,5},{7,4},{8,11},{9,10},{10,... | collective-permute-start | bytes 172040 | tf_op jit(solution)/shard_map/ppermute | solution.py:28
  144.9 4.6 %collective-permute-done.41 = f32[56,256]{1,0:T(8,128)S(1)} collective-permute-done((f32[56,256]{1,0:T(8,128)S(1)}, f32[56,256]{1,0:T(8,128)S(1)}, u32[]{:S(2)}, u32[]{:S(2)}) %collective-permute-start.41) | collective-permute-done | bytes 57376 | tf_op jit(solution)/shard_map/ppermute | solution.py:28
  149.5 1.4 collective-permute-start.43
  150.9 1.7 %collective-permute-start.44 = (f32[56,256]{1,0:T(8,128)S(1)}, f32[56,256]{1,0:T(8,128)S(1)}, u32[]{:S(2)}, u32[]{:S(2)}) collective-permute-start(f32[56,256]{1,0:T(8,128)S(1)} %fusion.2), channel_id=1, source_target_pairs={{0,16},{4,20},{8,24},{12,28},{16,0},{20,4},{24,8},{28,12},{1,17},{... | collective-permute-start | bytes 172040 | tf_op jit(solution)/shard_map/ppermute | solution.py:28
  152.6 0.5 collective-permute-start.45
  153.1 0.9 collective-permute-done.43
  154.0 1.7 %collective-permute-done.44 = f32[56,256]{1,0:T(8,128)S(1)} collective-permute-done((f32[56,256]{1,0:T(8,128)S(1)}, f32[56,256]{1,0:T(8,128)S(1)}, u32[]{:S(2)}, u32[]{:S(2)}) %collective-permute-start.44) | collective-permute-done | bytes 57376 | tf_op jit(solution)/shard_map/ppermute | solution.py:28
  155.7 2.0 %collective-permute-done.45 = f32[56,256]{1,0:T(8,128)S(1)} collective-permute-done((f32[56,256]{1,0:T(8,128)S(1)}, f32[56,256]{1,0:T(8,128)S(1)}, u32[]{:S(2)}, u32[]{:S(2)}) %collective-permute-start.45) | collective-permute-done | bytes 57376 | tf_op jit(solution)/shard_map/ppermute | solution.py:28
  157.8 1.2 collective-permute-done.46.other_ref
  159.0 1.2 shard_map.153
  160.2 0.6 reduce
  (66 shorter events, 1.7 us)
Async XLA Ops:
  0.6 25.7 %copy-start = (f32[32,1024]{1,0:T(8,128)S(1)}, f32[32,1024]{1,0:T(8,128)}, u32[]{:S(2)}) copy-start(f32[32,1024]{1,0:T(8,128)} %refs_0_) | copy-start | bytes 393220
  0.6 25.7 %collective-permute-start = (f32[32,1024]{1,0:T(8,128)}, f32[32,1024]{1,0:T(8,128)S(1)}, u32[]{:S(2)}, u32[]{:S(2)}) collective-permute-start(f32[32,1024]{1,0:T(8,128)} %refs_0_), channel_id=1, source_target_pairs={{0,8},{4,12},{8,0},{12,4},{16,24},{20,28},{24,16},{28,20},{1,9},{5... | collective-permute-start | bytes 393224 | tf_op jit(solution)/shard_map/ppermute | solution.py:28
  3.6 22.7 %collective-permute-start.1 = (f32[32,1024]{1,0:T(8,128)}, f32[32,1024]{1,0:T(8,128)S(1)}, u32[]{:S(2)}, u32[]{:S(2)}) collective-permute-start(f32[32,1024]{1,0:T(8,128)} %refs_0_), channel_id=1, source_target_pairs={{0,16},{4,20},{8,24},{12,28},{16,0},{20,4},{24,8},{28,12},{1,17},{... | collective-permute-start | bytes 393224 | tf_op jit(solution)/shard_map/ppermute | solution.py:28
  5.2 21.2 %collective-permute-start.2 = (f32[32,1024]{1,0:T(8,128)}, f32[32,1024]{1,0:T(8,128)S(1)}, u32[]{:S(2)}, u32[]{:S(2)}) collective-permute-start(f32[32,1024]{1,0:T(8,128)} %refs_0_), channel_id=1, source_target_pairs={{0,24},{4,28},{8,16},{12,20},{16,8},{20,12},{24,0},{28,4},{1,25},{... | collective-permute-start | bytes 393224 | tf_op jit(solution)/shard_map/ppermute | solution.py:28
  7.8 0.7 copy-start.2
  8.5 0.7 copy-start.4
  9.2 68.7 %copy-start.1 = (s32[1024]{0:T(1024)S(1)}, s32[1024]{0:T(1024)}, u32[]{:S(2)}) copy-start(s32[1024]{0:T(1024)} %param.14) | copy-start | bytes 12292
  26.4 3.1 %collective-permute-start.3 = (f32[32,1024]{1,0:T(8,128)S(1)}, f32[32,1024]{1,0:T(8,128)S(1)}, u32[]{:S(2)}, u32[]{:S(2)}) collective-permute-start(f32[32,1024]{1,0:T(8,128)S(1)} %copy-done), channel_id=1, source_target_pairs={{0,4},{4,0},{8,12},{12,8},{16,20},{20,16},{24,28},{28,24},{1,5},{5... | collective-permute-start | bytes 393224 | tf_op jit(solution)/shard_map/ppermute | solution.py:28
  26.4 5.6 %collective-permute-start.4 = (f32[32,1024]{1,0:T(8,128)S(1)}, f32[32,1024]{1,0:T(8,128)S(1)}, u32[]{:S(2)}, u32[]{:S(2)}) collective-permute-start(f32[32,1024]{1,0:T(8,128)S(1)} %collective-permute-done.refs_2_), channel_id=1, source_target_pairs={{0,4},{4,0},{8,12},{12,8},{16,20},{20,16},{24,28},{28,24},{1,5},{5... | collective-permute-start | bytes 393224 | tf_op jit(solution)/shard_map/ppermute | solution.py:28
  26.9 5.2 %collective-permute-start.5 = (f32[32,1024]{1,0:T(8,128)S(1)}, f32[32,1024]{1,0:T(8,128)S(1)}, u32[]{:S(2)}, u32[]{:S(2)}) collective-permute-start(f32[32,1024]{1,0:T(8,128)S(1)} %collective-permute-done.1.refs_4_), channel_id=1, source_target_pairs={{0,4},{4,0},{8,12},{12,8},{16,20},{20,16},{24,28},{28,24},{1,5},{5... | collective-permute-start | bytes 393224 | tf_op jit(solution)/shard_map/ppermute | solution.py:28
  27.0 5.2 %collective-permute-start.6 = (f32[32,1024]{1,0:T(8,128)S(1)}, f32[32,1024]{1,0:T(8,128)S(1)}, u32[]{:S(2)}, u32[]{:S(2)}) collective-permute-start(f32[32,1024]{1,0:T(8,128)S(1)} %collective-permute-done.2.refs_6_), channel_id=1, source_target_pairs={{0,4},{4,0},{8,12},{12,8},{16,20},{20,16},{24,28},{28,24},{1,5},{5... | collective-permute-start | bytes 393224 | tf_op jit(solution)/shard_map/ppermute | solution.py:28
  27.4 16.7 %collective-permute-start.10 = (f32[96,256]{1,0:T(8,128)S(1)}, f32[96,256]{1,0:T(8,128)S(1)}, u32[]{:S(2)}, u32[]{:S(2)}) collective-permute-start(f32[96,256]{1,0:T(8,128)S(1)} %maximum_maximum_fusion.refs_4_), channel_id=1, source_target_pairs={{0,1},{1,0},{2,3},{3,2},{4,5},{5,4},{6,7},{7,6},{8,9},{9,8},{10,11... | collective-permute-start | bytes 294920 | tf_op jit(solution)/shard_map/ppermute | solution.py:28
  29.5 14.8 %collective-permute-start.11 = (f32[96,256]{1,0:T(8,128)S(1)}, f32[96,256]{1,0:T(8,128)S(1)}, u32[]{:S(2)}, u32[]{:S(2)}) collective-permute-start(f32[96,256]{1,0:T(8,128)S(1)} %maximum_maximum_fusion.refs_4_), channel_id=1, source_target_pairs={{0,2},{1,3},{2,0},{3,1},{4,6},{5,7},{6,4},{7,5},{8,10},{9,11},{10,... | collective-permute-start | bytes 294920 | tf_op jit(solution)/shard_map/ppermute | solution.py:28
  32.1 12.2 %collective-permute-start.12 = (f32[96,256]{1,0:T(8,128)S(1)}, f32[96,256]{1,0:T(8,128)S(1)}, u32[]{:S(2)}, u32[]{:S(2)}) collective-permute-start(f32[96,256]{1,0:T(8,128)S(1)} %maximum_maximum_fusion.refs_4_), channel_id=1, source_target_pairs={{0,3},{1,2},{2,1},{3,0},{4,7},{5,6},{6,5},{7,4},{8,11},{9,10},{10,... | collective-permute-start | bytes 294920 | tf_op jit(solution)/shard_map/ppermute | solution.py:28
  32.2 63.3 %copy-start.3 = (s32[1024]{0:T(1024)S(1)}, s32[1024]{0:T(1024)}, u32[]{:S(2)}) copy-start(s32[1024]{0:T(1024)} %param.15) | copy-start | bytes 12292
  39.8 4.5 %collective-permute-start.7 = (f32[32,256]{1,0:T(8,128)S(1)}, f32[32,256]{1,0:T(8,128)S(1)}, u32[]{:S(2)}, u32[]{:S(2)}) collective-permute-start(f32[32,256]{1,0:T(8,128)S(1)} %get-tuple-element.70), channel_id=1, source_target_pairs={{0,1},{1,0},{2,3},{3,2},{4,5},{5,4},{6,7},{7,6},{8,9},{9,8},{10,11... | collective-permute-start | bytes 98312 | tf_op jit(solution)/shard_map/ppermute | solution.py:28
  40.7 5.7 %collective-permute-start.8 = (f32[32,256]{1,0:T(8,128)S(1)}, f32[32,256]{1,0:T(8,128)S(1)}, u32[]{:S(2)}, u32[]{:S(2)}) collective-permute-start(f32[32,256]{1,0:T(8,128)S(1)} %get-tuple-element.71), channel_id=1, source_target_pairs={{0,2},{1,3},{2,0},{3,1},{4,6},{5,7},{6,4},{7,5},{8,10},{9,11},{10,... | collective-permute-start | bytes 98312 | tf_op jit(solution)/shard_map/ppermute | solution.py:28
  44.1 5.7 %collective-permute-start.9 = (f32[32,256]{1,0:T(8,128)S(1)}, f32[32,256]{1,0:T(8,128)S(1)}, u32[]{:S(2)}, u32[]{:S(2)}) collective-permute-start(f32[32,256]{1,0:T(8,128)S(1)} %get-tuple-element.72), channel_id=1, source_target_pairs={{0,3},{1,2},{2,1},{3,0},{4,7},{5,6},{6,5},{7,4},{8,11},{9,10},{10,... | collective-permute-start | bytes 98312 | tf_op jit(solution)/shard_map/ppermute | solution.py:28
  51.2 4.5 %collective-permute-start.13 = (f32[48,256]{1,0:T(8,128)S(1)}, f32[48,256]{1,0:T(8,128)S(1)}, u32[]{:S(2)}, u32[]{:S(2)}) collective-permute-start(f32[48,256]{1,0:T(8,128)S(1)} %get-tuple-element.75), channel_id=1, source_target_pairs={{0,1},{1,0},{2,3},{3,2},{4,5},{5,4},{6,7},{7,6},{8,9},{9,8},{10,11... | collective-permute-start | bytes 147464 | tf_op jit(solution)/shard_map/ppermute | solution.py:28
  51.3 5.1 %collective-permute-start.14 = (f32[48,256]{1,0:T(8,128)S(1)}, f32[48,256]{1,0:T(8,128)S(1)}, u32[]{:S(2)}, u32[]{:S(2)}) collective-permute-start(f32[48,256]{1,0:T(8,128)S(1)} %get-tuple-element.76), channel_id=1, source_target_pairs={{0,2},{1,3},{2,0},{3,1},{4,6},{5,7},{6,4},{7,5},{8,10},{9,11},{10,... | collective-permute-start | bytes 147464 | tf_op jit(solution)/shard_map/ppermute | solution.py:28
  52.2 6.1 %collective-permute-start.15 = (f32[48,256]{1,0:T(8,128)S(1)}, f32[48,256]{1,0:T(8,128)S(1)}, u32[]{:S(2)}, u32[]{:S(2)}) collective-permute-start(f32[48,256]{1,0:T(8,128)S(1)} %get-tuple-element.77), channel_id=1, source_target_pairs={{0,3},{1,2},{2,1},{3,0},{4,7},{5,6},{6,5},{7,4},{8,11},{9,10},{10,... | collective-permute-start | bytes 147464 | tf_op jit(solution)/shard_map/ppermute | solution.py:28
  58.3 11.7 %collective-permute-start.17 = (f32[4,48,256]{2,1,0:T(8,128)S(1)}, f32[4,48,256]{2,1,0:T(8,128)S(1)}, u32[]{:S(2)}, u32[]{:S(2)}) collective-permute-start(f32[4,48,256]{2,1,0:T(8,128)S(1)} %shard_map.148.refs_0_), channel_id=1, source_target_pairs={{0,8},{4,12},{8,0},{12,4},{16,24},{20,28},{24,16},{28,20},{1,9},{5... | collective-permute-start | bytes 589832 | tf_op jit(solution)/shard_map/ppermute | solution.py:28
  58.4 16.8 %collective-permute-start.19 = (f32[4,48,256]{2,1,0:T(8,128)S(1)}, f32[4,48,256]{2,1,0:T(8,128)S(1)}, u32[]{:S(2)}, u32[]{:S(2)}) collective-permute-start(f32[4,48,256]{2,1,0:T(8,128)S(1)} %shard_map.148.refs_0_), channel_id=1, source_target_pairs={{0,16},{4,20},{8,24},{12,28},{16,0},{20,4},{24,8},{28,12},{1,17},{... | collective-permute-start | bytes 589832 | tf_op jit(solution)/shard_map/ppermute | solution.py:28
  69.9 6.6 %collective-permute-start.21 = (f32[4,48,256]{2,1,0:T(8,128)S(1)}, f32[4,48,256]{2,1,0:T(8,128)S(1)}, u32[]{:S(2)}, u32[]{:S(2)}) collective-permute-start(f32[4,48,256]{2,1,0:T(8,128)S(1)} %shard_map.148.refs_0_), channel_id=1, source_target_pairs={{0,24},{4,28},{8,16},{12,20},{16,8},{20,12},{24,0},{28,4},{1,25},{... | collective-permute-start | bytes 589832 | tf_op jit(solution)/shard_map/ppermute | solution.py:28
  69.9 6.6 %collective-permute-start.16 = (f32[4,48,256]{2,1,0:T(8,128)S(1)}, f32[4,48,256]{2,1,0:T(8,128)S(1)}, u32[]{:S(2)}, u32[]{:S(2)}) collective-permute-start(f32[4,48,256]{2,1,0:T(8,128)S(1)} %shard_map.148.refs_0_), channel_id=1, source_target_pairs={{0,4},{4,0},{8,12},{12,8},{16,20},{20,16},{24,28},{28,24},{1,5},{5... | collective-permute-start | bytes 589832 | tf_op jit(solution)/shard_map/ppermute | solution.py:28
  69.9 6.6 %collective-permute-start.18 = (f32[4,48,256]{2,1,0:T(8,128)S(1)}, f32[4,48,256]{2,1,0:T(8,128)S(1)}, u32[]{:S(2)}, u32[]{:S(2)}) collective-permute-start(f32[4,48,256]{2,1,0:T(8,128)S(1)} %collective-permute-done.17.refs_2_), channel_id=1, source_target_pairs={{0,4},{4,0},{8,12},{12,8},{16,20},{20,16},{24,28},{28,24},{1,5},{5... | collective-permute-start | bytes 589832 | tf_op jit(solution)/shard_map/ppermute | solution.py:28
  75.2 1.4 collective-permute-start.20
  76.5 1.4 collective-permute-start.22
  85.8 4.5 %collective-permute-start.26 = (f32[8,1024]{1,0:T(8,128)S(1)}, f32[8,1024]{1,0:T(8,128)S(1)}, u32[]{:S(2)}, u32[]{:S(2)}) collective-permute-start(f32[8,1024]{1,0:T(8,128)S(1)} %get-tuple-element.80.refs_0_), channel_id=1, source_target_pairs={{0,1},{1,0},{2,3},{3,2},{4,5},{5,4},{6,7},{7,6},{8,9},{9,8},{10,11... | collective-permute-start | bytes 98312 | tf_op jit(solution)/shard_map/ppermute | solution.py:28
  85.9 5.8 %collective-permute-start.27 = (f32[8,1024]{1,0:T(8,128)S(1)}, f32[8,1024]{1,0:T(8,128)S(1)}, u32[]{:S(2)}, u32[]{:S(2)}) collective-permute-start(f32[8,1024]{1,0:T(8,128)S(1)} %get-tuple-element.80.refs_0_), channel_id=1, source_target_pairs={{0,2},{1,3},{2,0},{3,1},{4,6},{5,7},{6,4},{7,5},{8,10},{9,11},{10,... | collective-permute-start | bytes 98312 | tf_op jit(solution)/shard_map/ppermute | solution.py:28
  89.7 5.7 %collective-permute-start.28 = (f32[8,1024]{1,0:T(8,128)S(1)}, f32[8,1024]{1,0:T(8,128)S(1)}, u32[]{:S(2)}, u32[]{:S(2)}) collective-permute-start(f32[8,1024]{1,0:T(8,128)S(1)} %get-tuple-element.80.refs_0_), channel_id=1, source_target_pairs={{0,3},{1,2},{2,1},{3,0},{4,7},{5,6},{6,5},{7,4},{8,11},{9,10},{10,... | collective-permute-start | bytes 98312 | tf_op jit(solution)/shard_map/ppermute | solution.py:28
  102.2 1.5 collective-permute-start.30
  102.3 1.7 %collective-permute-start.32 = (f32[48,1024]{1,0:T(8,128)S(1)}, f32[48,1024]{1,0:T(8,128)S(1)}, u32[]{:S(2)}, u32[]{:S(2)}) collective-permute-start(f32[48,1024]{1,0:T(8,128)S(1)} %get-tuple-element.86), channel_id=1, source_target_pairs={{0,4},{4,0},{8,12},{12,8},{16,20},{20,16},{24,28},{28,24},{1,5},{5... | collective-permute-start | bytes 589832 | tf_op jit(solution)/shard_map/ppermute | solution.py:28
  102.8 7.5 %collective-permute-start.34 = (f32[48,1024]{1,0:T(8,128)S(1)}, f32[48,1024]{1,0:T(8,128)S(1)}, u32[]{:S(2)}, u32[]{:S(2)}) collective-permute-start(f32[48,1024]{1,0:T(8,128)S(1)} %get-tuple-element.88), channel_id=1, source_target_pairs={{0,4},{4,0},{8,12},{12,8},{16,20},{20,16},{24,28},{28,24},{1,5},{5... | collective-permute-start | bytes 589832 | tf_op jit(solution)/shard_map/ppermute | solution.py:28
  102.8 10.8 %collective-permute-start.29 = (f32[48,1024]{1,0:T(8,128)S(1)}, f32[48,1024]{1,0:T(8,128)S(1)}, u32[]{:S(2)}, u32[]{:S(2)}) collective-permute-start(f32[48,1024]{1,0:T(8,128)S(1)} %get-tuple-element.82), channel_id=1, source_target_pairs={{0,4},{4,0},{8,12},{12,8},{16,20},{20,16},{24,28},{28,24},{1,5},{5... | collective-permute-start | bytes 589832 | tf_op jit(solution)/shard_map/ppermute | solution.py:28
  103.7 11.0 %collective-permute-start.31 = (f32[48,1024]{1,0:T(8,128)S(1)}, f32[48,1024]{1,0:T(8,128)S(1)}, u32[]{:S(2)}, u32[]{:S(2)}) collective-permute-start(f32[48,1024]{1,0:T(8,128)S(1)} %add.57), channel_id=1, source_target_pairs={{0,8},{4,12},{8,0},{12,4},{16,24},{20,28},{24,16},{28,20},{1,9},{5... | collective-permute-start | bytes 589832 | tf_op jit(solution)/shard_map/ppermute | solution.py:28
  104.0 15.4 %collective-permute-start.33 = (f32[48,1024]{1,0:T(8,128)S(1)}, f32[48,1024]{1,0:T(8,128)S(1)}, u32[]{:S(2)}, u32[]{:S(2)}) collective-permute-start(f32[48,1024]{1,0:T(8,128)S(1)} %add.59), channel_id=1, source_target_pairs={{0,16},{4,20},{8,24},{12,28},{16,0},{20,4},{24,8},{28,12},{1,17},{... | collective-permute-start | bytes 589832 | tf_op jit(solution)/shard_map/ppermute | solution.py:28
  110.3 9.1 %collective-permute-start.35 = (f32[48,1024]{1,0:T(8,128)S(1)}, f32[48,1024]{1,0:T(8,128)S(1)}, u32[]{:S(2)}, u32[]{:S(2)}) collective-permute-start(f32[48,1024]{1,0:T(8,128)S(1)} %add.61), channel_id=1, source_target_pairs={{0,24},{4,28},{8,16},{12,20},{16,8},{20,12},{24,0},{28,4},{1,25},{... | collective-permute-start | bytes 589832 | tf_op jit(solution)/shard_map/ppermute | solution.py:28
  113.6 9.5 %collective-permute-start.23 = (f32[48,1024]{1,0:T(8,128)S(1)}, f32[48,1024]{1,0:T(8,128)S(1)}, u32[]{:S(2)}, u32[]{:S(2)}) collective-permute-start(f32[48,1024]{1,0:T(8,128)S(1)} %get-tuple-element.78.refs_0_.logits_ref), channel_id=1, source_target_pairs={{0,1},{1,0},{2,3},{3,2},{4,5},{5,4},{6,7},{7,6},{8,9},{9,8},{10,11... | collective-permute-start | bytes 589832 | tf_op jit(solution)/shard_map/ppermute | solution.py:28
  113.7 19.3 %collective-permute-start.24 = (f32[48,1024]{1,0:T(8,128)S(1)}, f32[48,1024]{1,0:T(8,128)S(1)}, u32[]{:S(2)}, u32[]{:S(2)}) collective-permute-start(f32[48,1024]{1,0:T(8,128)S(1)} %get-tuple-element.78.refs_0_.logits_ref), channel_id=1, source_target_pairs={{0,2},{1,3},{2,0},{3,1},{4,6},{5,7},{6,4},{7,5},{8,10},{9,11},{10,... | collective-permute-start | bytes 589832 | tf_op jit(solution)/shard_map/ppermute | solution.py:28
  114.8 18.2 %collective-permute-start.25 = (f32[48,1024]{1,0:T(8,128)S(1)}, f32[48,1024]{1,0:T(8,128)S(1)}, u32[]{:S(2)}, u32[]{:S(2)}) collective-permute-start(f32[48,1024]{1,0:T(8,128)S(1)} %get-tuple-element.78.refs_0_.logits_ref), channel_id=1, source_target_pairs={{0,3},{1,2},{2,1},{3,0},{4,7},{5,6},{6,5},{7,4},{8,11},{9,10},{10,... | collective-permute-start | bytes 589832 | tf_op jit(solution)/shard_map/ppermute | solution.py:28
  119.5 14.9 %collective-permute-start.36 = (f32[48,256]{1,0:T(8,128)S(1)}, f32[48,256]{1,0:T(8,128)S(1)}, u32[]{:S(2)}, u32[]{:S(2)}) collective-permute-start(f32[48,256]{1,0:T(8,128)S(1)} %get-tuple-element.111), channel_id=1, source_target_pairs={{0,1},{1,0},{2,3},{3,2},{4,5},{5,4},{6,7},{7,6},{8,9},{9,8},{10,11... | collective-permute-start | bytes 147464 | tf_op jit(solution)/shard_map/ppermute | solution.py:28
  119.6 18.0 %collective-permute-start.37 = (f32[48,256]{1,0:T(8,128)S(1)}, f32[48,256]{1,0:T(8,128)S(1)}, u32[]{:S(2)}, u32[]{:S(2)}) collective-permute-start(f32[48,256]{1,0:T(8,128)S(1)} %get-tuple-element.110), channel_id=1, source_target_pairs={{0,2},{1,3},{2,0},{3,1},{4,6},{5,7},{6,4},{7,5},{8,10},{9,11},{10,... | collective-permute-start | bytes 147464 | tf_op jit(solution)/shard_map/ppermute | solution.py:28
  123.1 14.4 %collective-permute-start.38 = (f32[48,256]{1,0:T(8,128)S(1)}, f32[48,256]{1,0:T(8,128)S(1)}, u32[]{:S(2)}, u32[]{:S(2)}) collective-permute-start(f32[48,256]{1,0:T(8,128)S(1)} %get-tuple-element.109), channel_id=1, source_target_pairs={{0,3},{1,2},{2,1},{3,0},{4,7},{5,6},{6,5},{7,4},{8,11},{9,10},{10,... | collective-permute-start | bytes 147464 | tf_op jit(solution)/shard_map/ppermute | solution.py:28
  138.8 1.6 collective-permute-start.39
  140.4 4.5 %collective-permute-start.40 = (f32[56,256]{1,0:T(8,128)S(1)}, f32[56,256]{1,0:T(8,128)S(1)}, u32[]{:S(2)}, u32[]{:S(2)}) collective-permute-start(f32[56,256]{1,0:T(8,128)S(1)} %get-tuple-element.106), channel_id=1, source_target_pairs={{0,1},{1,0},{2,3},{3,2},{4,5},{5,4},{6,7},{7,6},{8,9},{9,8},{10,11... | collective-permute-start | bytes 172040 | tf_op jit(solution)/shard_map/ppermute | solution.py:28
  142.1 7.4 %collective-permute-start.41 = (f32[56,256]{1,0:T(8,128)S(1)}, f32[56,256]{1,0:T(8,128)S(1)}, u32[]{:S(2)}, u32[]{:S(2)}) collective-permute-start(f32[56,256]{1,0:T(8,128)S(1)} %get-tuple-element.108), channel_id=1, source_target_pairs={{0,2},{1,3},{2,0},{3,1},{4,6},{5,7},{6,4},{7,5},{8,10},{9,11},{10,... | collective-permute-start | bytes 172040 | tf_op jit(solution)/shard_map/ppermute | solution.py:28
  142.4 7.1 %collective-permute-start.42 = (f32[56,256]{1,0:T(8,128)S(1)}, f32[56,256]{1,0:T(8,128)S(1)}, u32[]{:S(2)}, u32[]{:S(2)}) collective-permute-start(f32[56,256]{1,0:T(8,128)S(1)} %get-tuple-element.107), channel_id=1, source_target_pairs={{0,3},{1,2},{2,1},{3,0},{4,7},{5,6},{6,5},{7,4},{8,11},{9,10},{10,... | collective-permute-start | bytes 172040 | tf_op jit(solution)/shard_map/ppermute | solution.py:28
  149.5 4.5 %collective-permute-start.43 = (f32[56,256]{1,0:T(8,128)S(1)}, f32[56,256]{1,0:T(8,128)S(1)}, u32[]{:S(2)}, u32[]{:S(2)}) collective-permute-start(f32[56,256]{1,0:T(8,128)S(1)} %fusion.2), channel_id=1, source_target_pairs={{0,8},{4,12},{8,0},{12,4},{16,24},{20,28},{24,16},{28,20},{1,9},{5... | collective-permute-start | bytes 172040 | tf_op jit(solution)/shard_map/ppermute | solution.py:28
  150.9 4.8 %collective-permute-start.44 = (f32[56,256]{1,0:T(8,128)S(1)}, f32[56,256]{1,0:T(8,128)S(1)}, u32[]{:S(2)}, u32[]{:S(2)}) collective-permute-start(f32[56,256]{1,0:T(8,128)S(1)} %fusion.2), channel_id=1, source_target_pairs={{0,16},{4,20},{8,24},{12,28},{16,0},{20,4},{24,8},{28,12},{1,17},{... | collective-permute-start | bytes 172040 | tf_op jit(solution)/shard_map/ppermute | solution.py:28
  152.6 5.1 %collective-permute-start.45 = (f32[56,256]{1,0:T(8,128)S(1)}, f32[56,256]{1,0:T(8,128)S(1)}, u32[]{:S(2)}, u32[]{:S(2)}) collective-permute-start(f32[56,256]{1,0:T(8,128)S(1)} %fusion.2), channel_id=1, source_target_pairs={{0,24},{4,28},{8,16},{12,20},{16,8},{20,12},{24,0},{28,4},{1,25},{... | collective-permute-start | bytes 172040 | tf_op jit(solution)/shard_map/ppermute | solution.py:28
  157.7 1.3 collective-permute-start.46

commit v2 on v1

--- a/solution.py
+++ b/solution.py
@@ -9,9 +9,11 @@
 
 BLOCK = 128
 CHUNK = 4
-UNROLL = 2
+UNROLL = 4
 FETCH = 4
+RING = 16
 PAD = 48
+HALF = 24
 
 f32 = jnp.float32
 bf16 = jnp.bfloat16
@@ -56,16 +58,39 @@
     )(*args)
 
 
-def pack_body(count_ref, column_ref, tiles_ref, pack_ref, list_ref, row_ref, total_ref, land, store, place, owner, sem, out_sem):
+def as_column(row):
+    size = row.shape[1]
+    shape = (size, size)
+    same = lax.broadcasted_iota(jnp.int32, shape, 0) == lax.broadcasted_iota(jnp.int32, shape, 1)
+    return jnp.sum(jnp.where(same, row, 0.0), axis=1, keepdims=True)
+
+
+def as_row(column):
+    size = column.shape[0]
+    shape = (size, size)
+    same = lax.broadcasted_iota(jnp.int32, shape, 0) == lax.broadcasted_iota(jnp.int32, shape, 1)
+    return jnp.sum(jnp.where(same, column, 0.0), axis=0, keepdims=True)
+
+
+def pack_body(
+    count_in, column_in, tiles_ref, pack_ref, list_ref, row_ref, total_ref,
+    count_ref, column_ref, land, store, place, owner, twin_from, twin_to, sem, out_sem, list_sem,
+):
     rows, slots = column_ref.shape
+    lists = [
+        pltpu.make_async_copy(count_in, count_ref, list_sem.at[0]),
+        pltpu.make_async_copy(column_in, column_ref, list_sem.at[1]),
+    ]
+    for copy in lists:
+        copy.start()
+    for copy in lists:
+        copy.wait()
 
     def copies(row, act):
-        buffer = lax.rem(row, 2)
-
         def one(group, _):
             part = pl.ds(group * FETCH, FETCH)
             copy = pltpu.make_async_copy(
-                tiles_ref.at[row, part], land.at[buffer, part], sem.at[buffer, group]
+                tiles_ref.at[row, part], land.at[pl.ds(row * slots + group * FETCH, FETCH)], sem.at[row, group]
             )
             act(copy)
             return 0
@@ -73,7 +98,12 @@
         lax.fori_loop(0, (count_ref[row] + FETCH - 1) // FETCH, one, 0)
 
     def leave(item):
-        return pltpu.make_async_copy(store.at[item], pack_ref.at[item], out_sem.at[item])
+        return pltpu.make_async_copy(store.at[lax.rem(item, RING)], pack_ref.at[item], out_sem.at[lax.rem(item, RING)])
+
+    def free(item):
+        @pl.when(item >= RING)
+        def _():
+            leave(item - RING).wait()
 
     def start(copy):
         copy.start()
@@ -81,74 +111,72 @@
     def wait(copy):
         copy.wait()
 
-    def blank_item(item):
-        for q in range(CHUNK):
-            list_ref[item * CHUNK + q] = 0
-
-    copies(0, start)
+    for row in range(rows):
+        copies(row, start)
+    land[rows * slots] = jnp.zeros((BLOCK, BLOCK), f32)
+
+    def clear(index, _):
+        place[index] = -1
+        return 0
+
+    lax.fori_loop(0, place.shape[0], clear, 0)
 
     def one_row(row, begin):
-        buffer = lax.rem(row, 2)
-        live = count_ref[row]
-
-        @pl.when(row + 1 < rows)
-        def _():
-            copies(row + 1, start)
-
-        def clear(slot, _):
-            place[column_ref[row, slot]] = -1
-            return 0
-
-        lax.fori_loop(0, live, clear, 0)
-        copies(row, wait)
-
-        def scan(slot, found):
+        stamp = row * slots
+
+        def scan(slot, state):
+            found, twins = state
             column = column_ref[row, slot]
             at = place[column]
-            fresh = at < 0
+            fresh = at < stamp
 
             @pl.when(fresh)
             def _():
-                place[column] = slot
-                owner[found] = slot
+                place[column] = stamp + slot
+                owner[found] = stamp + slot
                 list_ref[begin * CHUNK + found] = column
 
             @pl.when(jnp.logical_not(fresh))
             def _():
-                land[buffer, at] = land[buffer, at] + land[buffer, slot]
-
-            return found + fresh.astype(jnp.int32)
-
-        found = lax.fori_loop(0, live, scan, 0)
+                twin_from[twins] = stamp + slot
+                twin_to[twins] = at
+
+            step = fresh.astype(jnp.int32)
+            return found + step, twins + 1 - step
+
+        found, twins = lax.fori_loop(0, count_ref[row], scan, (0, 0))
         steps = (found + CHUNK - 1) // CHUNK
 
         def blank(index, _):
             list_ref[begin * CHUNK + index] = 0
+            owner[index] = rows * slots
             return 0
 
         lax.fori_loop(found, steps * CHUNK, blank, 0)
+        copies(row, wait)
+
+        def join(index, _):
+            to = twin_to[index]
+            land[to] = land[to] + land[twin_from[index]]
+            return 0
+
+        lax.fori_loop(0, twins, join, 0)
 
         def convert(step, _):
             item = begin + step
             row_ref[item] = row
+            free(item)
+            place_at = lax.rem(item, RING)
             for q in range(CHUNK):
-                index = step * CHUNK + q
                 at = slice(q * BLOCK, (q + 1) * BLOCK)
-
-                @pl.when(index < found)
-                def _():
-                    high, low = split(land[buffer, owner[index]])
-                    store[item, :BLOCK, at] = high
-                    store[item, BLOCK:, at] = low
-
-                @pl.when(index >= found)
-                def _():
-                    store[item, :, at] = jnp.zeros((2 * BLOCK, BLOCK), bf16)
-
+                high, low = split(land[owner[step * CHUNK + q]])
+                store[place_at, :BLOCK, at] = high
+                store[place_at, BLOCK:, at] = low
             leave(item).start()
             return 0
 
         lax.fori_loop(0, steps, convert, 0)
+
         return begin + steps
 
     used = lax.fori_loop(0, rows, one_row, 0)
@@ -156,8 +184,10 @@
 
     def fill(item, _):
         row_ref[item] = 0
-        blank_item(item)
-        store[item] = jnp.zeros(store.shape[1:], bf16)
+        for q in range(CHUNK):
+            list_ref[item * CHUNK + q] = 0
+        free(item)
+        store[lax.rem(item, RING)] = jnp.zeros(store.shape[1:], bf16)
         leave(item).start()
         return 0
 
@@ -168,7 +198,7 @@
         leave(item).wait()
         return 0
 
-    lax.fori_loop(0, total, last, 0)
+    lax.fori_loop(jnp.maximum(total - RING, 0), total, last, 0)
 
 
 def pack(tiles, tile_column, tile_count, block_total):
@@ -184,19 +214,24 @@
             shape((1,), jnp.int32),
         ],
         [
-            pltpu.VMEM((2, slots, BLOCK, BLOCK), f32),
-            pltpu.VMEM((items, 2 * BLOCK, CHUNK * BLOCK), bf16),
+            pltpu.SMEM(tile_count.shape, jnp.int32),
+            pltpu.SMEM(tile_column.shape, jnp.int32),
+            pltpu.VMEM((rows * slots + 1, BLOCK, BLOCK), f32),
+            pltpu.VMEM((RING, 2 * BLOCK, CHUNK * BLOCK), bf16),
             pltpu.SMEM((block_total,), jnp.int32),
             pltpu.SMEM((slots,), jnp.int32),
-            pltpu.SemaphoreType.DMA((2, slots // FETCH)),
-            pltpu.SemaphoreType.DMA((items,)),
+            pltpu.SMEM((slots,), jnp.int32),
+            pltpu.SMEM((slots,), jnp.int32),
+            pltpu.SemaphoreType.DMA((rows, slots // FETCH)),
+            pltpu.SemaphoreType.DMA((RING,)),
+            pltpu.SemaphoreType.DMA((2,)),
         ],
         tile_count,
         tile_column,
         tiles,
-        specs=[SMEM, SMEM, pl.BlockSpec(memory_space=pl.ANY)],
+        specs=[pl.BlockSpec(memory_space=pl.ANY)] * 3,
         out_specs=[pl.BlockSpec(memory_space=pltpu.HBM), SMEM, SMEM, SMEM],
-        limit=48,
+        limit=52,
         flops=10**8,
         moved=40 * MIB,
     )
@@ -278,16 +313,20 @@
     mixed = held[...].reshape(mixed_ref.shape)
     mixed_ref[...] = mixed
     weight_in = held_weights[:, :feats].reshape(feats * cols, units)
-    weight_tail = held_weights[:, feats:].reshape(units, units)
-    weight_out_ref[...] = weight_tail[:, :classes]
-    inner = product(weight_in, mixed, ((0,), (0,))) + weight_tail[:, classes : classes + 1]
+    own = units // cols
+    weight_out = held_weights[:, feats : feats + own].reshape(units, units)[:, :classes]
+    weight_out_ref[...] = weight_out
+    bias_in = jnp.concatenate(
+        [held_weights[group, feats + own : feats + own + 1, :own] for group in range(cols)], axis=1
+    )
+    inner = product(weight_in, mixed, ((0,), (0,))) + as_column(bias_in)
     bend = jnp.tanh(CURVE * (inner + CUBIC * inner * inner * inner))
     hidden = 0.5 * inner * (1.0 + bend)
     hidden_ref[...] = hidden
     slope_ref[...] = 0.5 * (1.0 + bend) + (0.5 * inner) * (1.0 - bend * bend) * (
         CURVE * (1.0 + 3.0 * CUBIC * inner * inner)
     )
-    value = product(weight_out_ref[...], hidden, ((0,), (0,)))
+    value = product(weight_out, hidden, ((0,), (0,)))
     scores[...] = jnp.zeros_like(scores)
     for group in range(cols):
         scores[group, :per] = value[group * per : (group + 1) * per]
@@ -302,11 +341,15 @@
 
 def mix_out_body(nodes, cols, per, ids_ref, total_ref, list_ref, row_ref, pack_ref, bias_ref, labels_ref, *refs):
     pieces = refs[:nodes]
-    logits_ref, stats_ref, values, sums, store, sem = refs[nodes:]
+    upper_ref, lower_ref, stats_ref, values, sums, groups, store, sem = refs[nodes:]
     one = bring(total_ref, pack_ref, store, sem)
     rows = sums.shape[0]
     node, col = ids_ref[0], ids_ref[1]
     slice_rows = rows // cols
+    column = as_column(bias_ref[...])
+    groups[...] = jnp.zeros_like(groups)
+    for group in range(cols):
+        groups[group, :per] = column[group * per : (group + 1) * per]
     for offset in range(nodes):
         base = (node ^ offset) * rows
         for group in range(cols):
@@ -318,8 +361,11 @@
                 )
     mix_rows(total_ref, list_ref, row_ref, one, store, values, sums)
     for row in range(rows):
-        logits_ref[:, row * BLOCK : (row + 1) * BLOCK] = mixed_row(sums, row) + bias_ref[col]
-    logits = logits_ref[...]
+        at = slice(row * BLOCK, (row + 1) * BLOCK)
+        total = mixed_row(sums, row) + groups[col]
+        upper_ref[:, at] = total[:HALF]
+        lower_ref[:, at] = total[HALF:]
+    logits = jnp.concatenate([upper_ref[...], lower_ref[...]], axis=0)
     place = lax.broadcasted_iota(jnp.int32, logits.shape, 0)
     inside = place < per
     top = jnp.max(jnp.where(inside, logits, -jnp.inf), axis=0, keepdims=True)
@@ -332,7 +378,7 @@
     stats_ref[2:3] = chosen
 
 
-def mix_back_body(nodes, cols, per, ids_ref, total_ref, list_ref, row_ref, pack_ref, logits_ref, labels_ref, mask_ref, *refs):
+def mix_back_body(nodes, cols, per, ids_ref, total_ref, list_ref, row_ref, pack_ref, upper_ref, lower_ref, labels_ref, mask_ref, *refs):
     stats, outs = refs[:cols], refs[cols : cols + nodes]
     extra_ref, sums, grads, store, sem = refs[cols + nodes :]
     one = bring(total_ref, pack_ref, store, sem)
@@ -343,7 +389,7 @@
     total = sum(ref[1:2] * jnp.exp(at - top) for ref, at in zip(stats, tops))
     chosen = sum(ref[2:3] for ref in stats)
     mask = mask_ref[...].astype(f32)
-    logits = logits_ref[...]
+    logits = jnp.concatenate([upper_ref[...], lower_ref[...]], axis=0)
     place = lax.broadcasted_iota(jnp.int32, logits.shape, 0)
     inside = place < per
     hit = place + col * per == labels_ref[...]
@@ -391,6 +437,23 @@
         base = (node ^ offset) * rows
         for part in range(rows):
             outs[offset][:, part * BLOCK : (part + 1) * BLOCK] = sums[base + part]
+
+
+def pair_body(*refs):
+    count = len(refs) // 3
+    for index in range(count):
+        refs[2 * count + index][...] = refs[index][...] + refs[count + index][...]
+
+
+def sum_body(cols, ids_ref, *refs):
+    parts, outs, held = refs[: -cols - 1], refs[-cols - 1 : -1], refs[-1]
+    col = ids_ref[1]
+    total = sum((ref[...] for ref in parts[1:]), parts[0][...])
+    width = total.shape[1] // cols
+    for group in range(cols):
+        held[group] = total[:, group * width : (group + 1) * width]
+    for offset in range(cols):
+        outs[offset][...] = held[col ^ offset]
 
 
 def grads_body(cols, per, ids_ref, mixed_ref, hidden_ref, slope_ref, weight_out_ref, extra_ref, *refs):
@@ -429,17 +492,18 @@
     feats, (units, classes) = weight_in_ref.shape[0], weight_out_ref.shape
     weight_in_ref[...] = value[:feats]
     weight_out_ref[...] = value[feats : feats + units, :classes]
-    bias_in_ref[...] = value[feats : feats + units, classes : classes + 1]
+    bias_in_ref[...] = as_row(value[feats : feats + units, classes : classes + 1])
     extra = value[feats + units : feats + units + 8]
     bias_out_ref[...] = jnp.concatenate([extra[group : group + 1, :per] for group in range(cols)], axis=1)
     loss_ref[...] = extra[cols : cols + 1, 0:1] / jnp.maximum(extra[cols : cols + 1, 1:2], 1.0)
 
 
 def logits_body(cols, per, ids_ref, *refs):
-    pieces, out_ref, held = refs[:cols], refs[cols], refs[-1]
+    uppers, lowers, out_ref, held = refs[:cols], refs[cols : 2 * cols], refs[-2], refs[-1]
     col = ids_ref[1]
     for offset in range(cols):
-        held[col ^ offset] = pieces[offset][...]
+        held[col ^ offset, :HALF] = uppers[offset][...]
+        held[col ^ offset, HALF:] = lowers[offset][...]
     out_ref[...] = jnp.concatenate([held[group, :per] for group in range(cols)], axis=0)
 
 
@@ -476,21 +540,19 @@
     shape = jax.ShapeDtypeStruct
     ids = jnp.stack([lax.axis_index("node"), lax.axis_index("col")]).astype(jnp.int32)
 
-    tail = jnp.concatenate(
-        [weight_out, bias_in[:, None], jnp.zeros((units // cols, units - classes - 1), f32)], axis=1
-    )
-    weights = jnp.concatenate([weight_in, tail], axis=0)
-    bias_groups = jnp.pad(bias_out.reshape(cols, per, 1), ((0, 0), (0, PAD - per), (0, 0)))
     labels = labels[None, :]
     train_mask = train_mask[None, :]
-    tile_count, ids, bias_groups, labels, train_mask, weights = lax.optimization_barrier(
-        (tile_count, ids, bias_groups, labels, train_mask, weights)
-    )
-
+    own = units // cols
+    height = feats + own + 8
+    weights = (
+        jnp.pad(weight_in, ((0, height - feats), (0, 0)))
+        + jnp.pad(weight_out, ((feats, 8), (0, units - classes)))
+        + jnp.pad(bias_in[None, :], ((feats + own, 7), (0, units - own)))
+    )
     even = gather_chips(features, nodes)
     weight_pieces = [weights] + [exchange(weights, "col", k) for k in range(1, cols)]
     packed, listed, placed, steps = pack(tiles, tile_column, tile_count, block_total)
-    steps, *even = lax.optimization_barrier((steps, *even))
+    steps, even, weight_pieces = lax.optimization_barrier((steps, even, weight_pieces))
     feature_pieces = gather_cores(even)
     sparse = (ids, steps, listed, placed, packed)
     sparse_specs = [SMEM] * 4 + [pl.BlockSpec(memory_space=pltpu.HBM)]
@@ -536,12 +598,12 @@
         moved=MIB,
     )
     scores = gather_cores(gather_chips(stacked, nodes))
-    logits_part, stats = call(
+    upper, lower, stats = call(
         functools.partial(mix_out_body, nodes, cols, per),
-        [shape((PAD, local), f32), shape((8, local), f32)],
-        [pltpu.VMEM((block_total, 2 * PAD, BLOCK), bf16), pltpu.VMEM((rows, 2 * PAD, 2 * BLOCK), f32), *held],
+        [shape((HALF, local), f32), shape((PAD - HALF, local), f32), shape((8, local), f32)],
+        [pltpu.VMEM((block_total, 2 * PAD, BLOCK), bf16), pltpu.VMEM((rows, 2 * PAD, 2 * BLOCK), f32), pltpu.VMEM((cols, PAD, 1), f32), *held],
         *sparse,
-        bias_groups,
+        bias_out[None, :],
         labels,
         *scores,
         specs=sparse_specs + [VMEM] * (2 + nodes),
@@ -559,37 +621,54 @@
             *held,
         ],
         *sparse,
-        logits_part,
+        upper,
+        lower,
         labels,
         train_mask,
         *stats_pieces,
-        specs=sparse_specs + [VMEM] * (3 + cols),
+        specs=sparse_specs + [VMEM] * (4 + cols),
         limit=44,
         flops=10**9,
         moved=16 * MIB,
     )
-    logit_pieces = [logits_part] + [exchange(logits_part, "col", k) for k in range(1, cols)]
+    uppers = [upper] + [exchange(upper, "col", k) for k in range(1, cols)]
+    spread_parts, uppers = lax.optimization_barrier((spread_parts, uppers))
+    paired = call(
+        pair_body,
+        [shape((PAD, local), f32)] * (nodes // 2),
+        [],
+        *spread_parts[::2],
+        *[exchange(part, "node", 1) for part in spread_parts[1::2]],
+        limit=8,
+        moved=2 * MIB,
+    )
+    paired, lower = lax.optimization_barrier((paired, lower))
+    chips = [exchange(paired[k], "node", 2 * k) for k in range(1, nodes // 2)]
+    lowers = [lower] + [exchange(lower, "col", k) for k in range(1, cols)]
+    spread_slices = call(
+        functools.partial(sum_body, cols),
+        [shape((PAD, slice_nodes), f32)] * cols,
+        [pltpu.VMEM((cols, PAD, slice_nodes), f32)],
+        ids,
+        paired[0],
+        *chips,
+        specs=[SMEM] + [VMEM] * (nodes // 2),
+        limit=8,
+        moved=MIB,
+    )
+    spread_slices, lowers = lax.optimization_barrier((spread_slices, lowers))
+    spread_pieces = [spread_slices[0]] + [exchange(spread_slices[k], "col", k) for k in range(1, cols)]
     (logits,) = call(
         functools.partial(logits_body, cols, per),
         [shape((classes, local), f32)],
         [pltpu.VMEM((cols, PAD, local), f32)],
         ids,
-        *logit_pieces,
-        specs=[SMEM] + [VMEM] * cols,
+        *uppers,
+        *lowers,
+        specs=[SMEM] + [VMEM] * (2 * cols),
+        limit=8,
         moved=2 * MIB,
     )
-
-    paired = [
-        spread_parts[k] + exchange(spread_parts[k + 1], "node", 1) for k in range(0, nodes, 2)
-    ]
-    spread = paired[0]
-    for index in range(1, nodes // 2):
-        spread = spread + exchange(paired[index], "node", 2 * index)
-    col = ids[1]
-    spread_slices = [
-        lax.dynamic_slice_in_dim(spread, (col ^ k) * slice_nodes, slice_nodes, axis=1) for k in range(cols)
-    ]
-    spread_pieces = [spread_slices[0]] + [exchange(spread_slices[k], "col", k) for k in range(1, cols)]
     logits, *spread_pieces = lax.optimization_barrier((logits, *spread_pieces))
 
     height = -(-(feats + units // cols + 8) // 16) * 16
@@ -620,7 +699,7 @@
         functools.partial(finish_body, cols, per),
         [
             shape((feats, units), f32),
-            shape((units // cols, 1), f32),
+            shape((1, units // cols), f32),
             shape((units // cols, classes), f32),
             shape((1, classes), f32),
             shape((1, 1), f32),
@@ -631,7 +710,14 @@
         other,
         specs=[SMEM, VMEM, VMEM],
     )
-    return (logits, mean_loss[0, 0], grad_in, grad_bias_in[:, 0], grad_out, grad_bias_out[0])
+    return (
+        logits,
+        mean_loss.reshape(()),
+        grad_in,
+        grad_bias_in.reshape(-1),
+        grad_out,
+        grad_bias_out.reshape(-1),
+    )
 
 
 def solution(mesh):

time: 159 us -> 138 us (0.87)
  waiting for transfers between devices: 48.4 us -> 38.7 us
  starting transfers between devices: 58.8 us -> 51.1 us
  between operations: 3.52 us -> 0.93 us
  local copies, waits for them, and re-layouts: 3.61 us -> 1.37 us
  Pallas kernels: 44.6 us -> 46.7 us
    ppermute x47 -> x50, waiting for transfers between devices: 48.4 us -> 38.7 us  [exchange(): return lax.ppermute(value, axis, [(i, i ^ offset) for i in range(total)])]
    ppermute x47 -> x50, starting transfers between devices: 58.8 us -> 51.1 us  [exchange(): return lax.ppermute(value, axis, [(i, i ^ offset) for i in range(total)])]
    pallas_call x9 -> x11, Pallas kernels: 44.6 us -> 46.7 us  [call(): pl.pallas_call(body, out_shape=outs, in_specs=specs or [VMEM] * len(args)...]
  transfers between devices with their start and end apart: 47 -> 50, of which waited for: 22 -> 29; matrix products, arithmetic and copies ran while one was open for 2% -> 0% of each run, Pallas kernels for 16% -> 18%
where the time goes in v2:
time: 138 us; the launch traced here: 140 us
  starting transfers between devices  51.1 us (37%)
  Pallas kernels  46.7 us (34%)
  waiting for transfers between devices  38.7 us (28%)
    ppermute x50, starting transfers between devices, exchange(): return lax.ppermute(value, axis, [(i, i ^ offset) for i in range(total)])  51.1 us
    pallas_call x11, Pallas kernels, call(): pl.pallas_call(body, out_shape=outs, in_specs=specs or [VMEM] * len(args)...  46.7 us
    ppermute x50, waiting for transfers between devices, exchange(): return lax.ppermute(value, axis, [(i, i ^ offset) for i in range(total)])  38.7 us
  transfers between devices with their start and end apart: 50, of which 29 were waited for; matrix products, arithmetic and copies ran while one was open for 0% of the time, Pallas kernels for 18%

profile of v2, /device:TPU:0, one launch (start us, length us, event | category | flops | bytes accessed | tf_op | source)
XLA Modules:
  0.0 139.9 jit_solution(4978591142545768273)
XLA Ops:
  0.7 0.9 pad_add_fusion.refs_4_
  1.6 5.1 %collective-permute-start.5 = (f32[104,256]{1,0:T(8,128)S(1)}, f32[104,256]{1,0:T(8,128)S(1)}, u32[]{:S(2)}, u32[]{:S(2)}) collective-permute-start(f32[104,256]{1,0:T(8,128)S(1)} %pad_add_fusion.refs_4_), channel_id=1, source_target_pairs={{0,3},{1,2},{2,1},{3,0},{4,7},{5,6},{6,5},{7,4},{8,11},{9,10},{10,... | collective-permute-start | bytes 319496 | tf_op jit(solution)/shard_map/ppermute | solution.py:30
  6.7 1.5 %collective-permute-start.1 = (f32[32,1024]{1,0:T(8,128)}, f32[32,1024]{1,0:T(8,128)S(1)}, u32[]{:S(2)}, u32[]{:S(2)}) collective-permute-start(f32[32,1024]{1,0:T(8,128)} %refs_0_), channel_id=1, source_target_pairs={{0,16},{4,20},{8,24},{12,28},{16,0},{20,4},{24,8},{28,12},{1,17},{... | collective-permute-start | bytes 393224 | tf_op jit(solution)/shard_map/ppermute | solution.py:30
  8.2 1.5 %collective-permute-start = (f32[32,1024]{1,0:T(8,128)}, f32[32,1024]{1,0:T(8,128)S(1)}, u32[]{:S(2)}, u32[]{:S(2)}) collective-permute-start(f32[32,1024]{1,0:T(8,128)} %refs_0_), channel_id=1, source_target_pairs={{0,8},{4,12},{8,0},{12,4},{16,24},{20,28},{24,16},{28,20},{1,9},{5... | collective-permute-start | bytes 393224 | tf_op jit(solution)/shard_map/ppermute | solution.py:30
  9.7 0.5 collective-permute-start.2
  10.2 1.5 %collective-permute-start.3 = (f32[104,256]{1,0:T(8,128)S(1)}, f32[104,256]{1,0:T(8,128)S(1)}, u32[]{:S(2)}, u32[]{:S(2)}) collective-permute-start(f32[104,256]{1,0:T(8,128)S(1)} %pad_add_fusion.refs_4_), channel_id=1, source_target_pairs={{0,1},{1,0},{2,3},{3,2},{4,5},{5,4},{6,7},{7,6},{8,9},{9,8},{10,11... | collective-permute-start | bytes 319496 | tf_op jit(solution)/shard_map/ppermute | solution.py:30
  11.6 0.7 copy-done.2
  12.3 0.7 copy-done.5
  13.0 16.0 %shard_map.145 = (bf16[128,256,512]{2,1,0:T(8,128)(2,1)}, s32[512]{0:T(512)S(1)}, s32[128]{0:T(128)S(1)}, s32[1]{0:T(128)}) custom-call(s32[8]{0:T(128)S(1)} %copy-done.5, s32[8,64]{1,0:T(8,128)S(1)} %copy-done.2, f32[8,64,128,128]{3,2,1,0:T(8,128)} %tiles_ref.1), custom_call_target="tpu_custom_call" | custom-call | flops 100000000 | bytes 41943040 | tf_op jit(solution)/shard_map/pallas_call | solution.py:50
  29.2 0.5 collective-permute-start.7
  29.8 0.4 collective-permute-start.9
  30.7 0.3 collective-permute-done.8.refs_5_
  31.2 8.6 %shard_map.146 = (f32[32,256]{1,0:T(8,128)S(1)}, f32[32,256]{1,0:T(8,128)S(1)}, f32[32,256]{1,0:T(8,128)S(1)}, f32[32,256]{1,0:T(8,128)S(1)}) custom-call(s32[2]{0:T(128)S(1)} %pad_add_fusion.1.ids_ref, s32[1]{0:T(128)} %get-tuple-element.89.total_ref, s32[512]{0:T(512)S(1)} %get-tuple-element.90.list_ref, s32[128]{0:T(128)S(1)} %get-tuple-element.91.row_ref, ...), custom_call_target="tpu_custom_call" | custom-call | flops 1000000000 | bytes 16777216 | tf_op jit(solution)/shard_map/pallas_call | solution.py:50
  39.9 0.6 collective-permute-start.10
  40.5 3.8 %collective-permute-start.11 = (f32[32,256]{1,0:T(8,128)S(1)}, f32[32,256]{1,0:T(8,128)S(1)}, u32[]{:S(2)}, u32[]{:S(2)}) collective-permute-start(f32[32,256]{1,0:T(8,128)S(1)} %get-tuple-element.99), channel_id=1, source_target_pairs={{0,2},{1,3},{2,0},{3,1},{4,6},{5,7},{6,4},{7,5},{8,10},{9,11},{10,... | collective-permute-start | bytes 98312 | tf_op jit(solution)/shard_map/ppermute | solution.py:30
  44.3 2.2 %collective-permute-done.11.refs_2_ = f32[32,256]{1,0:T(8,128)S(1)} collective-permute-done((f32[32,256]{1,0:T(8,128)S(1)}, f32[32,256]{1,0:T(8,128)S(1)}, u32[]{:S(2)}, u32[]{:S(2)}) %collective-permute-start.11) | collective-permute-done | bytes 32800 | tf_op jit(solution)/shard_map/ppermute | solution.py:30
  46.6 3.5 %collective-permute-done.12.refs_3_ = f32[32,256]{1,0:T(8,128)S(1)} collective-permute-done((f32[32,256]{1,0:T(8,128)S(1)}, f32[32,256]{1,0:T(8,128)S(1)}, u32[]{:S(2)}, u32[]{:S(2)}) %collective-permute-start.12) | collective-permute-done | bytes 32800 | tf_op jit(solution)/shard_map/ppermute | solution.py:30
  50.0 1.3 shard_map.147
  51.5 0.9 collective-permute-start.14
  52.4 3.5 %collective-permute-start.15 = (f32[48,256]{1,0:T(8,128)S(1)}, f32[48,256]{1,0:T(8,128)S(1)}, u32[]{:S(2)}, u32[]{:S(2)}) collective-permute-start(f32[48,256]{1,0:T(8,128)S(1)} %get-tuple-element.108), channel_id=1, source_target_pairs={{0,3},{1,2},{2,1},{3,0},{4,7},{5,6},{6,5},{7,4},{8,11},{9,10},{10,... | collective-permute-start | bytes 147464 | tf_op jit(solution)/shard_map/ppermute | solution.py:30
  55.8 0.7 collective-permute-done.14.refs_2_
  56.5 1.9 %collective-permute-done.15.refs_3_ = f32[48,256]{1,0:T(8,128)S(1)} collective-permute-done((f32[48,256]{1,0:T(8,128)S(1)}, f32[48,256]{1,0:T(8,128)S(1)}, u32[]{:S(2)}, u32[]{:S(2)}) %collective-permute-start.15) | collective-permute-done | bytes 49184 | tf_op jit(solution)/shard_map/ppermute | solution.py:30
  58.6 3.4 %collective-permute-start.17 = (f32[4,48,256]{2,1,0:T(8,128)S(1)}, f32[4,48,256]{2,1,0:T(8,128)S(1)}, u32[]{:S(2)}, u32[]{:S(2)}) collective-permute-start(f32[4,48,256]{2,1,0:T(8,128)S(1)} %shard_map.148.refs_0_), channel_id=1, source_target_pairs={{0,8},{4,12},{8,0},{12,4},{16,24},{20,28},{24,16},{28,20},{1,9},{5... | collective-permute-start | bytes 589832 | tf_op jit(solution)/shard_map/ppermute | solution.py:30
  62.0 3.2 %collective-permute-done.21.refs_6_ = f32[4,48,256]{2,1,0:T(8,128)S(1)} collective-permute-done((f32[4,48,256]{2,1,0:T(8,128)S(1)}, f32[4,48,256]{2,1,0:T(8,128)S(1)}, u32[]{:S(2)}, u32[]{:S(2)}) %collective-permute-start.21) | collective-permute-done | bytes 196640 | tf_op jit(solution)/shard_map/ppermute | solution.py:30
  65.2 1.2 collective-permute-done.19.refs_4_
  66.4 0.5 collective-permute-start.18
  66.9 0.9 collective-permute-done.20.refs_5_
  67.8 0.3 collective-permute-done.18.refs_3_
  68.1 8.9 %shard_map.149 = (f32[24,1024]{1,0:T(8,128)S(1)}, f32[24,1024]{1,0:T(8,128)S(1)}, f32[8,1024]{1,0:T(8,128)S(1)}) custom-call(s32[2]{0:T(128)S(1)} %pad_add_fusion.1.ids_ref, s32[1]{0:T(128)} %get-tuple-element.89.total_ref, s32[512]{0:T(512)S(1)} %get-tuple-element.90.list_ref, s32[128]{0:T(128)S(1)} %get-tuple-element.91.row_ref, ...), custom_call_target="tpu_custom_call" | custom-call | flops 1000000000 | bytes 16777216 | tf_op jit(solution)/shard_map/pallas_call | solution.py:50
  77.0 3.4 %collective-permute-start.25 = (f32[8,1024]{1,0:T(8,128)S(1)}, f32[8,1024]{1,0:T(8,128)S(1)}, u32[]{:S(2)}, u32[]{:S(2)}) collective-permute-start(f32[8,1024]{1,0:T(8,128)S(1)} %get-tuple-element.111.refs_0_), channel_id=1, source_target_pairs={{0,3},{1,2},{2,1},{3,0},{4,7},{5,6},{6,5},{7,4},{8,11},{9,10},{10,... | collective-permute-start | bytes 98312 | tf_op jit(solution)/shard_map/ppermute | solution.py:30
  80.4 1.1 collective-permute-start.23
  81.5 3.3 %collective-permute-start.28 = (f32[24,1024]{1,0:T(8,128)S(1)}, f32[24,1024]{1,0:T(8,128)S(1)}, u32[]{:S(2)}, u32[]{:S(2)}) collective-permute-start(f32[24,1024]{1,0:T(8,128)S(1)} %get-tuple-element.120.upper_ref.refs_0_), channel_id=1, source_target_pairs={{0,3},{1,2},{2,1},{3,0},{4,7},{5,6},{6,5},{7,4},{8,11},{9,10},{10,... | collective-permute-start | bytes 294920 | tf_op jit(solution)/shard_map/ppermute | solution.py:30
  84.8 1.1 collective-permute-start.26
  85.9 1.5 %collective-permute-done.24.refs_2_ = f32[8,1024]{1,0:T(8,128)S(1)} collective-permute-done((f32[8,1024]{1,0:T(8,128)S(1)}, f32[8,1024]{1,0:T(8,128)S(1)}, u32[]{:S(2)}, u32[]{:S(2)}) %collective-permute-start.24) | collective-permute-done | bytes 32800 | tf_op jit(solution)/shard_map/ppermute | solution.py:30
  87.4 7.0 %shard_map.150 = (f32[48,1024]{1,0:T(8,128)S(1)}, f32[48,1024]{1,0:T(8,128)S(1)}, f32[48,1024]{1,0:T(8,128)S(1)}, f32[48,1024]{1,0:T(8,128)S(1)}, f32[48,1024]{1...) custom-call(s32[2]{0:T(128)S(1)} %pad_add_fusion.1.ids_ref, ...), custom_call_target="tpu_custom_call" | custom-call | flops 1000000000 | bytes 16777216 | tf_op jit(solution)/shard_map/pallas_call | solution.py:50
  94.5 0.5 collective-permute-start.30
  95.1 0.4 collective-permute-start.32
  95.5 0.4 collective-permute-done.29.refs_4_
  95.9 0.3 collective-permute-done.30.refs_5_
  96.5 0.3 collective-permute-done.32.refs_7_
  97.0 3.4 %collective-permute-start.35 = (f32[48,1024]{1,0:T(8,128)S(1)}, f32[48,1024]{1,0:T(8,128)S(1)}, u32[]{:S(2)}, u32[]{:S(2)}) collective-permute-start(f32[48,1024]{1,0:T(8,128)S(1)} %get-tuple-element.139), channel_id=1, source_target_pairs={{0,24},{4,28},{8,16},{12,20},{16,8},{20,12},{24,0},{28,4},{1,25},{... | collective-permute-start | bytes 589832 | tf_op jit(solution)/shard_map/ppermute | solution.py:30
  100.4 1.8 %collective-permute-start.38 = (f32[24,1024]{1,0:T(8,128)S(1)}, f32[24,1024]{1,0:T(8,128)S(1)}, u32[]{:S(2)}, u32[]{:S(2)}) collective-permute-start(f32[24,1024]{1,0:T(8,128)S(1)} %get-tuple-element.145.lower_ref.refs_4_), channel_id=1, source_target_pairs={{0,3},{1,2},{2,1},{3,0},{4,7},{5,6},{6,5},{7,4},{8,11},{9,10},{10,... | collective-permute-start | bytes 294920 | tf_op jit(solution)/shard_map/ppermute | solution.py:30
  102.2 2.5 %collective-permute-done.33.refs_1_ = f32[48,1024]{1,0:T(8,128)S(1)} collective-permute-done((f32[48,1024]{1,0:T(8,128)S(1)}, f32[48,1024]{1,0:T(8,128)S(1)}, u32[]{:S(2)}, u32[]{:S(2)}) %collective-permute-start.33) | collective-permute-done | bytes 196640 | tf_op jit(solution)/shard_map/ppermute | solution.py:30
  104.8 3.4 %collective-permute-done.34.refs_2_ = f32[48,1024]{1,0:T(8,128)S(1)} collective-permute-done((f32[48,1024]{1,0:T(8,128)S(1)}, f32[48,1024]{1,0:T(8,128)S(1)}, u32[]{:S(2)}, u32[]{:S(2)}) %collective-permute-start.34) | collective-permute-done | bytes 196640 | tf_op jit(solution)/shard_map/ppermute | solution.py:30
  108.3 0.6 shard_map.152
  108.9 1.8 %collective-permute-done.37.refs_6_ = f32[24,1024]{1,0:T(8,128)S(1)} collective-permute-done((f32[24,1024]{1,0:T(8,128)S(1)}, f32[24,1024]{1,0:T(8,128)S(1)}, u32[]{:S(2)}, u32[]{:S(2)}) %collective-permute-start.37) | collective-permute-done | bytes 98336 | tf_op jit(solution)/shard_map/ppermute | solution.py:30
  110.7 0.5 collective-permute-done.36.refs_5_
  111.1 2.4 %collective-permute-start.40 = (f32[48,256]{1,0:T(8,128)S(1)}, f32[48,256]{1,0:T(8,128)S(1)}, u32[]{:S(2)}, u32[]{:S(2)}) collective-permute-start(f32[48,256]{1,0:T(8,128)S(1)} %get-tuple-element.151), channel_id=1, source_target_pairs={{0,2},{1,3},{2,0},{3,1},{4,6},{5,7},{6,4},{7,5},{8,10},{9,11},{10,... | collective-permute-start | bytes 147464 | tf_op jit(solution)/shard_map/ppermute | solution.py:30
  113.5 2.0 %collective-permute-start.41 = (f32[48,256]{1,0:T(8,128)S(1)}, f32[48,256]{1,0:T(8,128)S(1)}, u32[]{:S(2)}, u32[]{:S(2)}) collective-permute-start(f32[48,256]{1,0:T(8,128)S(1)} %get-tuple-element.152), channel_id=1, source_target_pairs={{0,3},{1,2},{2,1},{3,0},{4,7},{5,6},{6,5},{7,4},{8,11},{9,10},{10,... | collective-permute-start | bytes 147464 | tf_op jit(solution)/shard_map/ppermute | solution.py:30
  115.5 1.5 %shard_map.153 = f32[172,1024]{1,0:T(8,128)} custom-call(s32[2]{0:T(128)S(1)} %pad_add_fusion.1.ids_ref, f32[24,1024]{1,0:T(8,128)S(1)} %get-tuple-element.120.upper_ref.refs_0_, f32[24,1024]{1,0:T(8,128)S(1)} %collective-permute-done.26.refs_1_, f32[24,1024]{1,0:T(8,128)S(1)} %collective-permute-done.27.refs_2_, ...), custom_call_target="tpu_custom_call" | custom-call | bytes 2097152 | tf_op jit(solution)/shard_map/pallas_call | solution.py:50
  117.0 2.4 %collective-permute-done.41.refs_3_ = f32[48,256]{1,0:T(8,128)S(1)} collective-permute-done((f32[48,256]{1,0:T(8,128)S(1)}, f32[48,256]{1,0:T(8,128)S(1)}, u32[]{:S(2)}, u32[]{:S(2)}) %collective-permute-start.41) | collective-permute-done | bytes 49184 | tf_op jit(solution)/shard_map/ppermute | solution.py:30
  119.4 1.2 shard_map.154
  120.8 1.5 %collective-permute-done.42 = f32[4,56,256]{2,1,0:T(8,128)S(1)} collective-permute-done((f32[4,56,256]{2,1,0:T(8,128)S(1)}, f32[4,56,256]{2,1,0:T(8,128)S(1)}, u32[]{:S(2)}, u32[]{:S(2)}) %collective-permute-start.42) | collective-permute-done | bytes 229408 | tf_op jit(solution)/shard_map/ppermute | solution.py:30
  122.4 2.0 %collective-permute-start.45 = (f32[56,256]{1,0:T(8,128)S(1)}, f32[56,256]{1,0:T(8,128)S(1)}, u32[]{:S(2)}, u32[]{:S(2)}) collective-permute-start(f32[56,256]{1,0:T(8,128)S(1)} %get-tuple-element.171), channel_id=1, source_target_pairs={{0,3},{1,2},{2,1},{3,0},{4,7},{5,6},{6,5},{7,4},{8,11},{9,10},{10,... | collective-permute-start | bytes 172040 | tf_op jit(solution)/shard_map/ppermute | solution.py:30
  124.4 1.4 %collective-permute-start.44 = (f32[56,256]{1,0:T(8,128)S(1)}, f32[56,256]{1,0:T(8,128)S(1)}, u32[]{:S(2)}, u32[]{:S(2)}) collective-permute-start(f32[56,256]{1,0:T(8,128)S(1)} %get-tuple-element.172), channel_id=1, source_target_pairs={{0,2},{1,3},{2,0},{3,1},{4,6},{5,7},{6,4},{7,5},{8,10},{9,11},{10,... | collective-permute-start | bytes 172040 | tf_op jit(solution)/shard_map/ppermute | solution.py:30
  125.9 0.7 collective-permute-done.43
  126.5 2.3 %collective-permute-done.45 = f32[56,256]{1,0:T(8,128)S(1)} collective-permute-done((f32[56,256]{1,0:T(8,128)S(1)}, f32[56,256]{1,0:T(8,128)S(1)}, u32[]{:S(2)}, u32[]{:S(2)}) %collective-permute-start.45) | collective-permute-done | bytes 57376 | tf_op jit(solution)/shard_map/ppermute | solution.py:30
  128.9 2.4 %collective-permute-done.44 = f32[56,256]{1,0:T(8,128)S(1)} collective-permute-done((f32[56,256]{1,0:T(8,128)S(1)}, f32[56,256]{1,0:T(8,128)S(1)}, u32[]{:S(2)}, u32[]{:S(2)}) %collective-permute-start.44) | collective-permute-done | bytes 57376 | tf_op jit(solution)/shard_map/ppermute | solution.py:30
  131.5 1.6 %collective-permute-start.47 = (f32[56,256]{1,0:T(8,128)S(1)}, f32[56,256]{1,0:T(8,128)S(1)}, u32[]{:S(2)}, u32[]{:S(2)}) collective-permute-start(f32[56,256]{1,0:T(8,128)S(1)} %fusion.2), channel_id=1, source_target_pairs={{0,16},{4,20},{8,24},{12,28},{16,0},{20,4},{24,8},{28,12},{1,17},{... | collective-permute-start | bytes 172040 | tf_op jit(solution)/shard_map/ppermute | solution.py:30
  133.1 1.8 %collective-permute-start.46 = (f32[56,256]{1,0:T(8,128)S(1)}, f32[56,256]{1,0:T(8,128)S(1)}, u32[]{:S(2)}, u32[]{:S(2)}) collective-permute-start(f32[56,256]{1,0:T(8,128)S(1)} %fusion.2), channel_id=1, source_target_pairs={{0,8},{4,12},{8,0},{12,4},{16,24},{20,28},{24,16},{28,20},{1,9},{5... | collective-permute-start | bytes 172040 | tf_op jit(solution)/shard_map/ppermute | solution.py:30
  134.8 1.6 %collective-permute-done.48 = f32[56,256]{1,0:T(8,128)S(1)} collective-permute-done((f32[56,256]{1,0:T(8,128)S(1)}, f32[56,256]{1,0:T(8,128)S(1)}, u32[]{:S(2)}, u32[]{:S(2)}) %collective-permute-start.48) | collective-permute-done | bytes 57376 | tf_op jit(solution)/shard_map/ppermute | solution.py:30
  136.4 0.8 collective-permute-done.46
  137.4 1.2 collective-permute-done.49.other_ref
  138.6 1.3 shard_map.155
  (65 shorter events, 2.5 us)
Async XLA Ops:
  0.6 28.5 %copy-start = (f32[32,1024]{1,0:T(8,128)S(1)}, f32[32,1024]{1,0:T(8,128)}, u32[]{:S(2)}) copy-start(f32[32,1024]{1,0:T(8,128)} %refs_0_) | copy-start | bytes 393220
  0.6 67.4 %copy-start.4 = (f32[172]{0:T(256)S(1)}, f32[172]{0:T(256)}, u32[]{:S(2)}) copy-start(f32[172]{0:T(256)} %param.19) | copy-start | bytes 2068
  1.6 66.5 %copy-start.1 = (s32[1024]{0:T(1024)S(1)}, s32[1024]{0:T(1024)}, u32[]{:S(2)}) copy-start(s32[1024]{0:T(1024)} %param.14) | copy-start | bytes 12292
  1.6 8.6 %collective-permute-start.5 = (f32[104,256]{1,0:T(8,128)S(1)}, f32[104,256]{1,0:T(8,128)S(1)}, u32[]{:S(2)}, u32[]{:S(2)}) collective-permute-start(f32[104,256]{1,0:T(8,128)S(1)} %pad_add_fusion.refs_4_), channel_id=1, source_target_pairs={{0,3},{1,2},{2,1},{3,0},{4,7},{5,6},{6,5},{7,4},{8,11},{9,10},{10,... | collective-permute-start | bytes 319496 | tf_op jit(solution)/shard_map/ppermute | solution.py:30
  6.7 22.4 %collective-permute-start.1 = (f32[32,1024]{1,0:T(8,128)}, f32[32,1024]{1,0:T(8,128)S(1)}, u32[]{:S(2)}, u32[]{:S(2)}) collective-permute-start(f32[32,1024]{1,0:T(8,128)} %refs_0_), channel_id=1, source_target_pairs={{0,16},{4,20},{8,24},{12,28},{16,0},{20,4},{24,8},{28,12},{1,17},{... | collective-permute-start | bytes 393224 | tf_op jit(solution)/shard_map/ppermute | solution.py:30
  8.2 20.9 %collective-permute-start = (f32[32,1024]{1,0:T(8,128)}, f32[32,1024]{1,0:T(8,128)S(1)}, u32[]{:S(2)}, u32[]{:S(2)}) collective-permute-start(f32[32,1024]{1,0:T(8,128)} %refs_0_), channel_id=1, source_target_pairs={{0,8},{4,12},{8,0},{12,4},{16,24},{20,28},{24,16},{28,20},{1,9},{5... | collective-permute-start | bytes 393224 | tf_op jit(solution)/shard_map/ppermute | solution.py:30
  9.7 19.4 %collective-permute-start.2 = (f32[32,1024]{1,0:T(8,128)}, f32[32,1024]{1,0:T(8,128)S(1)}, u32[]{:S(2)}, u32[]{:S(2)}) collective-permute-start(f32[32,1024]{1,0:T(8,128)} %refs_0_), channel_id=1, source_target_pairs={{0,24},{4,28},{8,16},{12,20},{16,8},{20,12},{24,0},{28,4},{1,25},{... | collective-permute-start | bytes 393224 | tf_op jit(solution)/shard_map/ppermute | solution.py:30
  10.2 18.9 %collective-permute-start.4 = (f32[104,256]{1,0:T(8,128)S(1)}, f32[104,256]{1,0:T(8,128)S(1)}, u32[]{:S(2)}, u32[]{:S(2)}) collective-permute-start(f32[104,256]{1,0:T(8,128)S(1)} %pad_add_fusion.refs_4_), channel_id=1, source_target_pairs={{0,2},{1,3},{2,0},{3,1},{4,6},{5,7},{6,4},{7,5},{8,10},{9,11},{10,... | collective-permute-start | bytes 319496 | tf_op jit(solution)/shard_map/ppermute | solution.py:30
  10.2 18.9 %collective-permute-start.3 = (f32[104,256]{1,0:T(8,128)S(1)}, f32[104,256]{1,0:T(8,128)S(1)}, u32[]{:S(2)}, u32[]{:S(2)}) collective-permute-start(f32[104,256]{1,0:T(8,128)S(1)} %pad_add_fusion.refs_4_), channel_id=1, source_target_pairs={{0,1},{1,0},{2,3},{3,2},{4,5},{5,4},{6,7},{7,6},{8,9},{9,8},{10,11... | collective-permute-start | bytes 319496 | tf_op jit(solution)/shard_map/ppermute | solution.py:30
  11.6 0.7 copy-start.2
  12.3 0.7 copy-start.5
  29.1 1.4 %collective-permute-start.6 = (f32[32,1024]{1,0:T(8,128)S(1)}, f32[32,1024]{1,0:T(8,128)S(1)}, u32[]{:S(2)}, u32[]{:S(2)}) collective-permute-start(f32[32,1024]{1,0:T(8,128)S(1)} %copy-done), channel_id=1, source_target_pairs={{0,4},{4,0},{8,12},{12,8},{16,20},{20,16},{24,28},{28,24},{1,5},{5... | collective-permute-start | bytes 393224 | tf_op jit(solution)/shard_map/ppermute | solution.py:30
  29.2 1.5 %collective-permute-start.7 = (f32[32,1024]{1,0:T(8,128)S(1)}, f32[32,1024]{1,0:T(8,128)S(1)}, u32[]{:S(2)}, u32[]{:S(2)}) collective-permute-start(f32[32,1024]{1,0:T(8,128)S(1)} %collective-permute-done.refs_2_), channel_id=1, source_target_pairs={{0,4},{4,0},{8,12},{12,8},{16,20},{20,16},{24,28},{28,24},{1,5},{5... | collective-permute-start | bytes 393224 | tf_op jit(solution)/shard_map/ppermute | solution.py:30
  29.7 1.3 collective-permute-start.8
  29.8 1.5 %collective-permute-start.9 = (f32[32,1024]{1,0:T(8,128)S(1)}, f32[32,1024]{1,0:T(8,128)S(1)}, u32[]{:S(2)}, u32[]{:S(2)}) collective-permute-start(f32[32,1024]{1,0:T(8,128)S(1)} %collective-permute-done.2.refs_6_), channel_id=1, source_target_pairs={{0,4},{4,0},{8,12},{12,8},{16,20},{20,16},{24,28},{28,24},{1,5},{5... | collective-permute-start | bytes 393224 | tf_op jit(solution)/shard_map/ppermute | solution.py:30
  31.2 56.2 %copy-start.3 = (s32[1024]{0:T(1024)S(1)}, s32[1024]{0:T(1024)}, u32[]{:S(2)}) copy-start(s32[1024]{0:T(1024)} %param.15) | copy-start | bytes 12292
  39.9 4.5 %collective-permute-start.10 = (f32[32,256]{1,0:T(8,128)S(1)}, f32[32,256]{1,0:T(8,128)S(1)}, u32[]{:S(2)}, u32[]{:S(2)}) collective-permute-start(f32[32,256]{1,0:T(8,128)S(1)} %get-tuple-element.98), channel_id=1, source_target_pairs={{0,1},{1,0},{2,3},{3,2},{4,5},{5,4},{6,7},{7,6},{8,9},{9,8},{10,11... | collective-permute-start | bytes 98312 | tf_op jit(solution)/shard_map/ppermute | solution.py:30
  40.5 6.1 %collective-permute-start.11 = (f32[32,256]{1,0:T(8,128)S(1)}, f32[32,256]{1,0:T(8,128)S(1)}, u32[]{:S(2)}, u32[]{:S(2)}) collective-permute-start(f32[32,256]{1,0:T(8,128)S(1)} %get-tuple-element.99), channel_id=1, source_target_pairs={{0,2},{1,3},{2,0},{3,1},{4,6},{5,7},{6,4},{7,5},{8,10},{9,11},{10,... | collective-permute-start | bytes 98312 | tf_op jit(solution)/shard_map/ppermute | solution.py:30
  44.3 5.7 %collective-permute-start.12 = (f32[32,256]{1,0:T(8,128)S(1)}, f32[32,256]{1,0:T(8,128)S(1)}, u32[]{:S(2)}, u32[]{:S(2)}) collective-permute-start(f32[32,256]{1,0:T(8,128)S(1)} %get-tuple-element.100), channel_id=1, source_target_pairs={{0,3},{1,2},{2,1},{3,0},{4,7},{5,6},{6,5},{7,4},{8,11},{9,10},{10,... | collective-permute-start | bytes 98312 | tf_op jit(solution)/shard_map/ppermute | solution.py:30
  51.4 4.5 %collective-permute-start.13 = (f32[48,256]{1,0:T(8,128)S(1)}, f32[48,256]{1,0:T(8,128)S(1)}, u32[]{:S(2)}, u32[]{:S(2)}) collective-permute-start(f32[48,256]{1,0:T(8,128)S(1)} %get-tuple-element.106), channel_id=1, source_target_pairs={{0,1},{1,0},{2,3},{3,2},{4,5},{5,4},{6,7},{7,6},{8,9},{9,8},{10,11... | collective-permute-start | bytes 147464 | tf_op jit(solution)/shard_map/ppermute | solution.py:30
  51.5 5.1 %collective-permute-start.14 = (f32[48,256]{1,0:T(8,128)S(1)}, f32[48,256]{1,0:T(8,128)S(1)}, u32[]{:S(2)}, u32[]{:S(2)}) collective-permute-start(f32[48,256]{1,0:T(8,128)S(1)} %get-tuple-element.107), channel_id=1, source_target_pairs={{0,2},{1,3},{2,0},{3,1},{4,6},{5,7},{6,4},{7,5},{8,10},{9,11},{10,... | collective-permute-start | bytes 147464 | tf_op jit(solution)/shard_map/ppermute | solution.py:30
  52.4 6.1 %collective-permute-start.15 = (f32[48,256]{1,0:T(8,128)S(1)}, f32[48,256]{1,0:T(8,128)S(1)}, u32[]{:S(2)}, u32[]{:S(2)}) collective-permute-start(f32[48,256]{1,0:T(8,128)S(1)} %get-tuple-element.108), channel_id=1, source_target_pairs={{0,3},{1,2},{2,1},{3,0},{4,7},{5,6},{6,5},{7,4},{8,11},{9,10},{10,... | collective-permute-start | bytes 147464 | tf_op jit(solution)/shard_map/ppermute | solution.py:30
  58.4 6.7 %collective-permute-start.21 = (f32[4,48,256]{2,1,0:T(8,128)S(1)}, f32[4,48,256]{2,1,0:T(8,128)S(1)}, u32[]{:S(2)}, u32[]{:S(2)}) collective-permute-start(f32[4,48,256]{2,1,0:T(8,128)S(1)} %shard_map.148.refs_0_), channel_id=1, source_target_pairs={{0,24},{4,28},{8,16},{12,20},{16,8},{20,12},{24,0},{28,4},{1,25},{... | collective-permute-start | bytes 589832 | tf_op jit(solution)/shard_map/ppermute | solution.py:30
  58.5 7.8 %collective-permute-start.19 = (f32[4,48,256]{2,1,0:T(8,128)S(1)}, f32[4,48,256]{2,1,0:T(8,128)S(1)}, u32[]{:S(2)}, u32[]{:S(2)}) collective-permute-start(f32[4,48,256]{2,1,0:T(8,128)S(1)} %shard_map.148.refs_0_), channel_id=1, source_target_pairs={{0,16},{4,20},{8,24},{12,28},{16,0},{20,4},{24,8},{28,12},{1,17},{... | collective-permute-start | bytes 589832 | tf_op jit(solution)/shard_map/ppermute | solution.py:30
  58.6 7.8 %collective-permute-start.17 = (f32[4,48,256]{2,1,0:T(8,128)S(1)}, f32[4,48,256]{2,1,0:T(8,128)S(1)}, u32[]{:S(2)}, u32[]{:S(2)}) collective-permute-start(f32[4,48,256]{2,1,0:T(8,128)S(1)} %shard_map.148.refs_0_), channel_id=1, source_target_pairs={{0,8},{4,12},{8,0},{12,4},{16,24},{20,28},{24,16},{28,20},{1,9},{5... | collective-permute-start | bytes 589832 | tf_op jit(solution)/shard_map/ppermute | solution.py:30
  62.0 4.9 %collective-permute-start.16 = (f32[4,48,256]{2,1,0:T(8,128)S(1)}, f32[4,48,256]{2,1,0:T(8,128)S(1)}, u32[]{:S(2)}, u32[]{:S(2)}) collective-permute-start(f32[4,48,256]{2,1,0:T(8,128)S(1)} %shard_map.148.refs_0_), channel_id=1, source_target_pairs={{0,4},{4,0},{8,12},{12,8},{16,20},{20,16},{24,28},{28,24},{1,5},{5... | collective-permute-start | bytes 589832 | tf_op jit(solution)/shard_map/ppermute | solution.py:30
  65.2 1.7 %collective-permute-start.22 = (f32[4,48,256]{2,1,0:T(8,128)S(1)}, f32[4,48,256]{2,1,0:T(8,128)S(1)}, u32[]{:S(2)}, u32[]{:S(2)}) collective-permute-start(f32[4,48,256]{2,1,0:T(8,128)S(1)} %collective-permute-done.21.refs_6_), channel_id=1, source_target_pairs={{0,4},{4,0},{8,12},{12,8},{16,20},{20,16},{24,28},{28,24},{1,5},{5... | collective-permute-start | bytes 589832 | tf_op jit(solution)/shard_map/ppermute | solution.py:30
  66.4 1.4 %collective-permute-start.20 = (f32[4,48,256]{2,1,0:T(8,128)S(1)}, f32[4,48,256]{2,1,0:T(8,128)S(1)}, u32[]{:S(2)}, u32[]{:S(2)}) collective-permute-start(f32[4,48,256]{2,1,0:T(8,128)S(1)} %collective-permute-done.19.refs_4_), channel_id=1, source_target_pairs={{0,4},{4,0},{8,12},{12,8},{16,20},{20,16},{24,28},{28,24},{1,5},{5... | collective-permute-start | bytes 589832 | tf_op jit(solution)/shard_map/ppermute | solution.py:30
  66.4 1.7 %collective-permute-start.18 = (f32[4,48,256]{2,1,0:T(8,128)S(1)}, f32[4,48,256]{2,1,0:T(8,128)S(1)}, u32[]{:S(2)}, u32[]{:S(2)}) collective-permute-start(f32[4,48,256]{2,1,0:T(8,128)S(1)} %collective-permute-done.17.refs_2_), channel_id=1, source_target_pairs={{0,4},{4,0},{8,12},{12,8},{16,20},{20,16},{24,28},{28,24},{1,5},{5... | collective-permute-start | bytes 589832 | tf_op jit(solution)/shard_map/ppermute | solution.py:30
  77.0 7.8 %collective-permute-start.25 = (f32[8,1024]{1,0:T(8,128)S(1)}, f32[8,1024]{1,0:T(8,128)S(1)}, u32[]{:S(2)}, u32[]{:S(2)}) collective-permute-start(f32[8,1024]{1,0:T(8,128)S(1)} %get-tuple-element.111.refs_0_), channel_id=1, source_target_pairs={{0,3},{1,2},{2,1},{3,0},{4,7},{5,6},{6,5},{7,4},{8,11},{9,10},{10,... | collective-permute-start | bytes 98312 | tf_op jit(solution)/shard_map/ppermute | solution.py:30
  80.4 7.0 %collective-permute-start.24 = (f32[8,1024]{1,0:T(8,128)S(1)}, f32[8,1024]{1,0:T(8,128)S(1)}, u32[]{:S(2)}, u32[]{:S(2)}) collective-permute-start(f32[8,1024]{1,0:T(8,128)S(1)} %get-tuple-element.111.refs_0_), channel_id=1, source_target_pairs={{0,2},{1,3},{2,0},{3,1},{4,6},{5,7},{6,4},{7,5},{8,10},{9,11},{10,... | collective-permute-start | bytes 98312 | tf_op jit(solution)/shard_map/ppermute | solution.py:30
  80.4 7.0 %collective-permute-start.23 = (f32[8,1024]{1,0:T(8,128)S(1)}, f32[8,1024]{1,0:T(8,128)S(1)}, u32[]{:S(2)}, u32[]{:S(2)}) collective-permute-start(f32[8,1024]{1,0:T(8,128)S(1)} %get-tuple-element.111.refs_0_), channel_id=1, source_target_pairs={{0,1},{1,0},{2,3},{3,2},{4,5},{5,4},{6,7},{7,6},{8,9},{9,8},{10,11... | collective-permute-start | bytes 98312 | tf_op jit(solution)/shard_map/ppermute | solution.py:30
  81.5 12.9 %collective-permute-start.28 = (f32[24,1024]{1,0:T(8,128)S(1)}, f32[24,1024]{1,0:T(8,128)S(1)}, u32[]{:S(2)}, u32[]{:S(2)}) collective-permute-start(f32[24,1024]{1,0:T(8,128)S(1)} %get-tuple-element.120.upper_ref.refs_0_), channel_id=1, source_target_pairs={{0,3},{1,2},{2,1},{3,0},{4,7},{5,6},{6,5},{7,4},{8,11},{9,10},{10,... | collective-permute-start | bytes 294920 | tf_op jit(solution)/shard_map/ppermute | solution.py:30
  84.8 9.6 %collective-permute-start.27 = (f32[24,1024]{1,0:T(8,128)S(1)}, f32[24,1024]{1,0:T(8,128)S(1)}, u32[]{:S(2)}, u32[]{:S(2)}) collective-permute-start(f32[24,1024]{1,0:T(8,128)S(1)} %get-tuple-element.120.upper_ref.refs_0_), channel_id=1, source_target_pairs={{0,2},{1,3},{2,0},{3,1},{4,6},{5,7},{6,4},{7,5},{8,10},{9,11},{10,... | collective-permute-start | bytes 294920 | tf_op jit(solution)/shard_map/ppermute | solution.py:30
  84.8 9.7 %collective-permute-start.26 = (f32[24,1024]{1,0:T(8,128)S(1)}, f32[24,1024]{1,0:T(8,128)S(1)}, u32[]{:S(2)}, u32[]{:S(2)}) collective-permute-start(f32[24,1024]{1,0:T(8,128)S(1)} %get-tuple-element.120.upper_ref.refs_0_), channel_id=1, source_target_pairs={{0,1},{1,0},{2,3},{3,2},{4,5},{5,4},{6,7},{7,6},{8,9},{9,8},{10,11... | collective-permute-start | bytes 294920 | tf_op jit(solution)/shard_map/ppermute | solution.py:30
  94.4 1.5 %collective-permute-start.29 = (f32[48,1024]{1,0:T(8,128)S(1)}, f32[48,1024]{1,0:T(8,128)S(1)}, u32[]{:S(2)}, u32[]{:S(2)}) collective-permute-start(f32[48,1024]{1,0:T(8,128)S(1)} %get-tuple-element.128), channel_id=1, source_target_pairs={{0,4},{4,0},{8,12},{12,8},{16,20},{20,16},{24,28},{28,24},{1,5},{5... | collective-permute-start | bytes 589832 | tf_op jit(solution)/shard_map/ppermute | solution.py:30
  94.5 1.7 %collective-permute-start.30 = (f32[48,1024]{1,0:T(8,128)S(1)}, f32[48,1024]{1,0:T(8,128)S(1)}, u32[]{:S(2)}, u32[]{:S(2)}) collective-permute-start(f32[48,1024]{1,0:T(8,128)S(1)} %get-tuple-element.129), channel_id=1, source_target_pairs={{0,4},{4,0},{8,12},{12,8},{16,20},{20,16},{24,28},{28,24},{1,5},{5... | collective-permute-start | bytes 589832 | tf_op jit(solution)/shard_map/ppermute | solution.py:30
  95.0 1.5 %collective-permute-start.31 = (f32[48,1024]{1,0:T(8,128)S(1)}, f32[48,1024]{1,0:T(8,128)S(1)}, u32[]{:S(2)}, u32[]{:S(2)}) collective-permute-start(f32[48,1024]{1,0:T(8,128)S(1)} %get-tuple-element.130), channel_id=1, source_target_pairs={{0,4},{4,0},{8,12},{12,8},{16,20},{20,16},{24,28},{28,24},{1,5},{5... | collective-permute-start | bytes 589832 | tf_op jit(solution)/shard_map/ppermute | solution.py:30
  95.1 1.7 %collective-permute-start.32 = (f32[48,1024]{1,0:T(8,128)S(1)}, f32[48,1024]{1,0:T(8,128)S(1)}, u32[]{:S(2)}, u32[]{:S(2)}) collective-permute-start(f32[48,1024]{1,0:T(8,128)S(1)} %get-tuple-element.131), channel_id=1, source_target_pairs={{0,4},{4,0},{8,12},{12,8},{16,20},{20,16},{24,28},{28,24},{1,5},{5... | collective-permute-start | bytes 589832 | tf_op jit(solution)/shard_map/ppermute | solution.py:30
  96.9 7.8 %collective-permute-start.33 = (f32[48,1024]{1,0:T(8,128)S(1)}, f32[48,1024]{1,0:T(8,128)S(1)}, u32[]{:S(2)}, u32[]{:S(2)}) collective-permute-start(f32[48,1024]{1,0:T(8,128)S(1)} %get-tuple-element.137), channel_id=1, source_target_pairs={{0,8},{4,12},{8,0},{12,4},{16,24},{20,28},{24,16},{28,20},{1,9},{5... | collective-permute-start | bytes 589832 | tf_op jit(solution)/shard_map/ppermute | solution.py:30
  97.0 11.3 %collective-permute-start.34 = (f32[48,1024]{1,0:T(8,128)S(1)}, f32[48,1024]{1,0:T(8,128)S(1)}, u32[]{:S(2)}, u32[]{:S(2)}) collective-permute-start(f32[48,1024]{1,0:T(8,128)S(1)} %get-tuple-element.138), channel_id=1, source_target_pairs={{0,16},{4,20},{8,24},{12,28},{16,0},{20,4},{24,8},{28,12},{1,17},{... | collective-permute-start | bytes 589832 | tf_op jit(solution)/shard_map/ppermute | solution.py:30
  97.0 11.2 %collective-permute-start.35 = (f32[48,1024]{1,0:T(8,128)S(1)}, f32[48,1024]{1,0:T(8,128)S(1)}, u32[]{:S(2)}, u32[]{:S(2)}) collective-permute-start(f32[48,1024]{1,0:T(8,128)S(1)} %get-tuple-element.139), channel_id=1, source_target_pairs={{0,24},{4,28},{8,16},{12,20},{16,8},{20,12},{24,0},{28,4},{1,25},{... | collective-permute-start | bytes 589832 | tf_op jit(solution)/shard_map/ppermute | solution.py:30
  100.4 8.5 %collective-permute-start.38 = (f32[24,1024]{1,0:T(8,128)S(1)}, f32[24,1024]{1,0:T(8,128)S(1)}, u32[]{:S(2)}, u32[]{:S(2)}) collective-permute-start(f32[24,1024]{1,0:T(8,128)S(1)} %get-tuple-element.145.lower_ref.refs_4_), channel_id=1, source_target_pairs={{0,3},{1,2},{2,1},{3,0},{4,7},{5,6},{6,5},{7,4},{8,11},{9,10},{10,... | collective-permute-start | bytes 294920 | tf_op jit(solution)/shard_map/ppermute | solution.py:30
  102.2 8.5 %collective-permute-start.37 = (f32[24,1024]{1,0:T(8,128)S(1)}, f32[24,1024]{1,0:T(8,128)S(1)}, u32[]{:S(2)}, u32[]{:S(2)}) collective-permute-start(f32[24,1024]{1,0:T(8,128)S(1)} %get-tuple-element.145.lower_ref.refs_4_), channel_id=1, source_target_pairs={{0,2},{1,3},{2,0},{3,1},{4,6},{5,7},{6,4},{7,5},{8,10},{9,11},{10,... | collective-permute-start | bytes 294920 | tf_op jit(solution)/shard_map/ppermute | solution.py:30
  104.7 6.5 %collective-permute-start.36 = (f32[24,1024]{1,0:T(8,128)S(1)}, f32[24,1024]{1,0:T(8,128)S(1)}, u32[]{:S(2)}, u32[]{:S(2)}) collective-permute-start(f32[24,1024]{1,0:T(8,128)S(1)} %get-tuple-element.145.lower_ref.refs_4_), channel_id=1, source_target_pairs={{0,1},{1,0},{2,3},{3,2},{4,5},{5,4},{6,7},{7,6},{8,9},{9,8},{10,11... | collective-permute-start | bytes 294920 | tf_op jit(solution)/shard_map/ppermute | solution.py:30
  111.1 5.9 %collective-permute-start.39 = (f32[48,256]{1,0:T(8,128)S(1)}, f32[48,256]{1,0:T(8,128)S(1)}, u32[]{:S(2)}, u32[]{:S(2)}) collective-permute-start(f32[48,256]{1,0:T(8,128)S(1)} %get-tuple-element.150), channel_id=1, source_target_pairs={{0,1},{1,0},{2,3},{3,2},{4,5},{5,4},{6,7},{7,6},{8,9},{9,8},{10,11... | collective-permute-start | bytes 147464 | tf_op jit(solution)/shard_map/ppermute | solution.py:30
  111.1 5.9 %collective-permute-start.40 = (f32[48,256]{1,0:T(8,128)S(1)}, f32[48,256]{1,0:T(8,128)S(1)}, u32[]{:S(2)}, u32[]{:S(2)}) collective-permute-start(f32[48,256]{1,0:T(8,128)S(1)} %get-tuple-element.151), channel_id=1, source_target_pairs={{0,2},{1,3},{2,0},{3,1},{4,6},{5,7},{6,4},{7,5},{8,10},{9,11},{10,... | collective-permute-start | bytes 147464 | tf_op jit(solution)/shard_map/ppermute | solution.py:30
  113.5 5.9 %collective-permute-start.41 = (f32[48,256]{1,0:T(8,128)S(1)}, f32[48,256]{1,0:T(8,128)S(1)}, u32[]{:S(2)}, u32[]{:S(2)}) collective-permute-start(f32[48,256]{1,0:T(8,128)S(1)} %get-tuple-element.152), channel_id=1, source_target_pairs={{0,3},{1,2},{2,1},{3,0},{4,7},{5,6},{6,5},{7,4},{8,11},{9,10},{10,... | collective-permute-start | bytes 147464 | tf_op jit(solution)/shard_map/ppermute | solution.py:30
  120.7 1.6 %collective-permute-start.42 = (f32[4,56,256]{2,1,0:T(8,128)S(1)}, f32[4,56,256]{2,1,0:T(8,128)S(1)}, u32[]{:S(2)}, u32[]{:S(2)}) collective-permute-start(f32[4,56,256]{2,1,0:T(8,128)S(1)} %get-tuple-element.164), channel_id=1, source_target_pairs={{0,4},{4,0},{8,12},{12,8},{16,20},{20,16},{24,28},{28,24},{1,5},{5... | collective-permute-start | bytes 688136 | tf_op jit(solution)/shard_map/ppermute | solution.py:30
  122.3 4.2 %collective-permute-start.43 = (f32[56,256]{1,0:T(8,128)S(1)}, f32[56,256]{1,0:T(8,128)S(1)}, u32[]{:S(2)}, u32[]{:S(2)}) collective-permute-start(f32[56,256]{1,0:T(8,128)S(1)} %get-tuple-element.170), channel_id=1, source_target_pairs={{0,1},{1,0},{2,3},{3,2},{4,5},{5,4},{6,7},{7,6},{8,9},{9,8},{10,11... | collective-permute-start | bytes 172040 | tf_op jit(solution)/shard_map/ppermute | solution.py:30
  122.4 6.5 %collective-permute-start.45 = (f32[56,256]{1,0:T(8,128)S(1)}, f32[56,256]{1,0:T(8,128)S(1)}, u32[]{:S(2)}, u32[]{:S(2)}) collective-permute-start(f32[56,256]{1,0:T(8,128)S(1)} %get-tuple-element.171), channel_id=1, source_target_pairs={{0,3},{1,2},{2,1},{3,0},{4,7},{5,6},{6,5},{7,4},{8,11},{9,10},{10,... | collective-permute-start | bytes 172040 | tf_op jit(solution)/shard_map/ppermute | solution.py:30
  124.4 6.8 %collective-permute-start.44 = (f32[56,256]{1,0:T(8,128)S(1)}, f32[56,256]{1,0:T(8,128)S(1)}, u32[]{:S(2)}, u32[]{:S(2)}) collective-permute-start(f32[56,256]{1,0:T(8,128)S(1)} %get-tuple-element.172), channel_id=1, source_target_pairs={{0,2},{1,3},{2,0},{3,1},{4,6},{5,7},{6,4},{7,5},{8,10},{9,11},{10,... | collective-permute-start | bytes 172040 | tf_op jit(solution)/shard_map/ppermute | solution.py:30
  131.3 5.1 %collective-permute-start.48 = (f32[56,256]{1,0:T(8,128)S(1)}, f32[56,256]{1,0:T(8,128)S(1)}, u32[]{:S(2)}, u32[]{:S(2)}) collective-permute-start(f32[56,256]{1,0:T(8,128)S(1)} %fusion.2), channel_id=1, source_target_pairs={{0,24},{4,28},{8,16},{12,20},{16,8},{20,12},{24,0},{28,4},{1,25},{... | collective-permute-start | bytes 172040 | tf_op jit(solution)/shard_map/ppermute | solution.py:30
  131.5 5.0 %collective-permute-start.47 = (f32[56,256]{1,0:T(8,128)S(1)}, f32[56,256]{1,0:T(8,128)S(1)}, u32[]{:S(2)}, u32[]{:S(2)}) collective-permute-start(f32[56,256]{1,0:T(8,128)S(1)} %fusion.2), channel_id=1, source_target_pairs={{0,16},{4,20},{8,24},{12,28},{16,0},{20,4},{24,8},{28,12},{1,17},{... | collective-permute-start | bytes 172040 | tf_op jit(solution)/shard_map/ppermute | solution.py:30
  133.1 4.2 %collective-permute-start.46 = (f32[56,256]{1,0:T(8,128)S(1)}, f32[56,256]{1,0:T(8,128)S(1)}, u32[]{:S(2)}, u32[]{:S(2)}) collective-permute-start(f32[56,256]{1,0:T(8,128)S(1)} %fusion.2), channel_id=1, source_target_pairs={{0,8},{4,12},{8,0},{12,4},{16,24},{20,28},{24,16},{28,20},{1,9},{5... | collective-permute-start | bytes 172040 | tf_op jit(solution)/shard_map/ppermute | solution.py:30
  137.3 1.3 collective-permute-start.49

commit v3 on v2

--- a/solution.py
+++ b/solution.py
@@ -11,7 +11,7 @@
 CHUNK = 4
 UNROLL = 4
 FETCH = 4
-RING = 16
+DEPTH = 3
 PAD = 48
 HALF = 24
 
@@ -46,7 +46,7 @@
     return one(lh, rh) + (one(lh, rl) + one(ll, rh))
 
 
-def call(body, outs, scratch, *args, specs=None, out_specs=None, limit=12, flops=0, moved=0):
+def call(body, outs, scratch, *args, specs=None, out_specs=None, limit=20, flops=0, moved=0):
     return pl.pallas_call(
         body,
         out_shape=outs,
@@ -74,7 +74,7 @@
 
 def pack_body(
     count_in, column_in, tiles_ref, pack_ref, list_ref, row_ref, total_ref,
-    count_ref, column_ref, land, store, place, owner, twin_from, twin_to, sem, out_sem, list_sem,
+    count_ref, column_ref, land, place, owner, twin_from, twin_to, sem, list_sem,
 ):
     rows, slots = column_ref.shape
     lists = [
@@ -87,33 +87,27 @@
         copy.wait()
 
     def copies(row, act):
+        ring = lax.rem(row, DEPTH)
+
         def one(group, _):
             part = pl.ds(group * FETCH, FETCH)
             copy = pltpu.make_async_copy(
-                tiles_ref.at[row, part], land.at[pl.ds(row * slots + group * FETCH, FETCH)], sem.at[row, group]
+                tiles_ref.at[row, part], land.at[pl.ds(ring * slots + group * FETCH, FETCH)], sem.at[ring, group]
             )
             act(copy)
             return 0
 
         lax.fori_loop(0, (count_ref[row] + FETCH - 1) // FETCH, one, 0)
 
-    def leave(item):
-        return pltpu.make_async_copy(store.at[lax.rem(item, RING)], pack_ref.at[item], out_sem.at[lax.rem(item, RING)])
-
-    def free(item):
-        @pl.when(item >= RING)
-        def _():
-            leave(item - RING).wait()
-
     def start(copy):
         copy.start()
 
     def wait(copy):
         copy.wait()
 
-    for row in range(rows):
+    for row in range(DEPTH):
         copies(row, start)
-    land[rows * slots] = jnp.zeros((BLOCK, BLOCK), f32)
+    land[DEPTH * slots] = jnp.zeros((BLOCK, BLOCK), f32)
 
     def clear(index, _):
         place[index] = -1
@@ -123,6 +117,7 @@
 
     def one_row(row, begin):
         stamp = row * slots
+        shift = stamp - lax.rem(row, DEPTH) * slots
 
         def scan(slot, state):
             found, twins = state
@@ -133,13 +128,13 @@
             @pl.when(fresh)
             def _():
                 place[column] = stamp + slot
-                owner[found] = stamp + slot
+                owner[found] = stamp - shift + slot
                 list_ref[begin * CHUNK + found] = column
 
             @pl.when(jnp.logical_not(fresh))
             def _():
-                twin_from[twins] = stamp + slot
-                twin_to[twins] = at
+                twin_from[twins] = stamp - shift + slot
+                twin_to[twins] = at - shift
 
             step = fresh.astype(jnp.int32)
             return found + step, twins + 1 - step
@@ -149,7 +144,7 @@
 
         def blank(index, _):
             list_ref[begin * CHUNK + index] = 0
-            owner[index] = rows * slots
+            owner[index] = DEPTH * slots
             return 0
 
         lax.fori_loop(found, steps * CHUNK, blank, 0)
@@ -165,17 +160,18 @@
         def convert(step, _):
             item = begin + step
             row_ref[item] = row
-            free(item)
-            place_at = lax.rem(item, RING)
             for q in range(CHUNK):
                 at = slice(q * BLOCK, (q + 1) * BLOCK)
                 high, low = split(land[owner[step * CHUNK + q]])
-                store[place_at, :BLOCK, at] = high
-                store[place_at, BLOCK:, at] = low
-            leave(item).start()
+                pack_ref[item, :BLOCK, at] = high
+                pack_ref[item, BLOCK:, at] = low
             return 0
 
         lax.fori_loop(0, steps, convert, 0)
+
+        @pl.when(row + DEPTH < rows)
+        def _():
+            copies(row + DEPTH, start)
 
         return begin + steps
 
@@ -186,19 +182,11 @@
         row_ref[item] = 0
         for q in range(CHUNK):
             list_ref[item * CHUNK + q] = 0
-        free(item)
-        store[lax.rem(item, RING)] = jnp.zeros(store.shape[1:], bf16)
-        leave(item).start()
+        pack_ref[item] = jnp.zeros(pack_ref.shape[1:], bf16)
         return 0
 
     lax.fori_loop(used, total, fill, 0)
     total_ref[0] = total // UNROLL
-
-    def last(item, _):
-        leave(item).wait()
-        return 0
-
-    lax.fori_loop(jnp.maximum(total - RING, 0), total, last, 0)
 
 
 def pack(tiles, tile_column, tile_count, block_total):
@@ -208,7 +196,7 @@
     return call(
         pack_body,
         [
-            pltpu.HBM((items, 2 * BLOCK, CHUNK * BLOCK), bf16),
+            pltpu.VMEM((items, 2 * BLOCK, CHUNK * BLOCK), bf16),
             shape((items * CHUNK,), jnp.int32),
             shape((items,), jnp.int32),
             shape((1,), jnp.int32),
@@ -216,22 +204,20 @@
         [
             pltpu.SMEM(tile_count.shape, jnp.int32),
             pltpu.SMEM(tile_column.shape, jnp.int32),
-            pltpu.VMEM((rows * slots + 1, BLOCK, BLOCK), f32),
-            pltpu.VMEM((RING, 2 * BLOCK, CHUNK * BLOCK), bf16),
+            pltpu.VMEM((DEPTH * slots + 1, BLOCK, BLOCK), f32),
             pltpu.SMEM((block_total,), jnp.int32),
             pltpu.SMEM((slots,), jnp.int32),
             pltpu.SMEM((slots,), jnp.int32),
             pltpu.SMEM((slots,), jnp.int32),
-            pltpu.SemaphoreType.DMA((rows, slots // FETCH)),
-            pltpu.SemaphoreType.DMA((RING,)),
+            pltpu.SemaphoreType.DMA((DEPTH, slots // FETCH)),
             pltpu.SemaphoreType.DMA((2,)),
         ],
-        tile_count,
-        tile_column,
+        pltpu.with_memory_space_constraint(tile_count, pltpu.HBM),
+        pltpu.with_memory_space_constraint(tile_column, pltpu.HBM),
         tiles,
         specs=[pl.BlockSpec(memory_space=pl.ANY)] * 3,
-        out_specs=[pl.BlockSpec(memory_space=pltpu.HBM), SMEM, SMEM, SMEM],
-        limit=52,
+        out_specs=[VMEM, SMEM, SMEM, SMEM],
+        limit=20,
         flops=10**8,
         moved=40 * MIB,
     )
@@ -257,11 +243,10 @@
     values[at, channels:] = low
 
 
-def mix_rows(total_ref, list_ref, row_ref, one, store, values, sums):
+def mix_rows(total_ref, list_ref, row_ref, store, values, sums):
     sums[...] = jnp.zeros_like(sums)
 
     def step(group, _):
-        one(group).wait()
         for part in range(UNROLL):
             item = group * UNROLL + part
             left = jnp.concatenate([values[list_ref[item * CHUNK + q]] for q in range(CHUNK)], axis=1)
@@ -283,15 +268,14 @@
 
 def mix_in_body(nodes, cols, ids_ref, total_ref, list_ref, row_ref, pack_ref, *refs):
     pieces, outs = refs[:nodes], refs[nodes : nodes + cols]
-    values, sums, store, sem = refs[nodes + cols :]
-    one = bring(total_ref, pack_ref, store, sem)
+    values, sums = refs[nodes + cols :]
     rows = sums.shape[0]
     node, col = ids_ref[0], ids_ref[1]
     for offset in range(nodes):
         base = (node ^ offset) * rows
         for part in range(rows):
             store_block(values, base + part, pieces[offset][:, part * BLOCK : (part + 1) * BLOCK])
-    mix_rows(total_ref, list_ref, row_ref, one, store, values, sums)
+    mix_rows(total_ref, list_ref, row_ref, pack_ref, values, sums)
     slice_rows = rows // cols
     for offset in range(cols):
         for part in range(slice_rows):
@@ -301,8 +285,8 @@
 
 def dense_body(cols, per, ids_ref, *refs):
     pieces, weights = refs[:cols], refs[cols : 2 * cols]
-    mixed_ref, hidden_ref, slope_ref, weight_out_ref = refs[2 * cols : 2 * cols + 4]
-    outs = refs[2 * cols + 4 : 3 * cols + 4]
+    mixed_ref, hidden_ref, slope_ref, weight_out_ref = refs[2 * cols + 1 : 2 * cols + 5]
+    outs = refs[2 * cols + 5 : 3 * cols + 5]
     held, held_weights, scores = refs[-3:]
     col = ids_ref[1]
     for offset in range(cols):
@@ -335,14 +319,13 @@
 
 
 def stack_body(*refs):
-    for index, ref in enumerate(refs[:-1]):
+    for index, ref in enumerate(refs[:-2]):
         refs[-1][index] = ref[...]
 
 
 def mix_out_body(nodes, cols, per, ids_ref, total_ref, list_ref, row_ref, pack_ref, bias_ref, labels_ref, *refs):
     pieces = refs[:nodes]
-    upper_ref, lower_ref, stats_ref, values, sums, groups, store, sem = refs[nodes:]
-    one = bring(total_ref, pack_ref, store, sem)
+    upper_ref, lower_ref, stats_ref, values, sums, groups = refs[nodes:]
     rows = sums.shape[0]
     node, col = ids_ref[0], ids_ref[1]
     slice_rows = rows // cols
@@ -359,7 +342,7 @@
                     base + (col ^ group) * slice_rows + part,
                     pieces[offset][group, :, part * BLOCK : (part + 1) * BLOCK],
                 )
-    mix_rows(total_ref, list_ref, row_ref, one, store, values, sums)
+    mix_rows(total_ref, list_ref, row_ref, pack_ref, values, sums)
     for row in range(rows):
         at = slice(row * BLOCK, (row + 1) * BLOCK)
         total = mixed_row(sums, row) + groups[col]
@@ -380,8 +363,7 @@
 
 def mix_back_body(nodes, cols, per, ids_ref, total_ref, list_ref, row_ref, pack_ref, upper_ref, lower_ref, labels_ref, mask_ref, *refs):
     stats, outs = refs[:cols], refs[cols : cols + nodes]
-    extra_ref, sums, grads, store, sem = refs[cols + nodes :]
-    one = bring(total_ref, pack_ref, store, sem)
+    extra_ref, sums, grads = refs[cols + nodes :]
     rows = grads.shape[0]
     node, col = ids_ref[0], ids_ref[1]
     tops = [ref[0:1] for ref in stats]
@@ -421,10 +403,9 @@
     sums[...] = jnp.zeros_like(sums)
 
     def step(group, _):
-        one(group).wait()
         for part in range(UNROLL):
             item = group * UNROLL + part
-            terms = jnp.dot(grads[row_ref[item]], store[item], preferred_element_type=f32)
+            terms = jnp.dot(grads[row_ref[item]], pack_ref[item], preferred_element_type=f32)
             half = terms.shape[0] // 2
             terms = terms[:half] + terms[half:]
             for q in range(CHUNK):
@@ -549,23 +530,24 @@
         + jnp.pad(weight_out, ((feats, 8), (0, units - classes)))
         + jnp.pad(bias_in[None, :], ((feats + own, 7), (0, units - own)))
     )
+    ids, tile_count = lax.optimization_barrier((ids, tile_count))
     even = gather_chips(features, nodes)
     weight_pieces = [weights] + [exchange(weights, "col", k) for k in range(1, cols)]
     packed, listed, placed, steps = pack(tiles, tile_column, tile_count, block_total)
     steps, even, weight_pieces = lax.optimization_barrier((steps, even, weight_pieces))
     feature_pieces = gather_cores(even)
+    packed = pltpu.with_memory_space_constraint(packed, pltpu.VMEM)
     sparse = (ids, steps, listed, placed, packed)
-    sparse_specs = [SMEM] * 4 + [pl.BlockSpec(memory_space=pltpu.HBM)]
-    held = [pltpu.VMEM(packed.shape, bf16), pltpu.SemaphoreType.DMA((packed.shape[0] // UNROLL,))]
+    sparse_specs = [SMEM] * 4 + [VMEM]
 
     mixed_parts = call(
         functools.partial(mix_in_body, nodes, cols),
         [shape((feats, slice_nodes), f32)] * cols,
-        [pltpu.VMEM((block_total, 2 * feats, BLOCK), bf16), pltpu.VMEM((rows, 2 * feats, 2 * BLOCK), f32), *held],
+        [pltpu.VMEM((block_total, 2 * feats, BLOCK), bf16), pltpu.VMEM((rows, 2 * feats, 2 * BLOCK), f32)],
         *sparse,
         *feature_pieces,
         specs=sparse_specs + [VMEM] * nodes,
-        limit=44,
+        limit=20,
         flops=10**9,
         moved=16 * MIB,
     )
@@ -584,7 +566,8 @@
         ids,
         *mixed_pieces,
         *weight_pieces,
-        specs=[SMEM] + [VMEM] * (2 * cols),
+        packed,
+        specs=[SMEM] + [VMEM] * (2 * cols + 1),
         flops=10**8,
         moved=2 * MIB,
     )
@@ -593,21 +576,21 @@
         stack_body,
         [shape((cols, PAD, slice_nodes), f32)],
         [],
-        *score_pieces,
-        limit=4,
+        *score_pieces, packed,
+        limit=20,
         moved=MIB,
     )
     scores = gather_cores(gather_chips(stacked, nodes))
     upper, lower, stats = call(
         functools.partial(mix_out_body, nodes, cols, per),
         [shape((HALF, local), f32), shape((PAD - HALF, local), f32), shape((8, local), f32)],
-        [pltpu.VMEM((block_total, 2 * PAD, BLOCK), bf16), pltpu.VMEM((rows, 2 * PAD, 2 * BLOCK), f32), pltpu.VMEM((cols, PAD, 1), f32), *held],
+        [pltpu.VMEM((block_total, 2 * PAD, BLOCK), bf16), pltpu.VMEM((rows, 2 * PAD, 2 * BLOCK), f32), pltpu.VMEM((cols, PAD, 1), f32)],
         *sparse,
         bias_out[None, :],
         labels,
         *scores,
         specs=sparse_specs + [VMEM] * (2 + nodes),
-        limit=44,
+        limit=20,
         flops=10**9,
         moved=16 * MIB,
     )
@@ -618,7 +601,6 @@
         [
             pltpu.VMEM((block_total, PAD, BLOCK), f32),
             pltpu.VMEM((rows, 2 * PAD, 2 * BLOCK), bf16),
-            *held,
         ],
         *sparse,
         upper,
@@ -627,7 +609,7 @@
         train_mask,
         *stats_pieces,
         specs=sparse_specs + [VMEM] * (4 + cols),
-        limit=44,
+        limit=20,
         flops=10**9,
         moved=16 * MIB,
     )
@@ -639,7 +621,7 @@
         [],
         *spread_parts[::2],
         *[exchange(part, "node", 1) for part in spread_parts[1::2]],
-        limit=8,
+        limit=20,
         moved=2 * MIB,
     )
     paired, lower = lax.optimization_barrier((paired, lower))
@@ -653,7 +635,7 @@
         paired[0],
         *chips,
         specs=[SMEM] + [VMEM] * (nodes // 2),
-        limit=8,
+        limit=20,
         moved=MIB,
     )
     spread_slices, lowers = lax.optimization_barrier((spread_slices, lowers))
@@ -666,7 +648,7 @@
         *uppers,
         *lowers,
         specs=[SMEM] + [VMEM] * (2 * cols),
-        limit=8,
+        limit=20,
         moved=2 * MIB,
     )
     logits, *spread_pieces = lax.optimization_barrier((logits, *spread_pieces))

time: 138 us -> 129 us (0.935); the launches traced: 140 us -> 128 us
  Pallas kernels: 46.7 us -> 34.3 us
  waiting for transfers between devices: 38.7 us -> 40.6 us
    pallas_call x11, Pallas kernels: 46.7 us -> 34.3 us  [call(): pl.pallas_call(body, out_shape=outs, in_specs=specs or [VMEM] * len(args)...]
    ppermute x50, waiting for transfers between devices: 38.7 us -> 40.6 us  [exchange(): return lax.ppermute(value, axis, [(i, i ^ offset) for i in range(total)])]
  transfers between devices with their start and end apart: 50 -> 50, of which waited for: 29 -> 30; matrix products, arithmetic and copies ran while one was open for 0% -> 0% of each run, Pallas kernels for 18% -> 14%
where the time goes in v3:
time: 129 us; the launch traced here: 128 us
  starting transfers between devices  51.6 us (40%)
  waiting for transfers between devices  40.6 us (31%)
  Pallas kernels  34.3 us (27%)
    ppermute x50, starting transfers between devices, exchange(): return lax.ppermute(value, axis, [(i, i ^ offset) for i in range(total)])  51.6 us
    ppermute x50, waiting for transfers between devices, exchange(): return lax.ppermute(value, axis, [(i, i ^ offset) for i in range(total)])  40.6 us
    pallas_call x11, Pallas kernels, call(): pl.pallas_call(body, out_shape=outs, in_specs=specs or [VMEM] * len(args)...  34.3 us
  transfers between devices with their start and end apart: 50, of which 30 were waited for; matrix products, arithmetic and copies ran while one was open for 0% of the time, Pallas kernels for 14%

profile of v3, /device:TPU:0, one launch (start us, length us, event | category | flops | bytes accessed | tf_op | source)
XLA Modules:
  0.0 128.5 jit_solution(7185674151577668827)
XLA Ops:
  0.6 0.9 pad_add_fusion.refs_4_
  1.5 5.1 %collective-permute-start.5 = (f32[104,256]{1,0:T(8,128)S(1)}, f32[104,256]{1,0:T(8,128)S(1)}, u32[]{:S(2)}, u32[]{:S(2)}) collective-permute-start(f32[104,256]{1,0:T(8,128)S(1)} %pad_add_fusion.refs_4_), channel_id=1, source_target_pairs={{0,3},{1,2},{2,1},{3,0},{4,7},{5,6},{6,5},{7,4},{8,11},{9,10},{10,... | collective-permute-start | bytes 319496 | tf_op jit(solution)/shard_map/ppermute | solution.py:30
  6.7 1.5 %collective-permute-start.1 = (f32[32,1024]{1,0:T(8,128)}, f32[32,1024]{1,0:T(8,128)S(1)}, u32[]{:S(2)}, u32[]{:S(2)}) collective-permute-start(f32[32,1024]{1,0:T(8,128)} %refs_0_), channel_id=1, source_target_pairs={{0,16},{4,20},{8,24},{12,28},{16,0},{20,4},{24,8},{28,12},{1,17},{... | collective-permute-start | bytes 393224 | tf_op jit(solution)/shard_map/ppermute | solution.py:30
  8.2 1.5 %collective-permute-start = (f32[32,1024]{1,0:T(8,128)}, f32[32,1024]{1,0:T(8,128)S(1)}, u32[]{:S(2)}, u32[]{:S(2)}) collective-permute-start(f32[32,1024]{1,0:T(8,128)} %refs_0_), channel_id=1, source_target_pairs={{0,8},{4,12},{8,0},{12,4},{16,24},{20,28},{24,16},{28,20},{1,9},{5... | collective-permute-start | bytes 393224 | tf_op jit(solution)/shard_map/ppermute | solution.py:30
  9.7 0.5 collective-permute-start.2
  10.2 1.5 %collective-permute-start.3 = (f32[104,256]{1,0:T(8,128)S(1)}, f32[104,256]{1,0:T(8,128)S(1)}, u32[]{:S(2)}, u32[]{:S(2)}) collective-permute-start(f32[104,256]{1,0:T(8,128)S(1)} %pad_add_fusion.refs_4_), channel_id=1, source_target_pairs={{0,1},{1,0},{2,3},{3,2},{4,5},{5,4},{6,7},{7,6},{8,9},{9,8},{10,11... | collective-permute-start | bytes 319496 | tf_op jit(solution)/shard_map/ppermute | solution.py:30
  11.7 11.3 %shard_map.145 = (bf16[128,256,512]{2,1,0:T(8,128)(2,1)S(1)}, s32[512]{0:T(512)S(1)}, s32[128]{0:T(128)S(1)}, s32[1]{0:T(128)}) custom-call(s32[8]{0:T(128)} %count_in, s32[8,64]{1,0:T(8,128)} %column_in.1, f32[8,64,128,128]{3,2,1,0:T(8,128)} %tiles_ref.1), custom_call_target="tpu_custom_call" | custom-call | flops 100000000 | bytes 41943040 | tf_op jit(solution)/shard_map/pallas_call | solution.py:50
  23.2 0.5 collective-permute-start.7
  23.8 0.4 collective-permute-start.9
  25.2 5.9 %shard_map.146 = (f32[32,256]{1,0:T(8,128)S(1)}, f32[32,256]{1,0:T(8,128)S(1)}, f32[32,256]{1,0:T(8,128)S(1)}, f32[32,256]{1,0:T(8,128)S(1)}) custom-call(s32[2]{0:T(128)S(1)} %pad_add_fusion.1.ids_ref, s32[1]{0:T(128)} %get-tuple-element.93.total_ref, s32[512]{0:T(512)S(1)} %get-tuple-element.94.list_ref, s32[128]{0:T(128)S(1)} %get-tuple-element.95.row_ref, ...), custom_call_target="tpu_custom_call" | custom-call | flops 1000000000 | bytes 16777216 | tf_op jit(solution)/shard_map/pallas_call | solution.py:50
  31.1 0.6 collective-permute-start.10
  31.7 3.8 %collective-permute-start.11 = (f32[32,256]{1,0:T(8,128)S(1)}, f32[32,256]{1,0:T(8,128)S(1)}, u32[]{:S(2)}, u32[]{:S(2)}) collective-permute-start(f32[32,256]{1,0:T(8,128)S(1)} %get-tuple-element.103), channel_id=1, source_target_pairs={{0,2},{1,3},{2,0},{3,1},{4,6},{5,7},{6,4},{7,5},{8,10},{9,11},{10,... | collective-permute-start | bytes 98312 | tf_op jit(solution)/shard_map/ppermute | solution.py:30
  35.6 2.5 %collective-permute-done.11.refs_2_ = f32[32,256]{1,0:T(8,128)S(1)} collective-permute-done((f32[32,256]{1,0:T(8,128)S(1)}, f32[32,256]{1,0:T(8,128)S(1)}, u32[]{:S(2)}, u32[]{:S(2)}) %collective-permute-start.11) | collective-permute-done | bytes 32800 | tf_op jit(solution)/shard_map/ppermute | solution.py:30
  38.1 3.2 %collective-permute-done.12.refs_3_ = f32[32,256]{1,0:T(8,128)S(1)} collective-permute-done((f32[32,256]{1,0:T(8,128)S(1)}, f32[32,256]{1,0:T(8,128)S(1)}, u32[]{:S(2)}, u32[]{:S(2)}) %collective-permute-start.12) | collective-permute-done | bytes 32800 | tf_op jit(solution)/shard_map/ppermute | solution.py:30
  41.3 1.3 %shard_map.147 = (f32[128,256]{1,0:T(8,128)S(1)}, f32[256,256]{1,0:T(8,128)S(1)}, f32[256,256]{1,0:T(8,128)S(1)}, f32[256,172]{1,0:T(8,128)S(1)}, f32[48,256]{1,...) custom-call(s32[2]{0:T(128)S(1)} %pad_add_fusion.1.ids_ref, ...), custom_call_target="tpu_custom_call" | custom-call | flops 100000000 | bytes 2097152 | tf_op jit(solution)/shard_map/pallas_call | solution.py:50
  42.7 1.0 collective-permute-start.14
  43.7 3.4 %collective-permute-start.15 = (f32[48,256]{1,0:T(8,128)S(1)}, f32[48,256]{1,0:T(8,128)S(1)}, u32[]{:S(2)}, u32[]{:S(2)}) collective-permute-start(f32[48,256]{1,0:T(8,128)S(1)} %get-tuple-element.112), channel_id=1, source_target_pairs={{0,3},{1,2},{2,1},{3,0},{4,7},{5,6},{6,5},{7,4},{8,11},{9,10},{10,... | collective-permute-start | bytes 147464 | tf_op jit(solution)/shard_map/ppermute | solution.py:30
  47.1 0.8 collective-permute-done.13.refs_1_
  47.8 1.8 %collective-permute-done.15.refs_3_ = f32[48,256]{1,0:T(8,128)S(1)} collective-permute-done((f32[48,256]{1,0:T(8,128)S(1)}, f32[48,256]{1,0:T(8,128)S(1)}, u32[]{:S(2)}, u32[]{:S(2)}) %collective-permute-start.15) | collective-permute-done | bytes 49184 | tf_op jit(solution)/shard_map/ppermute | solution.py:30
  49.7 0.4 collective-permute-start.21
  50.0 1.0 collective-permute-start.19
  51.0 2.2 %collective-permute-start.17 = (f32[4,48,256]{2,1,0:T(8,128)S(1)}, f32[4,48,256]{2,1,0:T(8,128)S(1)}, u32[]{:S(2)}, u32[]{:S(2)}) collective-permute-start(f32[4,48,256]{2,1,0:T(8,128)S(1)} %shard_map.148.refs_0_), channel_id=1, source_target_pairs={{0,8},{4,12},{8,0},{12,4},{16,24},{20,28},{24,16},{28,20},{1,9},{5... | collective-permute-start | bytes 589832 | tf_op jit(solution)/shard_map/ppermute | solution.py:30
  53.2 3.8 %collective-permute-done.21.refs_6_ = f32[4,48,256]{2,1,0:T(8,128)S(1)} collective-permute-done((f32[4,48,256]{2,1,0:T(8,128)S(1)}, f32[4,48,256]{2,1,0:T(8,128)S(1)}, u32[]{:S(2)}, u32[]{:S(2)}) %collective-permute-start.21) | collective-permute-done | bytes 196640 | tf_op jit(solution)/shard_map/ppermute | solution.py:30
  57.0 1.8 %collective-permute-done.19.refs_4_ = f32[4,48,256]{2,1,0:T(8,128)S(1)} collective-permute-done((f32[4,48,256]{2,1,0:T(8,128)S(1)}, f32[4,48,256]{2,1,0:T(8,128)S(1)}, u32[]{:S(2)}, u32[]{:S(2)}) %collective-permute-start.19) | collective-permute-done | bytes 196640 | tf_op jit(solution)/shard_map/ppermute | solution.py:30
  58.9 0.5 collective-permute-start.18
  59.4 0.9 collective-permute-done.20.refs_5_
  60.6 6.2 %shard_map.149 = (f32[24,1024]{1,0:T(8,128)S(1)}, f32[24,1024]{1,0:T(8,128)S(1)}, f32[8,1024]{1,0:T(8,128)S(1)}) custom-call(s32[2]{0:T(128)S(1)} %pad_add_fusion.1.ids_ref, s32[1]{0:T(128)} %get-tuple-element.93.total_ref, s32[512]{0:T(512)S(1)} %get-tuple-element.94.list_ref, s32[128]{0:T(128)S(1)} %get-tuple-element.95.row_ref, ...), custom_call_target="tpu_custom_call" | custom-call | flops 1000000000 | bytes 16777216 | tf_op jit(solution)/shard_map/pallas_call | solution.py:50
  66.8 2.4 %collective-permute-start.25 = (f32[8,1024]{1,0:T(8,128)S(1)}, f32[8,1024]{1,0:T(8,128)S(1)}, u32[]{:S(2)}, u32[]{:S(2)}) collective-permute-start(f32[8,1024]{1,0:T(8,128)S(1)} %get-tuple-element.115.refs_0_), channel_id=1, source_target_pairs={{0,3},{1,2},{2,1},{3,0},{4,7},{5,6},{6,5},{7,4},{8,11},{9,10},{10,... | collective-permute-start | bytes 98312 | tf_op jit(solution)/shard_map/ppermute | solution.py:30
  69.2 2.0 %collective-permute-start.23 = (f32[8,1024]{1,0:T(8,128)S(1)}, f32[8,1024]{1,0:T(8,128)S(1)}, u32[]{:S(2)}, u32[]{:S(2)}) collective-permute-start(f32[8,1024]{1,0:T(8,128)S(1)} %get-tuple-element.115.refs_0_), channel_id=1, source_target_pairs={{0,1},{1,0},{2,3},{3,2},{4,5},{5,4},{6,7},{7,6},{8,9},{9,8},{10,11... | collective-permute-start | bytes 98312 | tf_op jit(solution)/shard_map/ppermute | solution.py:30
  71.2 2.3 %collective-permute-start.28 = (f32[24,1024]{1,0:T(8,128)S(1)}, f32[24,1024]{1,0:T(8,128)S(1)}, u32[]{:S(2)}, u32[]{:S(2)}) collective-permute-start(f32[24,1024]{1,0:T(8,128)S(1)} %get-tuple-element.124.upper_ref.refs_0_), channel_id=1, source_target_pairs={{0,3},{1,2},{2,1},{3,0},{4,7},{5,6},{6,5},{7,4},{8,11},{9,10},{10,... | collective-permute-start | bytes 294920 | tf_op jit(solution)/shard_map/ppermute | solution.py:30
  73.6 2.0 %collective-permute-start.26 = (f32[24,1024]{1,0:T(8,128)S(1)}, f32[24,1024]{1,0:T(8,128)S(1)}, u32[]{:S(2)}, u32[]{:S(2)}) collective-permute-start(f32[24,1024]{1,0:T(8,128)S(1)} %get-tuple-element.124.upper_ref.refs_0_), channel_id=1, source_target_pairs={{0,1},{1,0},{2,3},{3,2},{4,5},{5,4},{6,7},{7,6},{8,9},{9,8},{10,11... | collective-permute-start | bytes 294920 | tf_op jit(solution)/shard_map/ppermute | solution.py:30
  75.7 4.8 %shard_map.150 = (f32[48,1024]{1,0:T(8,128)S(1)}, f32[48,1024]{1,0:T(8,128)S(1)}, f32[48,1024]{1,0:T(8,128)S(1)}, f32[48,1024]{1,0:T(8,128)S(1)}, f32[48,1024]{1...) custom-call(s32[2]{0:T(128)S(1)} %pad_add_fusion.1.ids_ref, ...), custom_call_target="tpu_custom_call" | custom-call | flops 1000000000 | bytes 16777216 | tf_op jit(solution)/shard_map/pallas_call | solution.py:50
  80.5 1.6 %collective-permute-done.27.refs_2_ = f32[24,1024]{1,0:T(8,128)S(1)} collective-permute-done((f32[24,1024]{1,0:T(8,128)S(1)}, f32[24,1024]{1,0:T(8,128)S(1)}, u32[]{:S(2)}, u32[]{:S(2)}) %collective-permute-start.27) | collective-permute-done | bytes 98336 | tf_op jit(solution)/shard_map/ppermute | solution.py:30
  82.1 0.5 collective-permute-start.30
  82.6 0.5 collective-permute-start.32
  83.1 0.4 collective-permute-done.29.refs_4_
  84.4 1.0 collective-permute-start.33
  85.4 0.5 collective-permute-start.34
  86.0 2.0 %collective-permute-start.35 = (f32[48,1024]{1,0:T(8,128)S(1)}, f32[48,1024]{1,0:T(8,128)S(1)}, u32[]{:S(2)}, u32[]{:S(2)}) collective-permute-start(f32[48,1024]{1,0:T(8,128)S(1)} %get-tuple-element.143), channel_id=1, source_target_pairs={{0,24},{4,28},{8,16},{12,20},{16,8},{20,12},{24,0},{28,4},{1,25},{... | collective-permute-start | bytes 589832 | tf_op jit(solution)/shard_map/ppermute | solution.py:30
  88.0 2.3 %collective-permute-start.38 = (f32[24,1024]{1,0:T(8,128)S(1)}, f32[24,1024]{1,0:T(8,128)S(1)}, u32[]{:S(2)}, u32[]{:S(2)}) collective-permute-start(f32[24,1024]{1,0:T(8,128)S(1)} %get-tuple-element.149.lower_ref.refs_4_), channel_id=1, source_target_pairs={{0,3},{1,2},{2,1},{3,0},{4,7},{5,6},{6,5},{7,4},{8,11},{9,10},{10,... | collective-permute-start | bytes 294920 | tf_op jit(solution)/shard_map/ppermute | solution.py:30
  90.3 1.9 %collective-permute-done.33.refs_1_ = f32[48,1024]{1,0:T(8,128)S(1)} collective-permute-done((f32[48,1024]{1,0:T(8,128)S(1)}, f32[48,1024]{1,0:T(8,128)S(1)}, u32[]{:S(2)}, u32[]{:S(2)}) %collective-permute-start.33) | collective-permute-done | bytes 196640 | tf_op jit(solution)/shard_map/ppermute | solution.py:30
  92.4 4.0 %collective-permute-done.34.refs_2_ = f32[48,1024]{1,0:T(8,128)S(1)} collective-permute-done((f32[48,1024]{1,0:T(8,128)S(1)}, f32[48,1024]{1,0:T(8,128)S(1)}, u32[]{:S(2)}, u32[]{:S(2)}) %collective-permute-start.34) | collective-permute-done | bytes 196640 | tf_op jit(solution)/shard_map/ppermute | solution.py:30
  96.4 0.6 shard_map.152
  97.0 1.3 %collective-permute-done.37.refs_6_ = f32[24,1024]{1,0:T(8,128)S(1)} collective-permute-done((f32[24,1024]{1,0:T(8,128)S(1)}, f32[24,1024]{1,0:T(8,128)S(1)}, u32[]{:S(2)}, u32[]{:S(2)}) %collective-permute-start.37) | collective-permute-done | bytes 98336 | tf_op jit(solution)/shard_map/ppermute | solution.py:30
  98.3 0.4 collective-permute-done.36.refs_5_
  98.8 2.8 %collective-permute-start.40 = (f32[48,256]{1,0:T(8,128)S(1)}, f32[48,256]{1,0:T(8,128)S(1)}, u32[]{:S(2)}, u32[]{:S(2)}) collective-permute-start(f32[48,256]{1,0:T(8,128)S(1)} %get-tuple-element.155), channel_id=1, source_target_pairs={{0,2},{1,3},{2,0},{3,1},{4,6},{5,7},{6,4},{7,5},{8,10},{9,11},{10,... | collective-permute-start | bytes 147464 | tf_op jit(solution)/shard_map/ppermute | solution.py:30
  101.6 1.6 %collective-permute-start.41 = (f32[48,256]{1,0:T(8,128)S(1)}, f32[48,256]{1,0:T(8,128)S(1)}, u32[]{:S(2)}, u32[]{:S(2)}) collective-permute-start(f32[48,256]{1,0:T(8,128)S(1)} %get-tuple-element.156), channel_id=1, source_target_pairs={{0,3},{1,2},{2,1},{3,0},{4,7},{5,6},{6,5},{7,4},{8,11},{9,10},{10,... | collective-permute-start | bytes 147464 | tf_op jit(solution)/shard_map/ppermute | solution.py:30
  103.2 1.5 %shard_map.153 = f32[172,1024]{1,0:T(8,128)} custom-call(s32[2]{0:T(128)S(1)} %pad_add_fusion.1.ids_ref, f32[24,1024]{1,0:T(8,128)S(1)} %get-tuple-element.124.upper_ref.refs_0_, f32[24,1024]{1,0:T(8,128)S(1)} %collective-permute-done.26.refs_1_, f32[24,1024]{1,0:T(8,128)S(1)} %collective-permute-done.27.refs_2_, ...), custom_call_target="tpu_custom_call" | custom-call | bytes 2097152 | tf_op jit(solution)/shard_map/pallas_call | solution.py:50
  104.7 2.8 %collective-permute-done.41.refs_3_ = f32[48,256]{1,0:T(8,128)S(1)} collective-permute-done((f32[48,256]{1,0:T(8,128)S(1)}, f32[48,256]{1,0:T(8,128)S(1)}, u32[]{:S(2)}, u32[]{:S(2)}) %collective-permute-start.41) | collective-permute-done | bytes 49184 | tf_op jit(solution)/shard_map/ppermute | solution.py:30
  107.4 1.2 shard_map.154
  108.8 1.5 %collective-permute-done.42 = f32[4,56,256]{2,1,0:T(8,128)S(1)} collective-permute-done((f32[4,56,256]{2,1,0:T(8,128)S(1)}, f32[4,56,256]{2,1,0:T(8,128)S(1)}, u32[]{:S(2)}, u32[]{:S(2)}) %collective-permute-start.42) | collective-permute-done | bytes 229408 | tf_op jit(solution)/shard_map/ppermute | solution.py:30
  110.4 1.7 %collective-permute-start.45 = (f32[56,256]{1,0:T(8,128)S(1)}, f32[56,256]{1,0:T(8,128)S(1)}, u32[]{:S(2)}, u32[]{:S(2)}) collective-permute-start(f32[56,256]{1,0:T(8,128)S(1)} %get-tuple-element.175), channel_id=1, source_target_pairs={{0,3},{1,2},{2,1},{3,0},{4,7},{5,6},{6,5},{7,4},{8,11},{9,10},{10,... | collective-permute-start | bytes 172040 | tf_op jit(solution)/shard_map/ppermute | solution.py:30
  112.1 1.8 %collective-permute-start.44 = (f32[56,256]{1,0:T(8,128)S(1)}, f32[56,256]{1,0:T(8,128)S(1)}, u32[]{:S(2)}, u32[]{:S(2)}) collective-permute-start(f32[56,256]{1,0:T(8,128)S(1)} %get-tuple-element.176), channel_id=1, source_target_pairs={{0,2},{1,3},{2,0},{3,1},{4,6},{5,7},{6,4},{7,5},{8,10},{9,11},{10,... | collective-permute-start | bytes 172040 | tf_op jit(solution)/shard_map/ppermute | solution.py:30
  113.9 0.7 collective-permute-done.43
  114.6 2.4 %collective-permute-done.45 = f32[56,256]{1,0:T(8,128)S(1)} collective-permute-done((f32[56,256]{1,0:T(8,128)S(1)}, f32[56,256]{1,0:T(8,128)S(1)}, u32[]{:S(2)}, u32[]{:S(2)}) %collective-permute-start.45) | collective-permute-done | bytes 57376 | tf_op jit(solution)/shard_map/ppermute | solution.py:30
  116.9 2.4 %collective-permute-done.44 = f32[56,256]{1,0:T(8,128)S(1)} collective-permute-done((f32[56,256]{1,0:T(8,128)S(1)}, f32[56,256]{1,0:T(8,128)S(1)}, u32[]{:S(2)}, u32[]{:S(2)}) %collective-permute-start.44) | collective-permute-done | bytes 57376 | tf_op jit(solution)/shard_map/ppermute | solution.py:30
  119.3 1.0 collective-permute-start.48
  120.3 1.4 %collective-permute-start.47 = (f32[56,256]{1,0:T(8,128)S(1)}, f32[56,256]{1,0:T(8,128)S(1)}, u32[]{:S(2)}, u32[]{:S(2)}) collective-permute-start(f32[56,256]{1,0:T(8,128)S(1)} %fusion.2), channel_id=1, source_target_pairs={{0,16},{4,20},{8,24},{12,28},{16,0},{20,4},{24,8},{28,12},{1,17},{... | collective-permute-start | bytes 172040 | tf_op jit(solution)/shard_map/ppermute | solution.py:30
  121.7 1.2 collective-permute-start.46
  122.9 1.6 %collective-permute-done.48 = f32[56,256]{1,0:T(8,128)S(1)} collective-permute-done((f32[56,256]{1,0:T(8,128)S(1)}, f32[56,256]{1,0:T(8,128)S(1)}, u32[]{:S(2)}, u32[]{:S(2)}) %collective-permute-start.48) | collective-permute-done | bytes 57376 | tf_op jit(solution)/shard_map/ppermute | solution.py:30
  124.5 0.6 collective-permute-done.47
  125.1 0.8 collective-permute-done.46
  126.0 1.2 collective-permute-done.49.other_ref
  127.2 1.3 shard_map.155
  (61 shorter events, 3.1 us)
Async XLA Ops:
  0.6 22.5 %copy-start = (f32[32,1024]{1,0:T(8,128)S(1)}, f32[32,1024]{1,0:T(8,128)}, u32[]{:S(2)}) copy-start(f32[32,1024]{1,0:T(8,128)} %refs_0_) | copy-start | bytes 393220
  1.5 8.6 %collective-permute-start.5 = (f32[104,256]{1,0:T(8,128)S(1)}, f32[104,256]{1,0:T(8,128)S(1)}, u32[]{:S(2)}, u32[]{:S(2)}) collective-permute-start(f32[104,256]{1,0:T(8,128)S(1)} %pad_add_fusion.refs_4_), channel_id=1, source_target_pairs={{0,3},{1,2},{2,1},{3,0},{4,7},{5,6},{6,5},{7,4},{8,11},{9,10},{10,... | collective-permute-start | bytes 319496 | tf_op jit(solution)/shard_map/ppermute | solution.py:30
  6.7 16.4 %collective-permute-start.1 = (f32[32,1024]{1,0:T(8,128)}, f32[32,1024]{1,0:T(8,128)S(1)}, u32[]{:S(2)}, u32[]{:S(2)}) collective-permute-start(f32[32,1024]{1,0:T(8,128)} %refs_0_), channel_id=1, source_target_pairs={{0,16},{4,20},{8,24},{12,28},{16,0},{20,4},{24,8},{28,12},{1,17},{... | collective-permute-start | bytes 393224 | tf_op jit(solution)/shard_map/ppermute | solution.py:30
  8.2 14.9 %collective-permute-start = (f32[32,1024]{1,0:T(8,128)}, f32[32,1024]{1,0:T(8,128)S(1)}, u32[]{:S(2)}, u32[]{:S(2)}) collective-permute-start(f32[32,1024]{1,0:T(8,128)} %refs_0_), channel_id=1, source_target_pairs={{0,8},{4,12},{8,0},{12,4},{16,24},{20,28},{24,16},{28,20},{1,9},{5... | collective-permute-start | bytes 393224 | tf_op jit(solution)/shard_map/ppermute | solution.py:30
  9.7 13.4 %collective-permute-start.2 = (f32[32,1024]{1,0:T(8,128)}, f32[32,1024]{1,0:T(8,128)S(1)}, u32[]{:S(2)}, u32[]{:S(2)}) collective-permute-start(f32[32,1024]{1,0:T(8,128)} %refs_0_), channel_id=1, source_target_pairs={{0,24},{4,28},{8,16},{12,20},{16,8},{20,12},{24,0},{28,4},{1,25},{... | collective-permute-start | bytes 393224 | tf_op jit(solution)/shard_map/ppermute | solution.py:30
  10.1 12.9 %collective-permute-start.4 = (f32[104,256]{1,0:T(8,128)S(1)}, f32[104,256]{1,0:T(8,128)S(1)}, u32[]{:S(2)}, u32[]{:S(2)}) collective-permute-start(f32[104,256]{1,0:T(8,128)S(1)} %pad_add_fusion.refs_4_), channel_id=1, source_target_pairs={{0,2},{1,3},{2,0},{3,1},{4,6},{5,7},{6,4},{7,5},{8,10},{9,11},{10,... | collective-permute-start | bytes 319496 | tf_op jit(solution)/shard_map/ppermute | solution.py:30
  10.2 12.9 %collective-permute-start.3 = (f32[104,256]{1,0:T(8,128)S(1)}, f32[104,256]{1,0:T(8,128)S(1)}, u32[]{:S(2)}, u32[]{:S(2)}) collective-permute-start(f32[104,256]{1,0:T(8,128)S(1)} %pad_add_fusion.refs_4_), channel_id=1, source_target_pairs={{0,1},{1,0},{2,3},{3,2},{4,5},{5,4},{6,7},{7,6},{8,9},{9,8},{10,11... | collective-permute-start | bytes 319496 | tf_op jit(solution)/shard_map/ppermute | solution.py:30
  23.1 1.4 %collective-permute-start.6 = (f32[32,1024]{1,0:T(8,128)S(1)}, f32[32,1024]{1,0:T(8,128)S(1)}, u32[]{:S(2)}, u32[]{:S(2)}) collective-permute-start(f32[32,1024]{1,0:T(8,128)S(1)} %copy-done), channel_id=1, source_target_pairs={{0,4},{4,0},{8,12},{12,8},{16,20},{20,16},{24,28},{28,24},{1,5},{5... | collective-permute-start | bytes 393224 | tf_op jit(solution)/shard_map/ppermute | solution.py:30
  23.2 1.5 %collective-permute-start.7 = (f32[32,1024]{1,0:T(8,128)S(1)}, f32[32,1024]{1,0:T(8,128)S(1)}, u32[]{:S(2)}, u32[]{:S(2)}) collective-permute-start(f32[32,1024]{1,0:T(8,128)S(1)} %collective-permute-done.refs_2_), channel_id=1, source_target_pairs={{0,4},{4,0},{8,12},{12,8},{16,20},{20,16},{24,28},{28,24},{1,5},{5... | collective-permute-start | bytes 393224 | tf_op jit(solution)/shard_map/ppermute | solution.py:30
  23.7 1.3 %collective-permute-start.8 = (f32[32,1024]{1,0:T(8,128)S(1)}, f32[32,1024]{1,0:T(8,128)S(1)}, u32[]{:S(2)}, u32[]{:S(2)}) collective-permute-start(f32[32,1024]{1,0:T(8,128)S(1)} %collective-permute-done.1.refs_4_), channel_id=1, source_target_pairs={{0,4},{4,0},{8,12},{12,8},{16,20},{20,16},{24,28},{28,24},{1,5},{5... | collective-permute-start | bytes 393224 | tf_op jit(solution)/shard_map/ppermute | solution.py:30
  23.8 1.5 %collective-permute-start.9 = (f32[32,1024]{1,0:T(8,128)S(1)}, f32[32,1024]{1,0:T(8,128)S(1)}, u32[]{:S(2)}, u32[]{:S(2)}) collective-permute-start(f32[32,1024]{1,0:T(8,128)S(1)} %collective-permute-done.2.refs_6_), channel_id=1, source_target_pairs={{0,4},{4,0},{8,12},{12,8},{16,20},{20,16},{24,28},{28,24},{1,5},{5... | collective-permute-start | bytes 393224 | tf_op jit(solution)/shard_map/ppermute | solution.py:30
  31.1 4.5 %collective-permute-start.10 = (f32[32,256]{1,0:T(8,128)S(1)}, f32[32,256]{1,0:T(8,128)S(1)}, u32[]{:S(2)}, u32[]{:S(2)}) collective-permute-start(f32[32,256]{1,0:T(8,128)S(1)} %get-tuple-element.102), channel_id=1, source_target_pairs={{0,1},{1,0},{2,3},{3,2},{4,5},{5,4},{6,7},{7,6},{8,9},{9,8},{10,11... | collective-permute-start | bytes 98312 | tf_op jit(solution)/shard_map/ppermute | solution.py:30
  31.7 6.4 %collective-permute-start.11 = (f32[32,256]{1,0:T(8,128)S(1)}, f32[32,256]{1,0:T(8,128)S(1)}, u32[]{:S(2)}, u32[]{:S(2)}) collective-permute-start(f32[32,256]{1,0:T(8,128)S(1)} %get-tuple-element.103), channel_id=1, source_target_pairs={{0,2},{1,3},{2,0},{3,1},{4,6},{5,7},{6,4},{7,5},{8,10},{9,11},{10,... | collective-permute-start | bytes 98312 | tf_op jit(solution)/shard_map/ppermute | solution.py:30
  35.6 5.7 %collective-permute-start.12 = (f32[32,256]{1,0:T(8,128)S(1)}, f32[32,256]{1,0:T(8,128)S(1)}, u32[]{:S(2)}, u32[]{:S(2)}) collective-permute-start(f32[32,256]{1,0:T(8,128)S(1)} %get-tuple-element.104), channel_id=1, source_target_pairs={{0,3},{1,2},{2,1},{3,0},{4,7},{5,6},{6,5},{7,4},{8,11},{9,10},{10,... | collective-permute-start | bytes 98312 | tf_op jit(solution)/shard_map/ppermute | solution.py:30
  41.3 19.3 %copy-start.1 = (s32[1024]{0:T(1024)S(1)}, s32[1024]{0:T(1024)}, u32[]{:S(2)}) copy-start(s32[1024]{0:T(1024)} %param.14) | copy-start | bytes 12292
  41.3 19.3 %copy-start.3 = (f32[172]{0:T(256)S(1)}, f32[172]{0:T(256)}, u32[]{:S(2)}) copy-start(f32[172]{0:T(256)} %param.19) | copy-start | bytes 2068
  42.6 5.2 %collective-permute-start.13 = (f32[48,256]{1,0:T(8,128)S(1)}, f32[48,256]{1,0:T(8,128)S(1)}, u32[]{:S(2)}, u32[]{:S(2)}) collective-permute-start(f32[48,256]{1,0:T(8,128)S(1)} %get-tuple-element.110), channel_id=1, source_target_pairs={{0,1},{1,0},{2,3},{3,2},{4,5},{5,4},{6,7},{7,6},{8,9},{9,8},{10,11... | collective-permute-start | bytes 147464 | tf_op jit(solution)/shard_map/ppermute | solution.py:30
  42.7 5.1 %collective-permute-start.14 = (f32[48,256]{1,0:T(8,128)S(1)}, f32[48,256]{1,0:T(8,128)S(1)}, u32[]{:S(2)}, u32[]{:S(2)}) collective-permute-start(f32[48,256]{1,0:T(8,128)S(1)} %get-tuple-element.111), channel_id=1, source_target_pairs={{0,2},{1,3},{2,0},{3,1},{4,6},{5,7},{6,4},{7,5},{8,10},{9,11},{10,... | collective-permute-start | bytes 147464 | tf_op jit(solution)/shard_map/ppermute | solution.py:30
  43.7 6.0 %collective-permute-start.15 = (f32[48,256]{1,0:T(8,128)S(1)}, f32[48,256]{1,0:T(8,128)S(1)}, u32[]{:S(2)}, u32[]{:S(2)}) collective-permute-start(f32[48,256]{1,0:T(8,128)S(1)} %get-tuple-element.112), channel_id=1, source_target_pairs={{0,3},{1,2},{2,1},{3,0},{4,7},{5,6},{6,5},{7,4},{8,11},{9,10},{10,... | collective-permute-start | bytes 147464 | tf_op jit(solution)/shard_map/ppermute | solution.py:30
  49.7 26.0 %copy-start.2 = (s32[1024]{0:T(1024)S(1)}, s32[1024]{0:T(1024)}, u32[]{:S(2)}) copy-start(s32[1024]{0:T(1024)} %param.15) | copy-start | bytes 12292
  49.7 7.3 %collective-permute-start.21 = (f32[4,48,256]{2,1,0:T(8,128)S(1)}, f32[4,48,256]{2,1,0:T(8,128)S(1)}, u32[]{:S(2)}, u32[]{:S(2)}) collective-permute-start(f32[4,48,256]{2,1,0:T(8,128)S(1)} %shard_map.148.refs_0_), channel_id=1, source_target_pairs={{0,24},{4,28},{8,16},{12,20},{16,8},{20,12},{24,0},{28,4},{1,25},{... | collective-permute-start | bytes 589832 | tf_op jit(solution)/shard_map/ppermute | solution.py:30
  50.0 8.8 %collective-permute-start.19 = (f32[4,48,256]{2,1,0:T(8,128)S(1)}, f32[4,48,256]{2,1,0:T(8,128)S(1)}, u32[]{:S(2)}, u32[]{:S(2)}) collective-permute-start(f32[4,48,256]{2,1,0:T(8,128)S(1)} %shard_map.148.refs_0_), channel_id=1, source_target_pairs={{0,16},{4,20},{8,24},{12,28},{16,0},{20,4},{24,8},{28,12},{1,17},{... | collective-permute-start | bytes 589832 | tf_op jit(solution)/shard_map/ppermute | solution.py:30
  51.0 7.8 %collective-permute-start.17 = (f32[4,48,256]{2,1,0:T(8,128)S(1)}, f32[4,48,256]{2,1,0:T(8,128)S(1)}, u32[]{:S(2)}, u32[]{:S(2)}) collective-permute-start(f32[4,48,256]{2,1,0:T(8,128)S(1)} %shard_map.148.refs_0_), channel_id=1, source_target_pairs={{0,8},{4,12},{8,0},{12,4},{16,24},{20,28},{24,16},{28,20},{1,9},{5... | collective-permute-start | bytes 589832 | tf_op jit(solution)/shard_map/ppermute | solution.py:30
  53.2 6.1 %collective-permute-start.16 = (f32[4,48,256]{2,1,0:T(8,128)S(1)}, f32[4,48,256]{2,1,0:T(8,128)S(1)}, u32[]{:S(2)}, u32[]{:S(2)}) collective-permute-start(f32[4,48,256]{2,1,0:T(8,128)S(1)} %shard_map.148.refs_0_), channel_id=1, source_target_pairs={{0,4},{4,0},{8,12},{12,8},{16,20},{20,16},{24,28},{28,24},{1,5},{5... | collective-permute-start | bytes 589832 | tf_op jit(solution)/shard_map/ppermute | solution.py:30
  57.0 2.4 %collective-permute-start.22 = (f32[4,48,256]{2,1,0:T(8,128)S(1)}, f32[4,48,256]{2,1,0:T(8,128)S(1)}, u32[]{:S(2)}, u32[]{:S(2)}) collective-permute-start(f32[4,48,256]{2,1,0:T(8,128)S(1)} %collective-permute-done.21.refs_6_), channel_id=1, source_target_pairs={{0,4},{4,0},{8,12},{12,8},{16,20},{20,16},{24,28},{28,24},{1,5},{5... | collective-permute-start | bytes 589832 | tf_op jit(solution)/shard_map/ppermute | solution.py:30
  58.8 1.4 %collective-permute-start.20 = (f32[4,48,256]{2,1,0:T(8,128)S(1)}, f32[4,48,256]{2,1,0:T(8,128)S(1)}, u32[]{:S(2)}, u32[]{:S(2)}) collective-permute-start(f32[4,48,256]{2,1,0:T(8,128)S(1)} %collective-permute-done.19.refs_4_), channel_id=1, source_target_pairs={{0,4},{4,0},{8,12},{12,8},{16,20},{20,16},{24,28},{28,24},{1,5},{5... | collective-permute-start | bytes 589832 | tf_op jit(solution)/shard_map/ppermute | solution.py:30
  58.9 1.7 %collective-permute-start.18 = (f32[4,48,256]{2,1,0:T(8,128)S(1)}, f32[4,48,256]{2,1,0:T(8,128)S(1)}, u32[]{:S(2)}, u32[]{:S(2)}) collective-permute-start(f32[4,48,256]{2,1,0:T(8,128)S(1)} %collective-permute-done.17.refs_2_), channel_id=1, source_target_pairs={{0,4},{4,0},{8,12},{12,8},{16,20},{20,16},{24,28},{28,24},{1,5},{5... | collective-permute-start | bytes 589832 | tf_op jit(solution)/shard_map/ppermute | solution.py:30
  66.8 6.8 %collective-permute-start.25 = (f32[8,1024]{1,0:T(8,128)S(1)}, f32[8,1024]{1,0:T(8,128)S(1)}, u32[]{:S(2)}, u32[]{:S(2)}) collective-permute-start(f32[8,1024]{1,0:T(8,128)S(1)} %get-tuple-element.115.refs_0_), channel_id=1, source_target_pairs={{0,3},{1,2},{2,1},{3,0},{4,7},{5,6},{6,5},{7,4},{8,11},{9,10},{10,... | collective-permute-start | bytes 98312 | tf_op jit(solution)/shard_map/ppermute | solution.py:30
  69.2 6.4 %collective-permute-start.24 = (f32[8,1024]{1,0:T(8,128)S(1)}, f32[8,1024]{1,0:T(8,128)S(1)}, u32[]{:S(2)}, u32[]{:S(2)}) collective-permute-start(f32[8,1024]{1,0:T(8,128)S(1)} %get-tuple-element.115.refs_0_), channel_id=1, source_target_pairs={{0,2},{1,3},{2,0},{3,1},{4,6},{5,7},{6,4},{7,5},{8,10},{9,11},{10,... | collective-permute-start | bytes 98312 | tf_op jit(solution)/shard_map/ppermute | solution.py:30
  69.2 6.4 %collective-permute-start.23 = (f32[8,1024]{1,0:T(8,128)S(1)}, f32[8,1024]{1,0:T(8,128)S(1)}, u32[]{:S(2)}, u32[]{:S(2)}) collective-permute-start(f32[8,1024]{1,0:T(8,128)S(1)} %get-tuple-element.115.refs_0_), channel_id=1, source_target_pairs={{0,1},{1,0},{2,3},{3,2},{4,5},{5,4},{6,7},{7,6},{8,9},{9,8},{10,11... | collective-permute-start | bytes 98312 | tf_op jit(solution)/shard_map/ppermute | solution.py:30
  71.2 9.2 %collective-permute-start.28 = (f32[24,1024]{1,0:T(8,128)S(1)}, f32[24,1024]{1,0:T(8,128)S(1)}, u32[]{:S(2)}, u32[]{:S(2)}) collective-permute-start(f32[24,1024]{1,0:T(8,128)S(1)} %get-tuple-element.124.upper_ref.refs_0_), channel_id=1, source_target_pairs={{0,3},{1,2},{2,1},{3,0},{4,7},{5,6},{6,5},{7,4},{8,11},{9,10},{10,... | collective-permute-start | bytes 294920 | tf_op jit(solution)/shard_map/ppermute | solution.py:30
  73.6 8.5 %collective-permute-start.27 = (f32[24,1024]{1,0:T(8,128)S(1)}, f32[24,1024]{1,0:T(8,128)S(1)}, u32[]{:S(2)}, u32[]{:S(2)}) collective-permute-start(f32[24,1024]{1,0:T(8,128)S(1)} %get-tuple-element.124.upper_ref.refs_0_), channel_id=1, source_target_pairs={{0,2},{1,3},{2,0},{3,1},{4,6},{5,7},{6,4},{7,5},{8,10},{9,11},{10,... | collective-permute-start | bytes 294920 | tf_op jit(solution)/shard_map/ppermute | solution.py:30
  73.6 8.5 %collective-permute-start.26 = (f32[24,1024]{1,0:T(8,128)S(1)}, f32[24,1024]{1,0:T(8,128)S(1)}, u32[]{:S(2)}, u32[]{:S(2)}) collective-permute-start(f32[24,1024]{1,0:T(8,128)S(1)} %get-tuple-element.124.upper_ref.refs_0_), channel_id=1, source_target_pairs={{0,1},{1,0},{2,3},{3,2},{4,5},{5,4},{6,7},{7,6},{8,9},{9,8},{10,11... | collective-permute-start | bytes 294920 | tf_op jit(solution)/shard_map/ppermute | solution.py:30
  82.1 1.4 %collective-permute-start.29 = (f32[48,1024]{1,0:T(8,128)S(1)}, f32[48,1024]{1,0:T(8,128)S(1)}, u32[]{:S(2)}, u32[]{:S(2)}) collective-permute-start(f32[48,1024]{1,0:T(8,128)S(1)} %get-tuple-element.132), channel_id=1, source_target_pairs={{0,4},{4,0},{8,12},{12,8},{16,20},{20,16},{24,28},{28,24},{1,5},{5... | collective-permute-start | bytes 589832 | tf_op jit(solution)/shard_map/ppermute | solution.py:30
  82.1 1.7 %collective-permute-start.30 = (f32[48,1024]{1,0:T(8,128)S(1)}, f32[48,1024]{1,0:T(8,128)S(1)}, u32[]{:S(2)}, u32[]{:S(2)}) collective-permute-start(f32[48,1024]{1,0:T(8,128)S(1)} %get-tuple-element.133), channel_id=1, source_target_pairs={{0,4},{4,0},{8,12},{12,8},{16,20},{20,16},{24,28},{28,24},{1,5},{5... | collective-permute-start | bytes 589832 | tf_op jit(solution)/shard_map/ppermute | solution.py:30
  82.6 1.5 %collective-permute-start.31 = (f32[48,1024]{1,0:T(8,128)S(1)}, f32[48,1024]{1,0:T(8,128)S(1)}, u32[]{:S(2)}, u32[]{:S(2)}) collective-permute-start(f32[48,1024]{1,0:T(8,128)S(1)} %get-tuple-element.134), channel_id=1, source_target_pairs={{0,4},{4,0},{8,12},{12,8},{16,20},{20,16},{24,28},{28,24},{1,5},{5... | collective-permute-start | bytes 589832 | tf_op jit(solution)/shard_map/ppermute | solution.py:30
  82.6 1.8 %collective-permute-start.32 = (f32[48,1024]{1,0:T(8,128)S(1)}, f32[48,1024]{1,0:T(8,128)S(1)}, u32[]{:S(2)}, u32[]{:S(2)}) collective-permute-start(f32[48,1024]{1,0:T(8,128)S(1)} %get-tuple-element.135), channel_id=1, source_target_pairs={{0,4},{4,0},{8,12},{12,8},{16,20},{20,16},{24,28},{28,24},{1,5},{5... | collective-permute-start | bytes 589832 | tf_op jit(solution)/shard_map/ppermute | solution.py:30
  84.4 7.8 %collective-permute-start.33 = (f32[48,1024]{1,0:T(8,128)S(1)}, f32[48,1024]{1,0:T(8,128)S(1)}, u32[]{:S(2)}, u32[]{:S(2)}) collective-permute-start(f32[48,1024]{1,0:T(8,128)S(1)} %get-tuple-element.141), channel_id=1, source_target_pairs={{0,8},{4,12},{8,0},{12,4},{16,24},{20,28},{24,16},{28,20},{1,9},{5... | collective-permute-start | bytes 589832 | tf_op jit(solution)/shard_map/ppermute | solution.py:30
  85.4 11.0 %collective-permute-start.34 = (f32[48,1024]{1,0:T(8,128)S(1)}, f32[48,1024]{1,0:T(8,128)S(1)}, u32[]{:S(2)}, u32[]{:S(2)}) collective-permute-start(f32[48,1024]{1,0:T(8,128)S(1)} %get-tuple-element.142), channel_id=1, source_target_pairs={{0,16},{4,20},{8,24},{12,28},{16,0},{20,4},{24,8},{28,12},{1,17},{... | collective-permute-start | bytes 589832 | tf_op jit(solution)/shard_map/ppermute | solution.py:30
  86.0 10.5 %collective-permute-start.35 = (f32[48,1024]{1,0:T(8,128)S(1)}, f32[48,1024]{1,0:T(8,128)S(1)}, u32[]{:S(2)}, u32[]{:S(2)}) collective-permute-start(f32[48,1024]{1,0:T(8,128)S(1)} %get-tuple-element.143), channel_id=1, source_target_pairs={{0,24},{4,28},{8,16},{12,20},{16,8},{20,12},{24,0},{28,4},{1,25},{... | collective-permute-start | bytes 589832 | tf_op jit(solution)/shard_map/ppermute | solution.py:30
  88.0 9.0 %collective-permute-start.38 = (f32[24,1024]{1,0:T(8,128)S(1)}, f32[24,1024]{1,0:T(8,128)S(1)}, u32[]{:S(2)}, u32[]{:S(2)}) collective-permute-start(f32[24,1024]{1,0:T(8,128)S(1)} %get-tuple-element.149.lower_ref.refs_4_), channel_id=1, source_target_pairs={{0,3},{1,2},{2,1},{3,0},{4,7},{5,6},{6,5},{7,4},{8,11},{9,10},{10,... | collective-permute-start | bytes 294920 | tf_op jit(solution)/shard_map/ppermute | solution.py:30
  90.3 8.1 %collective-permute-start.37 = (f32[24,1024]{1,0:T(8,128)S(1)}, f32[24,1024]{1,0:T(8,128)S(1)}, u32[]{:S(2)}, u32[]{:S(2)}) collective-permute-start(f32[24,1024]{1,0:T(8,128)S(1)} %get-tuple-element.149.lower_ref.refs_4_), channel_id=1, source_target_pairs={{0,2},{1,3},{2,0},{3,1},{4,6},{5,7},{6,4},{7,5},{8,10},{9,11},{10,... | collective-permute-start | bytes 294920 | tf_op jit(solution)/shard_map/ppermute | solution.py:30
  92.2 6.5 %collective-permute-start.36 = (f32[24,1024]{1,0:T(8,128)S(1)}, f32[24,1024]{1,0:T(8,128)S(1)}, u32[]{:S(2)}, u32[]{:S(2)}) collective-permute-start(f32[24,1024]{1,0:T(8,128)S(1)} %get-tuple-element.149.lower_ref.refs_4_), channel_id=1, source_target_pairs={{0,1},{1,0},{2,3},{3,2},{4,5},{5,4},{6,7},{7,6},{8,9},{9,8},{10,11... | collective-permute-start | bytes 294920 | tf_op jit(solution)/shard_map/ppermute | solution.py:30
  98.8 5.9 %collective-permute-start.39 = (f32[48,256]{1,0:T(8,128)S(1)}, f32[48,256]{1,0:T(8,128)S(1)}, u32[]{:S(2)}, u32[]{:S(2)}) collective-permute-start(f32[48,256]{1,0:T(8,128)S(1)} %get-tuple-element.154), channel_id=1, source_target_pairs={{0,1},{1,0},{2,3},{3,2},{4,5},{5,4},{6,7},{7,6},{8,9},{9,8},{10,11... | collective-permute-start | bytes 147464 | tf_op jit(solution)/shard_map/ppermute | solution.py:30
  98.8 5.9 %collective-permute-start.40 = (f32[48,256]{1,0:T(8,128)S(1)}, f32[48,256]{1,0:T(8,128)S(1)}, u32[]{:S(2)}, u32[]{:S(2)}) collective-permute-start(f32[48,256]{1,0:T(8,128)S(1)} %get-tuple-element.155), channel_id=1, source_target_pairs={{0,2},{1,3},{2,0},{3,1},{4,6},{5,7},{6,4},{7,5},{8,10},{9,11},{10,... | collective-permute-start | bytes 147464 | tf_op jit(solution)/shard_map/ppermute | solution.py:30
  101.6 5.9 %collective-permute-start.41 = (f32[48,256]{1,0:T(8,128)S(1)}, f32[48,256]{1,0:T(8,128)S(1)}, u32[]{:S(2)}, u32[]{:S(2)}) collective-permute-start(f32[48,256]{1,0:T(8,128)S(1)} %get-tuple-element.156), channel_id=1, source_target_pairs={{0,3},{1,2},{2,1},{3,0},{4,7},{5,6},{6,5},{7,4},{8,11},{9,10},{10,... | collective-permute-start | bytes 147464 | tf_op jit(solution)/shard_map/ppermute | solution.py:30
  108.7 1.6 %collective-permute-start.42 = (f32[4,56,256]{2,1,0:T(8,128)S(1)}, f32[4,56,256]{2,1,0:T(8,128)S(1)}, u32[]{:S(2)}, u32[]{:S(2)}) collective-permute-start(f32[4,56,256]{2,1,0:T(8,128)S(1)} %get-tuple-element.168), channel_id=1, source_target_pairs={{0,4},{4,0},{8,12},{12,8},{16,20},{20,16},{24,28},{28,24},{1,5},{5... | collective-permute-start | bytes 688136 | tf_op jit(solution)/shard_map/ppermute | solution.py:30
  110.3 4.2 %collective-permute-start.43 = (f32[56,256]{1,0:T(8,128)S(1)}, f32[56,256]{1,0:T(8,128)S(1)}, u32[]{:S(2)}, u32[]{:S(2)}) collective-permute-start(f32[56,256]{1,0:T(8,128)S(1)} %get-tuple-element.174), channel_id=1, source_target_pairs={{0,1},{1,0},{2,3},{3,2},{4,5},{5,4},{6,7},{7,6},{8,9},{9,8},{10,11... | collective-permute-start | bytes 172040 | tf_op jit(solution)/shard_map/ppermute | solution.py:30
  110.4 6.5 %collective-permute-start.45 = (f32[56,256]{1,0:T(8,128)S(1)}, f32[56,256]{1,0:T(8,128)S(1)}, u32[]{:S(2)}, u32[]{:S(2)}) collective-permute-start(f32[56,256]{1,0:T(8,128)S(1)} %get-tuple-element.175), channel_id=1, source_target_pairs={{0,3},{1,2},{2,1},{3,0},{4,7},{5,6},{6,5},{7,4},{8,11},{9,10},{10,... | collective-permute-start | bytes 172040 | tf_op jit(solution)/shard_map/ppermute | solution.py:30
  112.1 7.2 %collective-permute-start.44 = (f32[56,256]{1,0:T(8,128)S(1)}, f32[56,256]{1,0:T(8,128)S(1)}, u32[]{:S(2)}, u32[]{:S(2)}) collective-permute-start(f32[56,256]{1,0:T(8,128)S(1)} %get-tuple-element.176), channel_id=1, source_target_pairs={{0,2},{1,3},{2,0},{3,1},{4,6},{5,7},{6,4},{7,5},{8,10},{9,11},{10,... | collective-permute-start | bytes 172040 | tf_op jit(solution)/shard_map/ppermute | solution.py:30
  119.3 5.2 %collective-permute-start.48 = (f32[56,256]{1,0:T(8,128)S(1)}, f32[56,256]{1,0:T(8,128)S(1)}, u32[]{:S(2)}, u32[]{:S(2)}) collective-permute-start(f32[56,256]{1,0:T(8,128)S(1)} %fusion.2), channel_id=1, source_target_pairs={{0,24},{4,28},{8,16},{12,20},{16,8},{20,12},{24,0},{28,4},{1,25},{... | collective-permute-start | bytes 172040 | tf_op jit(solution)/shard_map/ppermute | solution.py:30
  120.3 4.7 %collective-permute-start.47 = (f32[56,256]{1,0:T(8,128)S(1)}, f32[56,256]{1,0:T(8,128)S(1)}, u32[]{:S(2)}, u32[]{:S(2)}) collective-permute-start(f32[56,256]{1,0:T(8,128)S(1)} %fusion.2), channel_id=1, source_target_pairs={{0,16},{4,20},{8,24},{12,28},{16,0},{20,4},{24,8},{28,12},{1,17},{... | collective-permute-start | bytes 172040 | tf_op jit(solution)/shard_map/ppermute | solution.py:30
  121.7 4.2 %collective-permute-start.46 = (f32[56,256]{1,0:T(8,128)S(1)}, f32[56,256]{1,0:T(8,128)S(1)}, u32[]{:S(2)}, u32[]{:S(2)}) collective-permute-start(f32[56,256]{1,0:T(8,128)S(1)} %fusion.2), channel_id=1, source_target_pairs={{0,8},{4,12},{8,0},{12,4},{16,24},{20,28},{24,16},{28,20},{1,9},{5... | collective-permute-start | bytes 172040 | tf_op jit(solution)/shard_map/ppermute | solution.py:30
  125.9 1.3 %collective-permute-start.49 = (f32[56,256]{1,0:T(8,128)S(1)}, f32[56,256]{1,0:T(8,128)S(1)}, u32[]{:S(2)}, u32[]{:S(2)}) collective-permute-start(f32[56,256]{1,0:T(8,128)S(1)} %add_add_fusion.mine_ref), channel_id=1, source_target_pairs={{0,4},{4,0},{8,12},{12,8},{16,20},{20,16},{24,28},{28,24},{1,5},{5... | collective-permute-start | bytes 172040 | tf_op jit(solution)/shard_map/ppermute | solution.py:30

commit v4 on v3

--- a/solution.py
+++ b/solution.py
@@ -9,8 +9,7 @@
 
 BLOCK = 128
 CHUNK = 4
-UNROLL = 4
-FETCH = 4
+UNROLL = 8
 DEPTH = 3
 PAD = 48
 HALF = 24
@@ -88,16 +87,20 @@
 
     def copies(row, act):
         ring = lax.rem(row, DEPTH)
-
-        def one(group, _):
-            part = pl.ds(group * FETCH, FETCH)
-            copy = pltpu.make_async_copy(
-                tiles_ref.at[row, part], land.at[pl.ds(ring * slots + group * FETCH, FETCH)], sem.at[ring, group]
-            )
-            act(copy)
-            return 0
-
-        lax.fori_loop(0, (count_ref[row] + FETCH - 1) // FETCH, one, 0)
+        live = count_ref[row]
+        for power in range(slots.bit_length()):
+            size = 1 << power
+
+            @pl.when(live & size != 0)
+            def _():
+                first = live & ~(2 * size - 1)
+                act(
+                    pltpu.make_async_copy(
+                        tiles_ref.at[row, pl.ds(first, size)],
+                        land.at[pl.ds(ring * slots + first, size)],
+                        sem.at[ring, power],
+                    )
+                )
 
     def start(copy):
         copy.start()
@@ -124,18 +127,11 @@
             column = column_ref[row, slot]
             at = place[column]
             fresh = at < stamp
-
-            @pl.when(fresh)
-            def _():
-                place[column] = stamp + slot
-                owner[found] = stamp - shift + slot
-                list_ref[begin * CHUNK + found] = column
-
-            @pl.when(jnp.logical_not(fresh))
-            def _():
-                twin_from[twins] = stamp - shift + slot
-                twin_to[twins] = at - shift
-
+            place[column] = jnp.where(fresh, stamp + slot, at)
+            owner[found] = stamp - shift + slot
+            list_ref[begin * CHUNK + found] = column
+            twin_from[twins] = stamp - shift + slot
+            twin_to[twins] = at - shift
             step = fresh.astype(jnp.int32)
             return found + step, twins + 1 - step
 
@@ -209,7 +205,7 @@
             pltpu.SMEM((slots,), jnp.int32),
             pltpu.SMEM((slots,), jnp.int32),
             pltpu.SMEM((slots,), jnp.int32),
-            pltpu.SemaphoreType.DMA((DEPTH, slots // FETCH)),
+            pltpu.SemaphoreType.DMA((DEPTH, slots.bit_length())),
             pltpu.SemaphoreType.DMA((2,)),
         ],
         pltpu.with_memory_space_constraint(tile_count, pltpu.HBM),
@@ -444,20 +440,23 @@
     for offset in range(cols):
         held[col ^ offset] = pieces[offset][...]
     spread = jnp.concatenate([held[group, :per] for group in range(cols)], axis=0)
-    classes = spread.shape[0]
     hidden_grad = product(weight_out_ref[...], spread, ((1,), (0,)))
     inner_grad = hidden_grad * slope_ref[...]
     weight_in = product(mixed_ref[...], inner_grad, ((1,), (1,)))
-    weight_out = product(hidden_ref[...], spread, ((1,), (1,)))
-    bias_in = jnp.sum(inner_grad, axis=1, keepdims=True)
-    feats, units = weight_in.shape[0] // cols, weight_out.shape[0] // cols
-    packed[...] = jnp.zeros_like(packed)
+    weight_out = product(spread, hidden_ref[...], ((1,), (1,)))
+    bias_in = as_row(jnp.sum(inner_grad, axis=1, keepdims=True))
+    feats, units = weight_in.shape[0] // cols, weight_out.shape[1] // cols
+    extra = extra_ref[: cols + 1]
+    line = lax.broadcasted_iota(jnp.int32, extra.shape, 0)
     for group in range(cols):
-        packed[group, :feats] = weight_in[group * feats : (group + 1) * feats]
-        rows = slice(group * units, (group + 1) * units)
-        packed[group, feats : feats + units, :classes] = weight_out[rows]
-        packed[group, feats : feats + units, classes : classes + 1] = bias_in[rows]
-        packed[group, feats + units : feats + units + 8] = extra_ref[...]
+        mine = slice(group * units, (group + 1) * units)
+        folded = jnp.concatenate([weight_out[q * per : (q + 1) * per, mine] for q in range(cols)], axis=1)
+        spare = jnp.zeros((1, BLOCK), f32)
+        bias = jnp.concatenate([spare, bias_in[:, mine], spare[:, : BLOCK - units]], axis=1)
+        packed[group] = jnp.concatenate(
+            [weight_in[group * feats : (group + 1) * feats], folded, jnp.where(line == cols, extra + bias, extra)],
+            axis=0,
+        )
     half = packed.shape[1] // 2
     for offset in range(cols):
         keep_ref[offset] = packed[col ^ offset, pl.ds(pl.multiple_of(core * half, 8), half)]
@@ -472,9 +471,11 @@
     value = whole[...].reshape(2 * half, mine_ref.shape[1])
     feats, (units, classes) = weight_in_ref.shape[0], weight_out_ref.shape
     weight_in_ref[...] = value[:feats]
-    weight_out_ref[...] = value[feats : feats + units, :classes]
-    bias_in_ref[...] = as_row(value[feats : feats + units, classes : classes + 1])
-    extra = value[feats + units : feats + units + 8]
+    folded = value[feats : feats + per]
+    spread = jnp.concatenate([folded[:, q * units : (q + 1) * units] for q in range(cols)], axis=0)
+    weight_out_ref[...] = spread.T
+    extra = value[feats + per : feats + per + cols + 1]
+    bias_in_ref[...] = extra[cols : cols + 1, BLOCK : BLOCK + units]
     bias_out_ref[...] = jnp.concatenate([extra[group : group + 1, :per] for group in range(cols)], axis=1)
     loss_ref[...] = extra[cols : cols + 1, 0:1] / jnp.maximum(extra[cols : cols + 1, 1:2], 1.0)
 
@@ -653,7 +654,7 @@
     )
     logits, *spread_pieces = lax.optimization_barrier((logits, *spread_pieces))
 
-    height = -(-(feats + units // cols + 8) // 16) * 16
+    height = feats + per + cols + 1
     keep, send = call(
         functools.partial(grads_body, cols, per),
         [shape((cols, height // 2, units), f32)] * 2,

time: 129 us -> 126 us (0.977)
  Pallas kernels: 34.3 us -> 32 us
    pallas_call x11, Pallas kernels: 34.3 us -> 32 us  [call(): pl.pallas_call(body, out_shape=outs, in_specs=specs or [VMEM] * len(args)...]
  transfers between devices with their start and end apart: 50 -> 50, of which waited for: 30 -> 29; matrix products, arithmetic and copies ran while one was open for 0% -> 0% of each run, Pallas kernels for 14% -> 14%
where the time goes in v4:
time: 126 us
  starting transfers between devices  51.6 us (41%)
  waiting for transfers between devices  40.5 us (32%)
  Pallas kernels  32 us (25%)
    ppermute x50, starting transfers between devices, exchange(): return lax.ppermute(value, axis, [(i, i ^ offset) for i in range(total)])  51.6 us
    ppermute x50, waiting for transfers between devices, exchange(): return lax.ppermute(value, axis, [(i, i ^ offset) for i in range(total)])  40.5 us
    pallas_call x11, Pallas kernels, call(): pl.pallas_call(body, out_shape=outs, in_specs=specs or [VMEM] * len(args)...  32 us
  transfers between devices with their start and end apart: 50, of which 29 were waited for; matrix products, arithmetic and copies ran while one was open for 0% of the time, Pallas kernels for 14%

profile of v4, /device:TPU:0, one launch (start us, length us, event | category | flops | bytes accessed | tf_op | source)
XLA Modules:
  0.0 126.0 jit_solution(6678696830180063295)
XLA Ops:
  0.6 0.9 pad_add_fusion.refs_4_
  1.5 5.1 %collective-permute-start.5 = (f32[104,256]{1,0:T(8,128)S(1)}, f32[104,256]{1,0:T(8,128)S(1)}, u32[]{:S(2)}, u32[]{:S(2)}) collective-permute-start(f32[104,256]{1,0:T(8,128)S(1)} %pad_add_fusion.refs_4_), channel_id=1, source_target_pairs={{0,3},{1,2},{2,1},{3,0},{4,7},{5,6},{6,5},{7,4},{8,11},{9,10},{10,... | collective-permute-start | bytes 319496 | tf_op jit(solution)/shard_map/ppermute | solution.py:29
  6.7 1.5 %collective-permute-start.1 = (f32[32,1024]{1,0:T(8,128)}, f32[32,1024]{1,0:T(8,128)S(1)}, u32[]{:S(2)}, u32[]{:S(2)}) collective-permute-start(f32[32,1024]{1,0:T(8,128)} %refs_0_), channel_id=1, source_target_pairs={{0,16},{4,20},{8,24},{12,28},{16,0},{20,4},{24,8},{28,12},{1,17},{... | collective-permute-start | bytes 393224 | tf_op jit(solution)/shard_map/ppermute | solution.py:29
  8.2 1.5 %collective-permute-start = (f32[32,1024]{1,0:T(8,128)}, f32[32,1024]{1,0:T(8,128)S(1)}, u32[]{:S(2)}, u32[]{:S(2)}) collective-permute-start(f32[32,1024]{1,0:T(8,128)} %refs_0_), channel_id=1, source_target_pairs={{0,8},{4,12},{8,0},{12,4},{16,24},{20,28},{24,16},{28,20},{1,9},{5... | collective-permute-start | bytes 393224 | tf_op jit(solution)/shard_map/ppermute | solution.py:29
  9.7 0.5 collective-permute-start.2
  10.2 1.5 %collective-permute-start.3 = (f32[104,256]{1,0:T(8,128)S(1)}, f32[104,256]{1,0:T(8,128)S(1)}, u32[]{:S(2)}, u32[]{:S(2)}) collective-permute-start(f32[104,256]{1,0:T(8,128)S(1)} %pad_add_fusion.refs_4_), channel_id=1, source_target_pairs={{0,1},{1,0},{2,3},{3,2},{4,5},{5,4},{6,7},{7,6},{8,9},{9,8},{10,11... | collective-permute-start | bytes 319496 | tf_op jit(solution)/shard_map/ppermute | solution.py:29
  11.7 11.0 %shard_map.145 = (bf16[128,256,512]{2,1,0:T(8,128)(2,1)S(1)}, s32[512]{0:T(512)S(1)}, s32[128]{0:T(128)S(1)}, s32[1]{0:T(128)}) custom-call(s32[8]{0:T(128)} %count_in, s32[8,64]{1,0:T(8,128)} %column_in.1, f32[8,64,128,128]{3,2,1,0:T(8,128)} %tiles_ref.1), custom_call_target="tpu_custom_call" | custom-call | flops 100000000 | bytes 41943040 | tf_op jit(solution)/shard_map/pallas_call | solution.py:49
  22.8 0.5 collective-permute-start.7
  23.4 0.4 collective-permute-start.9
  23.8 0.3 collective-permute-done.6.refs_1_
  24.3 0.3 collective-permute-done.8.refs_5_
  24.9 5.2 %shard_map.146 = (f32[32,256]{1,0:T(8,128)S(1)}, f32[32,256]{1,0:T(8,128)S(1)}, f32[32,256]{1,0:T(8,128)S(1)}, f32[32,256]{1,0:T(8,128)S(1)}) custom-call(s32[2]{0:T(128)S(1)} %pad_add_fusion.1.ids_ref, s32[1]{0:T(128)} %get-tuple-element.93.total_ref, s32[512]{0:T(512)S(1)} %get-tuple-element.94.list_ref, s32[128]{0:T(128)S(1)} %get-tuple-element.95.row_ref, ...), custom_call_target="tpu_custom_call" | custom-call | flops 1000000000 | bytes 16777216 | tf_op jit(solution)/shard_map/pallas_call | solution.py:49
  30.1 0.6 collective-permute-start.10
  30.7 3.8 %collective-permute-start.11 = (f32[32,256]{1,0:T(8,128)S(1)}, f32[32,256]{1,0:T(8,128)S(1)}, u32[]{:S(2)}, u32[]{:S(2)}) collective-permute-start(f32[32,256]{1,0:T(8,128)S(1)} %get-tuple-element.103), channel_id=1, source_target_pairs={{0,2},{1,3},{2,0},{3,1},{4,6},{5,7},{6,4},{7,5},{8,10},{9,11},{10,... | collective-permute-start | bytes 98312 | tf_op jit(solution)/shard_map/ppermute | solution.py:29
  34.5 2.5 %collective-permute-done.11.refs_2_ = f32[32,256]{1,0:T(8,128)S(1)} collective-permute-done((f32[32,256]{1,0:T(8,128)S(1)}, f32[32,256]{1,0:T(8,128)S(1)}, u32[]{:S(2)}, u32[]{:S(2)}) %collective-permute-start.11) | collective-permute-done | bytes 32800 | tf_op jit(solution)/shard_map/ppermute | solution.py:29
  37.1 3.2 %collective-permute-done.12.refs_3_ = f32[32,256]{1,0:T(8,128)S(1)} collective-permute-done((f32[32,256]{1,0:T(8,128)S(1)}, f32[32,256]{1,0:T(8,128)S(1)}, u32[]{:S(2)}, u32[]{:S(2)}) %collective-permute-start.12) | collective-permute-done | bytes 32800 | tf_op jit(solution)/shard_map/ppermute | solution.py:29
  40.2 1.3 %shard_map.147 = (f32[128,256]{1,0:T(8,128)S(1)}, f32[256,256]{1,0:T(8,128)S(1)}, f32[256,256]{1,0:T(8,128)S(1)}, f32[256,172]{1,0:T(8,128)S(1)}, f32[48,256]{1,...) custom-call(s32[2]{0:T(128)S(1)} %pad_add_fusion.1.ids_ref, ...), custom_call_target="tpu_custom_call" | custom-call | flops 100000000 | bytes 2097152 | tf_op jit(solution)/shard_map/pallas_call | solution.py:49
  41.7 1.0 collective-permute-start.14
  42.6 3.4 %collective-permute-start.15 = (f32[48,256]{1,0:T(8,128)S(1)}, f32[48,256]{1,0:T(8,128)S(1)}, u32[]{:S(2)}, u32[]{:S(2)}) collective-permute-start(f32[48,256]{1,0:T(8,128)S(1)} %get-tuple-element.112), channel_id=1, source_target_pairs={{0,3},{1,2},{2,1},{3,0},{4,7},{5,6},{6,5},{7,4},{8,11},{9,10},{10,... | collective-permute-start | bytes 147464 | tf_op jit(solution)/shard_map/ppermute | solution.py:29
  46.0 0.8 collective-permute-done.13.refs_1_
  46.8 1.8 %collective-permute-done.15.refs_3_ = f32[48,256]{1,0:T(8,128)S(1)} collective-permute-done((f32[48,256]{1,0:T(8,128)S(1)}, f32[48,256]{1,0:T(8,128)S(1)}, u32[]{:S(2)}, u32[]{:S(2)}) %collective-permute-start.15) | collective-permute-done | bytes 49184 | tf_op jit(solution)/shard_map/ppermute | solution.py:29
  48.6 1.5 %collective-permute-start.21 = (f32[4,48,256]{2,1,0:T(8,128)S(1)}, f32[4,48,256]{2,1,0:T(8,128)S(1)}, u32[]{:S(2)}, u32[]{:S(2)}) collective-permute-start(f32[4,48,256]{2,1,0:T(8,128)S(1)} %shard_map.148.refs_0_), channel_id=1, source_target_pairs={{0,24},{4,28},{8,16},{12,20},{16,8},{20,12},{24,0},{28,4},{1,25},{... | collective-permute-start | bytes 589832 | tf_op jit(solution)/shard_map/ppermute | solution.py:29
  50.3 1.9 %collective-permute-start.17 = (f32[4,48,256]{2,1,0:T(8,128)S(1)}, f32[4,48,256]{2,1,0:T(8,128)S(1)}, u32[]{:S(2)}, u32[]{:S(2)}) collective-permute-start(f32[4,48,256]{2,1,0:T(8,128)S(1)} %shard_map.148.refs_0_), channel_id=1, source_target_pairs={{0,8},{4,12},{8,0},{12,4},{16,24},{20,28},{24,16},{28,20},{1,9},{5... | collective-permute-start | bytes 589832 | tf_op jit(solution)/shard_map/ppermute | solution.py:29
  52.2 4.1 %collective-permute-done.21.refs_6_ = f32[4,48,256]{2,1,0:T(8,128)S(1)} collective-permute-done((f32[4,48,256]{2,1,0:T(8,128)S(1)}, f32[4,48,256]{2,1,0:T(8,128)S(1)}, u32[]{:S(2)}, u32[]{:S(2)}) %collective-permute-start.21) | collective-permute-done | bytes 196640 | tf_op jit(solution)/shard_map/ppermute | solution.py:29
  56.3 1.6 %collective-permute-done.19.refs_4_ = f32[4,48,256]{2,1,0:T(8,128)S(1)} collective-permute-done((f32[4,48,256]{2,1,0:T(8,128)S(1)}, f32[4,48,256]{2,1,0:T(8,128)S(1)}, u32[]{:S(2)}, u32[]{:S(2)}) %collective-permute-start.19) | collective-permute-done | bytes 196640 | tf_op jit(solution)/shard_map/ppermute | solution.py:29
  57.9 0.5 collective-permute-start.18
  58.5 0.9 collective-permute-done.20.refs_5_
  59.7 5.5 %shard_map.149 = (f32[24,1024]{1,0:T(8,128)S(1)}, f32[24,1024]{1,0:T(8,128)S(1)}, f32[8,1024]{1,0:T(8,128)S(1)}) custom-call(s32[2]{0:T(128)S(1)} %pad_add_fusion.1.ids_ref, s32[1]{0:T(128)} %get-tuple-element.93.total_ref, s32[512]{0:T(512)S(1)} %get-tuple-element.94.list_ref, s32[128]{0:T(128)S(1)} %get-tuple-element.95.row_ref, ...), custom_call_target="tpu_custom_call" | custom-call | flops 1000000000 | bytes 16777216 | tf_op jit(solution)/shard_map/pallas_call | solution.py:49
  65.2 3.1 %collective-permute-start.25 = (f32[8,1024]{1,0:T(8,128)S(1)}, f32[8,1024]{1,0:T(8,128)S(1)}, u32[]{:S(2)}, u32[]{:S(2)}) collective-permute-start(f32[8,1024]{1,0:T(8,128)S(1)} %get-tuple-element.115.refs_0_), channel_id=1, source_target_pairs={{0,3},{1,2},{2,1},{3,0},{4,7},{5,6},{6,5},{7,4},{8,11},{9,10},{10,... | collective-permute-start | bytes 98312 | tf_op jit(solution)/shard_map/ppermute | solution.py:29
  68.3 1.3 %collective-permute-start.23 = (f32[8,1024]{1,0:T(8,128)S(1)}, f32[8,1024]{1,0:T(8,128)S(1)}, u32[]{:S(2)}, u32[]{:S(2)}) collective-permute-start(f32[8,1024]{1,0:T(8,128)S(1)} %get-tuple-element.115.refs_0_), channel_id=1, source_target_pairs={{0,1},{1,0},{2,3},{3,2},{4,5},{5,4},{6,7},{7,6},{8,9},{9,8},{10,11... | collective-permute-start | bytes 98312 | tf_op jit(solution)/shard_map/ppermute | solution.py:29
  69.6 3.0 %collective-permute-start.28 = (f32[24,1024]{1,0:T(8,128)S(1)}, f32[24,1024]{1,0:T(8,128)S(1)}, u32[]{:S(2)}, u32[]{:S(2)}) collective-permute-start(f32[24,1024]{1,0:T(8,128)S(1)} %get-tuple-element.124.upper_ref.refs_0_), channel_id=1, source_target_pairs={{0,3},{1,2},{2,1},{3,0},{4,7},{5,6},{6,5},{7,4},{8,11},{9,10},{10,... | collective-permute-start | bytes 294920 | tf_op jit(solution)/shard_map/ppermute | solution.py:29
  72.7 1.4 %collective-permute-start.26 = (f32[24,1024]{1,0:T(8,128)S(1)}, f32[24,1024]{1,0:T(8,128)S(1)}, u32[]{:S(2)}, u32[]{:S(2)}) collective-permute-start(f32[24,1024]{1,0:T(8,128)S(1)} %get-tuple-element.124.upper_ref.refs_0_), channel_id=1, source_target_pairs={{0,1},{1,0},{2,3},{3,2},{4,5},{5,4},{6,7},{7,6},{8,9},{9,8},{10,11... | collective-permute-start | bytes 294920 | tf_op jit(solution)/shard_map/ppermute | solution.py:29
  74.0 4.1 %shard_map.150 = (f32[48,1024]{1,0:T(8,128)S(1)}, f32[48,1024]{1,0:T(8,128)S(1)}, f32[48,1024]{1,0:T(8,128)S(1)}, f32[48,1024]{1,0:T(8,128)S(1)}, f32[48,1024]{1...) custom-call(s32[2]{0:T(128)S(1)} %pad_add_fusion.1.ids_ref, ...), custom_call_target="tpu_custom_call" | custom-call | flops 1000000000 | bytes 16777216 | tf_op jit(solution)/shard_map/pallas_call | solution.py:49
  78.1 2.7 %collective-permute-done.27.refs_2_ = f32[24,1024]{1,0:T(8,128)S(1)} collective-permute-done((f32[24,1024]{1,0:T(8,128)S(1)}, f32[24,1024]{1,0:T(8,128)S(1)}, u32[]{:S(2)}, u32[]{:S(2)}) %collective-permute-start.27) | collective-permute-done | bytes 98336 | tf_op jit(solution)/shard_map/ppermute | solution.py:29
  80.9 0.5 collective-permute-start.30
  81.4 0.5 collective-permute-start.32
  81.9 0.4 collective-permute-done.29.refs_4_
  82.3 0.3 collective-permute-done.30.refs_5_
  82.9 0.3 collective-permute-done.32.refs_7_
  83.2 1.0 collective-permute-start.33
  84.2 2.1 %collective-permute-start.34 = (f32[48,1024]{1,0:T(8,128)S(1)}, f32[48,1024]{1,0:T(8,128)S(1)}, u32[]{:S(2)}, u32[]{:S(2)}) collective-permute-start(f32[48,1024]{1,0:T(8,128)S(1)} %get-tuple-element.142), channel_id=1, source_target_pairs={{0,16},{4,20},{8,24},{12,28},{16,0},{20,4},{24,8},{28,12},{1,17},{... | collective-permute-start | bytes 589832 | tf_op jit(solution)/shard_map/ppermute | solution.py:29
  86.3 0.5 collective-permute-start.35
  86.8 2.3 %collective-permute-start.38 = (f32[24,1024]{1,0:T(8,128)S(1)}, f32[24,1024]{1,0:T(8,128)S(1)}, u32[]{:S(2)}, u32[]{:S(2)}) collective-permute-start(f32[24,1024]{1,0:T(8,128)S(1)} %get-tuple-element.149.lower_ref.refs_4_), channel_id=1, source_target_pairs={{0,3},{1,2},{2,1},{3,0},{4,7},{5,6},{6,5},{7,4},{8,11},{9,10},{10,... | collective-permute-start | bytes 294920 | tf_op jit(solution)/shard_map/ppermute | solution.py:29
  89.0 2.0 %collective-permute-done.33.refs_1_ = f32[48,1024]{1,0:T(8,128)S(1)} collective-permute-done((f32[48,1024]{1,0:T(8,128)S(1)}, f32[48,1024]{1,0:T(8,128)S(1)}, u32[]{:S(2)}, u32[]{:S(2)}) %collective-permute-start.33) | collective-permute-done | bytes 196640 | tf_op jit(solution)/shard_map/ppermute | solution.py:29
  91.2 4.3 %collective-permute-done.34.refs_2_ = f32[48,1024]{1,0:T(8,128)S(1)} collective-permute-done((f32[48,1024]{1,0:T(8,128)S(1)}, f32[48,1024]{1,0:T(8,128)S(1)}, u32[]{:S(2)}, u32[]{:S(2)}) %collective-permute-start.34) | collective-permute-done | bytes 196640 | tf_op jit(solution)/shard_map/ppermute | solution.py:29
  95.5 0.6 shard_map.152
  96.1 1.3 %collective-permute-done.37.refs_6_ = f32[24,1024]{1,0:T(8,128)S(1)} collective-permute-done((f32[24,1024]{1,0:T(8,128)S(1)}, f32[24,1024]{1,0:T(8,128)S(1)}, u32[]{:S(2)}, u32[]{:S(2)}) %collective-permute-start.37) | collective-permute-done | bytes 98336 | tf_op jit(solution)/shard_map/ppermute | solution.py:29
  97.6 2.7 %collective-permute-start.40 = (f32[48,256]{1,0:T(8,128)S(1)}, f32[48,256]{1,0:T(8,128)S(1)}, u32[]{:S(2)}, u32[]{:S(2)}) collective-permute-start(f32[48,256]{1,0:T(8,128)S(1)} %get-tuple-element.155), channel_id=1, source_target_pairs={{0,2},{1,3},{2,0},{3,1},{4,6},{5,7},{6,4},{7,5},{8,10},{9,11},{10,... | collective-permute-start | bytes 147464 | tf_op jit(solution)/shard_map/ppermute | solution.py:29
  100.3 1.6 %collective-permute-start.41 = (f32[48,256]{1,0:T(8,128)S(1)}, f32[48,256]{1,0:T(8,128)S(1)}, u32[]{:S(2)}, u32[]{:S(2)}) collective-permute-start(f32[48,256]{1,0:T(8,128)S(1)} %get-tuple-element.156), channel_id=1, source_target_pairs={{0,3},{1,2},{2,1},{3,0},{4,7},{5,6},{6,5},{7,4},{8,11},{9,10},{10,... | collective-permute-start | bytes 147464 | tf_op jit(solution)/shard_map/ppermute | solution.py:29
  102.0 1.5 %shard_map.153 = f32[172,1024]{1,0:T(8,128)} custom-call(s32[2]{0:T(128)S(1)} %pad_add_fusion.1.ids_ref, f32[24,1024]{1,0:T(8,128)S(1)} %get-tuple-element.124.upper_ref.refs_0_, f32[24,1024]{1,0:T(8,128)S(1)} %collective-permute-done.26.refs_1_, f32[24,1024]{1,0:T(8,128)S(1)} %collective-permute-done.27.refs_2_, ...), custom_call_target="tpu_custom_call" | custom-call | bytes 2097152 | tf_op jit(solution)/shard_map/pallas_call | solution.py:49
  103.5 2.7 %collective-permute-done.41.refs_3_ = f32[48,256]{1,0:T(8,128)S(1)} collective-permute-done((f32[48,256]{1,0:T(8,128)S(1)}, f32[48,256]{1,0:T(8,128)S(1)}, u32[]{:S(2)}, u32[]{:S(2)}) %collective-permute-start.41) | collective-permute-done | bytes 49184 | tf_op jit(solution)/shard_map/ppermute | solution.py:29
  106.2 1.3 %shard_map.154 = (f32[4,40,256]{2,1,0:T(8,128)S(1)}, f32[4,40,256]{2,1,0:T(8,128)S(1)}) custom-call(s32[2]{0:T(128)S(1)} %pad_add_fusion.1.ids_ref, f32[128,256]{1,0:T(8,128)S(1)} %get-tuple-element.158.mixed_ref, f32[256,256]{1,0:T(8,128)S(1)} %get-tuple-element.159.hidden_ref, f32[256,256]{1,0:T(8,128)S(1)} %get-tuple-element.160.slope_ref, ...), custom_call_target="tpu_custom_call" | custom-call | flops 100000000 | bytes 2097152 | tf_op jit(solution)/shard_map/pallas_call | solution.py:49
  107.6 1.4 %collective-permute-done.42 = f32[4,40,256]{2,1,0:T(8,128)S(1)} collective-permute-done((f32[4,40,256]{2,1,0:T(8,128)S(1)}, f32[4,40,256]{2,1,0:T(8,128)S(1)}, u32[]{:S(2)}, u32[]{:S(2)}) %collective-permute-start.42) | collective-permute-done | bytes 163872 | tf_op jit(solution)/shard_map/ppermute | solution.py:29
  109.1 1.7 %collective-permute-start.45 = (f32[40,256]{1,0:T(8,128)S(1)}, f32[40,256]{1,0:T(8,128)S(1)}, u32[]{:S(2)}, u32[]{:S(2)}) collective-permute-start(f32[40,256]{1,0:T(8,128)S(1)} %get-tuple-element.175), channel_id=1, source_target_pairs={{0,3},{1,2},{2,1},{3,0},{4,7},{5,6},{6,5},{7,4},{8,11},{9,10},{10,... | collective-permute-start | bytes 122888 | tf_op jit(solution)/shard_map/ppermute | solution.py:29
  110.8 1.8 %collective-permute-start.44 = (f32[40,256]{1,0:T(8,128)S(1)}, f32[40,256]{1,0:T(8,128)S(1)}, u32[]{:S(2)}, u32[]{:S(2)}) collective-permute-start(f32[40,256]{1,0:T(8,128)S(1)} %get-tuple-element.176), channel_id=1, source_target_pairs={{0,2},{1,3},{2,0},{3,1},{4,6},{5,7},{6,4},{7,5},{8,10},{9,11},{10,... | collective-permute-start | bytes 122888 | tf_op jit(solution)/shard_map/ppermute | solution.py:29
  112.6 0.5 collective-permute-done.43
  113.1 2.2 %collective-permute-done.45 = f32[40,256]{1,0:T(8,128)S(1)} collective-permute-done((f32[40,256]{1,0:T(8,128)S(1)}, f32[40,256]{1,0:T(8,128)S(1)}, u32[]{:S(2)}, u32[]{:S(2)}) %collective-permute-start.45) | collective-permute-done | bytes 40992 | tf_op jit(solution)/shard_map/ppermute | solution.py:29
  115.3 1.5 %collective-permute-done.44 = f32[40,256]{1,0:T(8,128)S(1)} collective-permute-done((f32[40,256]{1,0:T(8,128)S(1)}, f32[40,256]{1,0:T(8,128)S(1)}, u32[]{:S(2)}, u32[]{:S(2)}) %collective-permute-start.44) | collective-permute-done | bytes 40992 | tf_op jit(solution)/shard_map/ppermute | solution.py:29
  116.8 2.5 %collective-permute-start.48 = (f32[40,256]{1,0:T(8,128)S(1)}, f32[40,256]{1,0:T(8,128)S(1)}, u32[]{:S(2)}, u32[]{:S(2)}) collective-permute-start(f32[40,256]{1,0:T(8,128)S(1)} %fusion.2), channel_id=1, source_target_pairs={{0,24},{4,28},{8,16},{12,20},{16,8},{20,12},{24,0},{28,4},{1,25},{... | collective-permute-start | bytes 122888 | tf_op jit(solution)/shard_map/ppermute | solution.py:29
  119.3 1.0 collective-permute-start.46
  120.4 1.5 %collective-permute-done.48 = f32[40,256]{1,0:T(8,128)S(1)} collective-permute-done((f32[40,256]{1,0:T(8,128)S(1)}, f32[40,256]{1,0:T(8,128)S(1)}, u32[]{:S(2)}, u32[]{:S(2)}) %collective-permute-start.48) | collective-permute-done | bytes 40992 | tf_op jit(solution)/shard_map/ppermute | solution.py:29
  121.9 1.5 %collective-permute-done.47 = f32[40,256]{1,0:T(8,128)S(1)} collective-permute-done((f32[40,256]{1,0:T(8,128)S(1)}, f32[40,256]{1,0:T(8,128)S(1)}, u32[]{:S(2)}, u32[]{:S(2)}) %collective-permute-start.47) | collective-permute-done | bytes 40992 | tf_op jit(solution)/shard_map/ppermute | solution.py:29
  123.4 1.2 collective-permute-done.49.other_ref
  124.6 1.3 %shard_map.155 = (f32[32,256]{1,0:T(8,128)}, f32[1,64]{1,0:T(1,128)}, f32[64,172]{1,0:T(8,128)}, f32[1,172]{1,0:T(1,128)}, f32[1,1]{1,0:T(1,128)}) custom-call(s32[2]{0:T(128)S(1)} %pad_add_fusion.1.ids_ref, f32[40,256]{1,0:T(8,128)S(1)} %add_add_fusion.mine_ref, f32[40,256]{1,0:T(8,128)S(1)} %collective-permute-done.49.other_ref), custom_call_target="tpu_custom_call" | custom-call | tf_op jit(solution)/shard_map/pallas_call | solution.py:49
  (61 shorter events, 2.1 us)
Async XLA Ops:
  0.6 22.1 %copy-start = (f32[32,1024]{1,0:T(8,128)S(1)}, f32[32,1024]{1,0:T(8,128)}, u32[]{:S(2)}) copy-start(f32[32,1024]{1,0:T(8,128)} %refs_0_) | copy-start | bytes 393220
  1.5 8.6 %collective-permute-start.5 = (f32[104,256]{1,0:T(8,128)S(1)}, f32[104,256]{1,0:T(8,128)S(1)}, u32[]{:S(2)}, u32[]{:S(2)}) collective-permute-start(f32[104,256]{1,0:T(8,128)S(1)} %pad_add_fusion.refs_4_), channel_id=1, source_target_pairs={{0,3},{1,2},{2,1},{3,0},{4,7},{5,6},{6,5},{7,4},{8,11},{9,10},{10,... | collective-permute-start | bytes 319496 | tf_op jit(solution)/shard_map/ppermute | solution.py:29
  6.7 16.1 %collective-permute-start.1 = (f32[32,1024]{1,0:T(8,128)}, f32[32,1024]{1,0:T(8,128)S(1)}, u32[]{:S(2)}, u32[]{:S(2)}) collective-permute-start(f32[32,1024]{1,0:T(8,128)} %refs_0_), channel_id=1, source_target_pairs={{0,16},{4,20},{8,24},{12,28},{16,0},{20,4},{24,8},{28,12},{1,17},{... | collective-permute-start | bytes 393224 | tf_op jit(solution)/shard_map/ppermute | solution.py:29
  8.2 14.5 %collective-permute-start = (f32[32,1024]{1,0:T(8,128)}, f32[32,1024]{1,0:T(8,128)S(1)}, u32[]{:S(2)}, u32[]{:S(2)}) collective-permute-start(f32[32,1024]{1,0:T(8,128)} %refs_0_), channel_id=1, source_target_pairs={{0,8},{4,12},{8,0},{12,4},{16,24},{20,28},{24,16},{28,20},{1,9},{5... | collective-permute-start | bytes 393224 | tf_op jit(solution)/shard_map/ppermute | solution.py:29
  9.7 13.1 %collective-permute-start.2 = (f32[32,1024]{1,0:T(8,128)}, f32[32,1024]{1,0:T(8,128)S(1)}, u32[]{:S(2)}, u32[]{:S(2)}) collective-permute-start(f32[32,1024]{1,0:T(8,128)} %refs_0_), channel_id=1, source_target_pairs={{0,24},{4,28},{8,16},{12,20},{16,8},{20,12},{24,0},{28,4},{1,25},{... | collective-permute-start | bytes 393224 | tf_op jit(solution)/shard_map/ppermute | solution.py:29
  10.1 12.5 %collective-permute-start.4 = (f32[104,256]{1,0:T(8,128)S(1)}, f32[104,256]{1,0:T(8,128)S(1)}, u32[]{:S(2)}, u32[]{:S(2)}) collective-permute-start(f32[104,256]{1,0:T(8,128)S(1)} %pad_add_fusion.refs_4_), channel_id=1, source_target_pairs={{0,2},{1,3},{2,0},{3,1},{4,6},{5,7},{6,4},{7,5},{8,10},{9,11},{10,... | collective-permute-start | bytes 319496 | tf_op jit(solution)/shard_map/ppermute | solution.py:29
  10.2 12.5 %collective-permute-start.3 = (f32[104,256]{1,0:T(8,128)S(1)}, f32[104,256]{1,0:T(8,128)S(1)}, u32[]{:S(2)}, u32[]{:S(2)}) collective-permute-start(f32[104,256]{1,0:T(8,128)S(1)} %pad_add_fusion.refs_4_), channel_id=1, source_target_pairs={{0,1},{1,0},{2,3},{3,2},{4,5},{5,4},{6,7},{7,6},{8,9},{9,8},{10,11... | collective-permute-start | bytes 319496 | tf_op jit(solution)/shard_map/ppermute | solution.py:29
  22.7 1.4 %collective-permute-start.6 = (f32[32,1024]{1,0:T(8,128)S(1)}, f32[32,1024]{1,0:T(8,128)S(1)}, u32[]{:S(2)}, u32[]{:S(2)}) collective-permute-start(f32[32,1024]{1,0:T(8,128)S(1)} %copy-done), channel_id=1, source_target_pairs={{0,4},{4,0},{8,12},{12,8},{16,20},{20,16},{24,28},{28,24},{1,5},{5... | collective-permute-start | bytes 393224 | tf_op jit(solution)/shard_map/ppermute | solution.py:29
  22.8 1.5 %collective-permute-start.7 = (f32[32,1024]{1,0:T(8,128)S(1)}, f32[32,1024]{1,0:T(8,128)S(1)}, u32[]{:S(2)}, u32[]{:S(2)}) collective-permute-start(f32[32,1024]{1,0:T(8,128)S(1)} %collective-permute-done.refs_2_), channel_id=1, source_target_pairs={{0,4},{4,0},{8,12},{12,8},{16,20},{20,16},{24,28},{28,24},{1,5},{5... | collective-permute-start | bytes 393224 | tf_op jit(solution)/shard_map/ppermute | solution.py:29
  23.3 1.3 %collective-permute-start.8 = (f32[32,1024]{1,0:T(8,128)S(1)}, f32[32,1024]{1,0:T(8,128)S(1)}, u32[]{:S(2)}, u32[]{:S(2)}) collective-permute-start(f32[32,1024]{1,0:T(8,128)S(1)} %collective-permute-done.1.refs_4_), channel_id=1, source_target_pairs={{0,4},{4,0},{8,12},{12,8},{16,20},{20,16},{24,28},{28,24},{1,5},{5... | collective-permute-start | bytes 393224 | tf_op jit(solution)/shard_map/ppermute | solution.py:29
  23.4 1.5 %collective-permute-start.9 = (f32[32,1024]{1,0:T(8,128)S(1)}, f32[32,1024]{1,0:T(8,128)S(1)}, u32[]{:S(2)}, u32[]{:S(2)}) collective-permute-start(f32[32,1024]{1,0:T(8,128)S(1)} %collective-permute-done.2.refs_6_), channel_id=1, source_target_pairs={{0,4},{4,0},{8,12},{12,8},{16,20},{20,16},{24,28},{28,24},{1,5},{5... | collective-permute-start | bytes 393224 | tf_op jit(solution)/shard_map/ppermute | solution.py:29
  30.1 4.5 %collective-permute-start.10 = (f32[32,256]{1,0:T(8,128)S(1)}, f32[32,256]{1,0:T(8,128)S(1)}, u32[]{:S(2)}, u32[]{:S(2)}) collective-permute-start(f32[32,256]{1,0:T(8,128)S(1)} %get-tuple-element.102), channel_id=1, source_target_pairs={{0,1},{1,0},{2,3},{3,2},{4,5},{5,4},{6,7},{7,6},{8,9},{9,8},{10,11... | collective-permute-start | bytes 98312 | tf_op jit(solution)/shard_map/ppermute | solution.py:29
  30.7 6.4 %collective-permute-start.11 = (f32[32,256]{1,0:T(8,128)S(1)}, f32[32,256]{1,0:T(8,128)S(1)}, u32[]{:S(2)}, u32[]{:S(2)}) collective-permute-start(f32[32,256]{1,0:T(8,128)S(1)} %get-tuple-element.103), channel_id=1, source_target_pairs={{0,2},{1,3},{2,0},{3,1},{4,6},{5,7},{6,4},{7,5},{8,10},{9,11},{10,... | collective-permute-start | bytes 98312 | tf_op jit(solution)/shard_map/ppermute | solution.py:29
  34.5 5.7 %collective-permute-start.12 = (f32[32,256]{1,0:T(8,128)S(1)}, f32[32,256]{1,0:T(8,128)S(1)}, u32[]{:S(2)}, u32[]{:S(2)}) collective-permute-start(f32[32,256]{1,0:T(8,128)S(1)} %get-tuple-element.104), channel_id=1, source_target_pairs={{0,3},{1,2},{2,1},{3,0},{4,7},{5,6},{6,5},{7,4},{8,11},{9,10},{10,... | collective-permute-start | bytes 98312 | tf_op jit(solution)/shard_map/ppermute | solution.py:29
  40.2 19.4 %copy-start.1 = (s32[1024]{0:T(1024)S(1)}, s32[1024]{0:T(1024)}, u32[]{:S(2)}) copy-start(s32[1024]{0:T(1024)} %param.14) | copy-start | bytes 12292
  40.2 19.4 %copy-start.3 = (f32[172]{0:T(256)S(1)}, f32[172]{0:T(256)}, u32[]{:S(2)}) copy-start(f32[172]{0:T(256)} %param.19) | copy-start | bytes 2068
  41.6 5.2 %collective-permute-start.13 = (f32[48,256]{1,0:T(8,128)S(1)}, f32[48,256]{1,0:T(8,128)S(1)}, u32[]{:S(2)}, u32[]{:S(2)}) collective-permute-start(f32[48,256]{1,0:T(8,128)S(1)} %get-tuple-element.110), channel_id=1, source_target_pairs={{0,1},{1,0},{2,3},{3,2},{4,5},{5,4},{6,7},{7,6},{8,9},{9,8},{10,11... | collective-permute-start | bytes 147464 | tf_op jit(solution)/shard_map/ppermute | solution.py:29
  41.7 5.1 %collective-permute-start.14 = (f32[48,256]{1,0:T(8,128)S(1)}, f32[48,256]{1,0:T(8,128)S(1)}, u32[]{:S(2)}, u32[]{:S(2)}) collective-permute-start(f32[48,256]{1,0:T(8,128)S(1)} %get-tuple-element.111), channel_id=1, source_target_pairs={{0,2},{1,3},{2,0},{3,1},{4,6},{5,7},{6,4},{7,5},{8,10},{9,11},{10,... | collective-permute-start | bytes 147464 | tf_op jit(solution)/shard_map/ppermute | solution.py:29
  42.6 6.0 %collective-permute-start.15 = (f32[48,256]{1,0:T(8,128)S(1)}, f32[48,256]{1,0:T(8,128)S(1)}, u32[]{:S(2)}, u32[]{:S(2)}) collective-permute-start(f32[48,256]{1,0:T(8,128)S(1)} %get-tuple-element.112), channel_id=1, source_target_pairs={{0,3},{1,2},{2,1},{3,0},{4,7},{5,6},{6,5},{7,4},{8,11},{9,10},{10,... | collective-permute-start | bytes 147464 | tf_op jit(solution)/shard_map/ppermute | solution.py:29
  48.6 25.4 %copy-start.2 = (s32[1024]{0:T(1024)S(1)}, s32[1024]{0:T(1024)}, u32[]{:S(2)}) copy-start(s32[1024]{0:T(1024)} %param.15) | copy-start | bytes 12292
  48.6 7.6 %collective-permute-start.21 = (f32[4,48,256]{2,1,0:T(8,128)S(1)}, f32[4,48,256]{2,1,0:T(8,128)S(1)}, u32[]{:S(2)}, u32[]{:S(2)}) collective-permute-start(f32[4,48,256]{2,1,0:T(8,128)S(1)} %shard_map.148.refs_0_), channel_id=1, source_target_pairs={{0,24},{4,28},{8,16},{12,20},{16,8},{20,12},{24,0},{28,4},{1,25},{... | collective-permute-start | bytes 589832 | tf_op jit(solution)/shard_map/ppermute | solution.py:29
  50.2 7.7 %collective-permute-start.19 = (f32[4,48,256]{2,1,0:T(8,128)S(1)}, f32[4,48,256]{2,1,0:T(8,128)S(1)}, u32[]{:S(2)}, u32[]{:S(2)}) collective-permute-start(f32[4,48,256]{2,1,0:T(8,128)S(1)} %shard_map.148.refs_0_), channel_id=1, source_target_pairs={{0,16},{4,20},{8,24},{12,28},{16,0},{20,4},{24,8},{28,12},{1,17},{... | collective-permute-start | bytes 589832 | tf_op jit(solution)/shard_map/ppermute | solution.py:29
  50.3 7.6 %collective-permute-start.17 = (f32[4,48,256]{2,1,0:T(8,128)S(1)}, f32[4,48,256]{2,1,0:T(8,128)S(1)}, u32[]{:S(2)}, u32[]{:S(2)}) collective-permute-start(f32[4,48,256]{2,1,0:T(8,128)S(1)} %shard_map.148.refs_0_), channel_id=1, source_target_pairs={{0,8},{4,12},{8,0},{12,4},{16,24},{20,28},{24,16},{28,20},{1,9},{5... | collective-permute-start | bytes 589832 | tf_op jit(solution)/shard_map/ppermute | solution.py:29
  52.2 6.2 %collective-permute-start.16 = (f32[4,48,256]{2,1,0:T(8,128)S(1)}, f32[4,48,256]{2,1,0:T(8,128)S(1)}, u32[]{:S(2)}, u32[]{:S(2)}) collective-permute-start(f32[4,48,256]{2,1,0:T(8,128)S(1)} %shard_map.148.refs_0_), channel_id=1, source_target_pairs={{0,4},{4,0},{8,12},{12,8},{16,20},{20,16},{24,28},{28,24},{1,5},{5... | collective-permute-start | bytes 589832 | tf_op jit(solution)/shard_map/ppermute | solution.py:29
  56.3 2.2 %collective-permute-start.22 = (f32[4,48,256]{2,1,0:T(8,128)S(1)}, f32[4,48,256]{2,1,0:T(8,128)S(1)}, u32[]{:S(2)}, u32[]{:S(2)}) collective-permute-start(f32[4,48,256]{2,1,0:T(8,128)S(1)} %collective-permute-done.21.refs_6_), channel_id=1, source_target_pairs={{0,4},{4,0},{8,12},{12,8},{16,20},{20,16},{24,28},{28,24},{1,5},{5... | collective-permute-start | bytes 589832 | tf_op jit(solution)/shard_map/ppermute | solution.py:29
  57.9 1.4 %collective-permute-start.20 = (f32[4,48,256]{2,1,0:T(8,128)S(1)}, f32[4,48,256]{2,1,0:T(8,128)S(1)}, u32[]{:S(2)}, u32[]{:S(2)}) collective-permute-start(f32[4,48,256]{2,1,0:T(8,128)S(1)} %collective-permute-done.19.refs_4_), channel_id=1, source_target_pairs={{0,4},{4,0},{8,12},{12,8},{16,20},{20,16},{24,28},{28,24},{1,5},{5... | collective-permute-start | bytes 589832 | tf_op jit(solution)/shard_map/ppermute | solution.py:29
  57.9 1.7 %collective-permute-start.18 = (f32[4,48,256]{2,1,0:T(8,128)S(1)}, f32[4,48,256]{2,1,0:T(8,128)S(1)}, u32[]{:S(2)}, u32[]{:S(2)}) collective-permute-start(f32[4,48,256]{2,1,0:T(8,128)S(1)} %collective-permute-done.17.refs_2_), channel_id=1, source_target_pairs={{0,4},{4,0},{8,12},{12,8},{16,20},{20,16},{24,28},{28,24},{1,5},{5... | collective-permute-start | bytes 589832 | tf_op jit(solution)/shard_map/ppermute | solution.py:29
  65.2 7.5 %collective-permute-start.25 = (f32[8,1024]{1,0:T(8,128)S(1)}, f32[8,1024]{1,0:T(8,128)S(1)}, u32[]{:S(2)}, u32[]{:S(2)}) collective-permute-start(f32[8,1024]{1,0:T(8,128)S(1)} %get-tuple-element.115.refs_0_), channel_id=1, source_target_pairs={{0,3},{1,2},{2,1},{3,0},{4,7},{5,6},{6,5},{7,4},{8,11},{9,10},{10,... | collective-permute-start | bytes 98312 | tf_op jit(solution)/shard_map/ppermute | solution.py:29
  68.3 5.7 %collective-permute-start.24 = (f32[8,1024]{1,0:T(8,128)S(1)}, f32[8,1024]{1,0:T(8,128)S(1)}, u32[]{:S(2)}, u32[]{:S(2)}) collective-permute-start(f32[8,1024]{1,0:T(8,128)S(1)} %get-tuple-element.115.refs_0_), channel_id=1, source_target_pairs={{0,2},{1,3},{2,0},{3,1},{4,6},{5,7},{6,4},{7,5},{8,10},{9,11},{10,... | collective-permute-start | bytes 98312 | tf_op jit(solution)/shard_map/ppermute | solution.py:29
  68.3 5.7 %collective-permute-start.23 = (f32[8,1024]{1,0:T(8,128)S(1)}, f32[8,1024]{1,0:T(8,128)S(1)}, u32[]{:S(2)}, u32[]{:S(2)}) collective-permute-start(f32[8,1024]{1,0:T(8,128)S(1)} %get-tuple-element.115.refs_0_), channel_id=1, source_target_pairs={{0,1},{1,0},{2,3},{3,2},{4,5},{5,4},{6,7},{7,6},{8,9},{9,8},{10,11... | collective-permute-start | bytes 98312 | tf_op jit(solution)/shard_map/ppermute | solution.py:29
  69.6 8.5 %collective-permute-start.28 = (f32[24,1024]{1,0:T(8,128)S(1)}, f32[24,1024]{1,0:T(8,128)S(1)}, u32[]{:S(2)}, u32[]{:S(2)}) collective-permute-start(f32[24,1024]{1,0:T(8,128)S(1)} %get-tuple-element.124.upper_ref.refs_0_), channel_id=1, source_target_pairs={{0,3},{1,2},{2,1},{3,0},{4,7},{5,6},{6,5},{7,4},{8,11},{9,10},{10,... | collective-permute-start | bytes 294920 | tf_op jit(solution)/shard_map/ppermute | solution.py:29
  72.7 8.2 %collective-permute-start.27 = (f32[24,1024]{1,0:T(8,128)S(1)}, f32[24,1024]{1,0:T(8,128)S(1)}, u32[]{:S(2)}, u32[]{:S(2)}) collective-permute-start(f32[24,1024]{1,0:T(8,128)S(1)} %get-tuple-element.124.upper_ref.refs_0_), channel_id=1, source_target_pairs={{0,2},{1,3},{2,0},{3,1},{4,6},{5,7},{6,4},{7,5},{8,10},{9,11},{10,... | collective-permute-start | bytes 294920 | tf_op jit(solution)/shard_map/ppermute | solution.py:29
  72.7 8.2 %collective-permute-start.26 = (f32[24,1024]{1,0:T(8,128)S(1)}, f32[24,1024]{1,0:T(8,128)S(1)}, u32[]{:S(2)}, u32[]{:S(2)}) collective-permute-start(f32[24,1024]{1,0:T(8,128)S(1)} %get-tuple-element.124.upper_ref.refs_0_), channel_id=1, source_target_pairs={{0,1},{1,0},{2,3},{3,2},{4,5},{5,4},{6,7},{7,6},{8,9},{9,8},{10,11... | collective-permute-start | bytes 294920 | tf_op jit(solution)/shard_map/ppermute | solution.py:29
  80.9 1.4 %collective-permute-start.29 = (f32[48,1024]{1,0:T(8,128)S(1)}, f32[48,1024]{1,0:T(8,128)S(1)}, u32[]{:S(2)}, u32[]{:S(2)}) collective-permute-start(f32[48,1024]{1,0:T(8,128)S(1)} %get-tuple-element.132), channel_id=1, source_target_pairs={{0,4},{4,0},{8,12},{12,8},{16,20},{20,16},{24,28},{28,24},{1,5},{5... | collective-permute-start | bytes 589832 | tf_op jit(solution)/shard_map/ppermute | solution.py:29
  80.9 1.7 %collective-permute-start.30 = (f32[48,1024]{1,0:T(8,128)S(1)}, f32[48,1024]{1,0:T(8,128)S(1)}, u32[]{:S(2)}, u32[]{:S(2)}) collective-permute-start(f32[48,1024]{1,0:T(8,128)S(1)} %get-tuple-element.133), channel_id=1, source_target_pairs={{0,4},{4,0},{8,12},{12,8},{16,20},{20,16},{24,28},{28,24},{1,5},{5... | collective-permute-start | bytes 589832 | tf_op jit(solution)/shard_map/ppermute | solution.py:29
  81.4 1.5 %collective-permute-start.31 = (f32[48,1024]{1,0:T(8,128)S(1)}, f32[48,1024]{1,0:T(8,128)S(1)}, u32[]{:S(2)}, u32[]{:S(2)}) collective-permute-start(f32[48,1024]{1,0:T(8,128)S(1)} %get-tuple-element.134), channel_id=1, source_target_pairs={{0,4},{4,0},{8,12},{12,8},{16,20},{20,16},{24,28},{28,24},{1,5},{5... | collective-permute-start | bytes 589832 | tf_op jit(solution)/shard_map/ppermute | solution.py:29
  81.4 1.8 %collective-permute-start.32 = (f32[48,1024]{1,0:T(8,128)S(1)}, f32[48,1024]{1,0:T(8,128)S(1)}, u32[]{:S(2)}, u32[]{:S(2)}) collective-permute-start(f32[48,1024]{1,0:T(8,128)S(1)} %get-tuple-element.135), channel_id=1, source_target_pairs={{0,4},{4,0},{8,12},{12,8},{16,20},{20,16},{24,28},{28,24},{1,5},{5... | collective-permute-start | bytes 589832 | tf_op jit(solution)/shard_map/ppermute | solution.py:29
  83.2 7.8 %collective-permute-start.33 = (f32[48,1024]{1,0:T(8,128)S(1)}, f32[48,1024]{1,0:T(8,128)S(1)}, u32[]{:S(2)}, u32[]{:S(2)}) collective-permute-start(f32[48,1024]{1,0:T(8,128)S(1)} %get-tuple-element.141), channel_id=1, source_target_pairs={{0,8},{4,12},{8,0},{12,4},{16,24},{20,28},{24,16},{28,20},{1,9},{5... | collective-permute-start | bytes 589832 | tf_op jit(solution)/shard_map/ppermute | solution.py:29
  84.2 11.3 %collective-permute-start.34 = (f32[48,1024]{1,0:T(8,128)S(1)}, f32[48,1024]{1,0:T(8,128)S(1)}, u32[]{:S(2)}, u32[]{:S(2)}) collective-permute-start(f32[48,1024]{1,0:T(8,128)S(1)} %get-tuple-element.142), channel_id=1, source_target_pairs={{0,16},{4,20},{8,24},{12,28},{16,0},{20,4},{24,8},{28,12},{1,17},{... | collective-permute-start | bytes 589832 | tf_op jit(solution)/shard_map/ppermute | solution.py:29
  86.3 9.2 %collective-permute-start.35 = (f32[48,1024]{1,0:T(8,128)S(1)}, f32[48,1024]{1,0:T(8,128)S(1)}, u32[]{:S(2)}, u32[]{:S(2)}) collective-permute-start(f32[48,1024]{1,0:T(8,128)S(1)} %get-tuple-element.143), channel_id=1, source_target_pairs={{0,24},{4,28},{8,16},{12,20},{16,8},{20,12},{24,0},{28,4},{1,25},{... | collective-permute-start | bytes 589832 | tf_op jit(solution)/shard_map/ppermute | solution.py:29
  86.8 9.3 %collective-permute-start.38 = (f32[24,1024]{1,0:T(8,128)S(1)}, f32[24,1024]{1,0:T(8,128)S(1)}, u32[]{:S(2)}, u32[]{:S(2)}) collective-permute-start(f32[24,1024]{1,0:T(8,128)S(1)} %get-tuple-element.149.lower_ref.refs_4_), channel_id=1, source_target_pairs={{0,3},{1,2},{2,1},{3,0},{4,7},{5,6},{6,5},{7,4},{8,11},{9,10},{10,... | collective-permute-start | bytes 294920 | tf_op jit(solution)/shard_map/ppermute | solution.py:29
  89.0 8.4 %collective-permute-start.37 = (f32[24,1024]{1,0:T(8,128)S(1)}, f32[24,1024]{1,0:T(8,128)S(1)}, u32[]{:S(2)}, u32[]{:S(2)}) collective-permute-start(f32[24,1024]{1,0:T(8,128)S(1)} %get-tuple-element.149.lower_ref.refs_4_), channel_id=1, source_target_pairs={{0,2},{1,3},{2,0},{3,1},{4,6},{5,7},{6,4},{7,5},{8,10},{9,11},{10,... | collective-permute-start | bytes 294920 | tf_op jit(solution)/shard_map/ppermute | solution.py:29
  91.0 6.5 %collective-permute-start.36 = (f32[24,1024]{1,0:T(8,128)S(1)}, f32[24,1024]{1,0:T(8,128)S(1)}, u32[]{:S(2)}, u32[]{:S(2)}) collective-permute-start(f32[24,1024]{1,0:T(8,128)S(1)} %get-tuple-element.149.lower_ref.refs_4_), channel_id=1, source_target_pairs={{0,1},{1,0},{2,3},{3,2},{4,5},{5,4},{6,7},{7,6},{8,9},{9,8},{10,11... | collective-permute-start | bytes 294920 | tf_op jit(solution)/shard_map/ppermute | solution.py:29
  97.6 5.9 %collective-permute-start.39 = (f32[48,256]{1,0:T(8,128)S(1)}, f32[48,256]{1,0:T(8,128)S(1)}, u32[]{:S(2)}, u32[]{:S(2)}) collective-permute-start(f32[48,256]{1,0:T(8,128)S(1)} %get-tuple-element.154), channel_id=1, source_target_pairs={{0,1},{1,0},{2,3},{3,2},{4,5},{5,4},{6,7},{7,6},{8,9},{9,8},{10,11... | collective-permute-start | bytes 147464 | tf_op jit(solution)/shard_map/ppermute | solution.py:29
  97.6 5.9 %collective-permute-start.40 = (f32[48,256]{1,0:T(8,128)S(1)}, f32[48,256]{1,0:T(8,128)S(1)}, u32[]{:S(2)}, u32[]{:S(2)}) collective-permute-start(f32[48,256]{1,0:T(8,128)S(1)} %get-tuple-element.155), channel_id=1, source_target_pairs={{0,2},{1,3},{2,0},{3,1},{4,6},{5,7},{6,4},{7,5},{8,10},{9,11},{10,... | collective-permute-start | bytes 147464 | tf_op jit(solution)/shard_map/ppermute | solution.py:29
  100.3 5.9 %collective-permute-start.41 = (f32[48,256]{1,0:T(8,128)S(1)}, f32[48,256]{1,0:T(8,128)S(1)}, u32[]{:S(2)}, u32[]{:S(2)}) collective-permute-start(f32[48,256]{1,0:T(8,128)S(1)} %get-tuple-element.156), channel_id=1, source_target_pairs={{0,3},{1,2},{2,1},{3,0},{4,7},{5,6},{6,5},{7,4},{8,11},{9,10},{10,... | collective-permute-start | bytes 147464 | tf_op jit(solution)/shard_map/ppermute | solution.py:29
  107.5 1.5 %collective-permute-start.42 = (f32[4,40,256]{2,1,0:T(8,128)S(1)}, f32[4,40,256]{2,1,0:T(8,128)S(1)}, u32[]{:S(2)}, u32[]{:S(2)}) collective-permute-start(f32[4,40,256]{2,1,0:T(8,128)S(1)} %get-tuple-element.168), channel_id=1, source_target_pairs={{0,4},{4,0},{8,12},{12,8},{16,20},{20,16},{24,28},{28,24},{1,5},{5... | collective-permute-start | bytes 491528 | tf_op jit(solution)/shard_map/ppermute | solution.py:29
  109.0 4.1 %collective-permute-start.43 = (f32[40,256]{1,0:T(8,128)S(1)}, f32[40,256]{1,0:T(8,128)S(1)}, u32[]{:S(2)}, u32[]{:S(2)}) collective-permute-start(f32[40,256]{1,0:T(8,128)S(1)} %get-tuple-element.174), channel_id=1, source_target_pairs={{0,1},{1,0},{2,3},{3,2},{4,5},{5,4},{6,7},{7,6},{8,9},{9,8},{10,11... | collective-permute-start | bytes 122888 | tf_op jit(solution)/shard_map/ppermute | solution.py:29
  109.1 6.2 %collective-permute-start.45 = (f32[40,256]{1,0:T(8,128)S(1)}, f32[40,256]{1,0:T(8,128)S(1)}, u32[]{:S(2)}, u32[]{:S(2)}) collective-permute-start(f32[40,256]{1,0:T(8,128)S(1)} %get-tuple-element.175), channel_id=1, source_target_pairs={{0,3},{1,2},{2,1},{3,0},{4,7},{5,6},{6,5},{7,4},{8,11},{9,10},{10,... | collective-permute-start | bytes 122888 | tf_op jit(solution)/shard_map/ppermute | solution.py:29
  110.8 6.0 %collective-permute-start.44 = (f32[40,256]{1,0:T(8,128)S(1)}, f32[40,256]{1,0:T(8,128)S(1)}, u32[]{:S(2)}, u32[]{:S(2)}) collective-permute-start(f32[40,256]{1,0:T(8,128)S(1)} %get-tuple-element.176), channel_id=1, source_target_pairs={{0,2},{1,3},{2,0},{3,1},{4,6},{5,7},{6,4},{7,5},{8,10},{9,11},{10,... | collective-permute-start | bytes 122888 | tf_op jit(solution)/shard_map/ppermute | solution.py:29
  116.8 5.1 %collective-permute-start.48 = (f32[40,256]{1,0:T(8,128)S(1)}, f32[40,256]{1,0:T(8,128)S(1)}, u32[]{:S(2)}, u32[]{:S(2)}) collective-permute-start(f32[40,256]{1,0:T(8,128)S(1)} %fusion.2), channel_id=1, source_target_pairs={{0,24},{4,28},{8,16},{12,20},{16,8},{20,12},{24,0},{28,4},{1,25},{... | collective-permute-start | bytes 122888 | tf_op jit(solution)/shard_map/ppermute | solution.py:29
  119.3 4.0 %collective-permute-start.47 = (f32[40,256]{1,0:T(8,128)S(1)}, f32[40,256]{1,0:T(8,128)S(1)}, u32[]{:S(2)}, u32[]{:S(2)}) collective-permute-start(f32[40,256]{1,0:T(8,128)S(1)} %fusion.2), channel_id=1, source_target_pairs={{0,16},{4,20},{8,24},{12,28},{16,0},{20,4},{24,8},{28,12},{1,17},{... | collective-permute-start | bytes 122888 | tf_op jit(solution)/shard_map/ppermute | solution.py:29
  119.3 4.0 %collective-permute-start.46 = (f32[40,256]{1,0:T(8,128)S(1)}, f32[40,256]{1,0:T(8,128)S(1)}, u32[]{:S(2)}, u32[]{:S(2)}) collective-permute-start(f32[40,256]{1,0:T(8,128)S(1)} %fusion.2), channel_id=1, source_target_pairs={{0,8},{4,12},{8,0},{12,4},{16,24},{20,28},{24,16},{28,20},{1,9},{5... | collective-permute-start | bytes 122888 | tf_op jit(solution)/shard_map/ppermute | solution.py:29
  123.3 1.3 %collective-permute-start.49 = (f32[40,256]{1,0:T(8,128)S(1)}, f32[40,256]{1,0:T(8,128)S(1)}, u32[]{:S(2)}, u32[]{:S(2)}) collective-permute-start(f32[40,256]{1,0:T(8,128)S(1)} %add_add_fusion.mine_ref), channel_id=1, source_target_pairs={{0,4},{4,0},{8,12},{12,8},{16,20},{20,16},{24,28},{28,24},{1,5},{5... | collective-permute-start | bytes 122888 | tf_op jit(solution)/shard_map/ppermute | solution.py:29

commit v5 on v4

--- a/solution.py
+++ b/solution.py
@@ -351,10 +351,9 @@
     total = jnp.sum(jnp.where(inside, jnp.exp(logits - top), 0.0), axis=0, keepdims=True)
     hit = inside & (place + col * per == labels_ref[...])
     chosen = jnp.sum(jnp.where(hit, logits, 0.0), axis=0, keepdims=True)
-    stats_ref[...] = jnp.zeros_like(stats_ref)
-    stats_ref[0:1] = top
-    stats_ref[1:2] = total
-    stats_ref[2:3] = chosen
+    for kind, value in enumerate((top, total, chosen)):
+        for row in range(rows):
+            stats_ref[kind * rows + row : kind * rows + row + 1] = value[:, row * BLOCK : (row + 1) * BLOCK]
 
 
 def mix_back_body(nodes, cols, per, ids_ref, total_ref, list_ref, row_ref, pack_ref, upper_ref, lower_ref, labels_ref, mask_ref, *refs):
@@ -362,10 +361,15 @@
     extra_ref, sums, grads = refs[cols + nodes :]
     rows = grads.shape[0]
     node, col = ids_ref[0], ids_ref[1]
-    tops = [ref[0:1] for ref in stats]
+
+    def unfold(kind, ref):
+        lines = [ref[kind * rows + row : kind * rows + row + 1] for row in range(rows)]
+        return jnp.concatenate(lines, axis=1)
+
+    tops = [unfold(0, ref) for ref in stats]
     top = functools.reduce(jnp.maximum, tops)
-    total = sum(ref[1:2] * jnp.exp(at - top) for ref, at in zip(stats, tops))
-    chosen = sum(ref[2:3] for ref in stats)
+    total = sum(unfold(1, ref) * jnp.exp(at - top) for ref, at in zip(stats, tops))
+    chosen = sum(unfold(2, ref) for ref in stats)
     mask = mask_ref[...].astype(f32)
     logits = jnp.concatenate([upper_ref[...], lower_ref[...]], axis=0)
     place = lax.broadcasted_iota(jnp.int32, logits.shape, 0)
@@ -584,7 +588,7 @@
     scores = gather_cores(gather_chips(stacked, nodes))
     upper, lower, stats = call(
         functools.partial(mix_out_body, nodes, cols, per),
-        [shape((HALF, local), f32), shape((PAD - HALF, local), f32), shape((8, local), f32)],
+        [shape((HALF, local), f32), shape((PAD - HALF, local), f32), shape((3 * rows, BLOCK), f32)],
         [pltpu.VMEM((block_total, 2 * PAD, BLOCK), bf16), pltpu.VMEM((rows, 2 * PAD, 2 * BLOCK), f32), pltpu.VMEM((cols, PAD, 1), f32)],
         *sparse,
         bias_out[None, :],
@@ -639,7 +643,6 @@
         limit=20,
         moved=MIB,
     )
-    spread_slices, lowers = lax.optimization_barrier((spread_slices, lowers))
     spread_pieces = [spread_slices[0]] + [exchange(spread_slices[k], "col", k) for k in range(1, cols)]
     (logits,) = call(
         functools.partial(logits_body, cols, per),

time: 126 us -> 124 us (0.984)
  Pallas kernels: 32 us -> 26.2 us
  starting transfers between devices: 51.6 us -> 53.4 us
    pallas_call x11, Pallas kernels: 32 us -> 26.2 us  [call(): pl.pallas_call(body, out_shape=outs, in_specs=specs or [VMEM] * len(args)...]
    ppermute x50, starting transfers between devices: 51.6 us -> 53.4 us  [exchange(): return lax.ppermute(value, axis, [(i, i ^ offset) for i in range(total)])]
  transfers between devices with their start and end apart: 50 -> 50, of which waited for: 29 -> 28; matrix products, arithmetic and copies ran while one was open for 0% -> 0% of each run, Pallas kernels for 14% -> 12%
where the time goes in v5:
time: 124 us; the launch traced here: 123 us
  starting transfers between devices  53.4 us (43%)
  waiting for transfers between devices  41.7 us (34%)
  Pallas kernels  26.2 us (21%)
    ppermute x50, starting transfers between devices, exchange(): return lax.ppermute(value, axis, [(i, i ^ offset) for i in range(total)])  53.4 us
    ppermute x50, waiting for transfers between devices, exchange(): return lax.ppermute(value, axis, [(i, i ^ offset) for i in range(total)])  41.7 us
    pallas_call x11, Pallas kernels, call(): pl.pallas_call(body, out_shape=outs, in_specs=specs or [VMEM] * len(args)...  26.2 us
  transfers between devices with their start and end apart: 50, of which 28 were waited for; matrix products, arithmetic and copies ran while one was open for 0% of the time, Pallas kernels for 12%

profile of v5, /device:TPU:0, one launch (start us, length us, event | category | flops | bytes accessed | tf_op | source)
XLA Modules:
  0.0 123.2 jit_solution(17718843342074010169)
XLA Ops:
  0.6 0.9 pad_add_fusion.refs_4_
  1.5 5.1 %collective-permute-start.5 = (f32[104,256]{1,0:T(8,128)S(1)}, f32[104,256]{1,0:T(8,128)S(1)}, u32[]{:S(2)}, u32[]{:S(2)}) collective-permute-start(f32[104,256]{1,0:T(8,128)S(1)} %pad_add_fusion.refs_4_), channel_id=1, source_target_pairs={{0,3},{1,2},{2,1},{3,0},{4,7},{5,6},{6,5},{7,4},{8,11},{9,10},{10,... | collective-permute-start | bytes 319496 | tf_op jit(solution)/shard_map/ppermute | solution.py:29
  6.7 1.5 %collective-permute-start.1 = (f32[32,1024]{1,0:T(8,128)}, f32[32,1024]{1,0:T(8,128)S(1)}, u32[]{:S(2)}, u32[]{:S(2)}) collective-permute-start(f32[32,1024]{1,0:T(8,128)} %refs_0_), channel_id=1, source_target_pairs={{0,16},{4,20},{8,24},{12,28},{16,0},{20,4},{24,8},{28,12},{1,17},{... | collective-permute-start | bytes 393224 | tf_op jit(solution)/shard_map/ppermute | solution.py:29
  8.2 1.5 %collective-permute-start = (f32[32,1024]{1,0:T(8,128)}, f32[32,1024]{1,0:T(8,128)S(1)}, u32[]{:S(2)}, u32[]{:S(2)}) collective-permute-start(f32[32,1024]{1,0:T(8,128)} %refs_0_), channel_id=1, source_target_pairs={{0,8},{4,12},{8,0},{12,4},{16,24},{20,28},{24,16},{28,20},{1,9},{5... | collective-permute-start | bytes 393224 | tf_op jit(solution)/shard_map/ppermute | solution.py:29
  9.7 0.5 collective-permute-start.2
  10.2 1.5 %collective-permute-start.3 = (f32[104,256]{1,0:T(8,128)S(1)}, f32[104,256]{1,0:T(8,128)S(1)}, u32[]{:S(2)}, u32[]{:S(2)}) collective-permute-start(f32[104,256]{1,0:T(8,128)S(1)} %pad_add_fusion.refs_4_), channel_id=1, source_target_pairs={{0,1},{1,0},{2,3},{3,2},{4,5},{5,4},{6,7},{7,6},{8,9},{9,8},{10,11... | collective-permute-start | bytes 319496 | tf_op jit(solution)/shard_map/ppermute | solution.py:29
  11.7 9.2 %shard_map.145 = (bf16[128,256,512]{2,1,0:T(8,128)(2,1)S(1)}, s32[512]{0:T(512)S(1)}, s32[128]{0:T(128)S(1)}, s32[1]{0:T(128)}) custom-call(s32[8]{0:T(128)} %count_in, s32[8,64]{1,0:T(8,128)} %column_in.1, f32[8,64,128,128]{3,2,1,0:T(8,128)} %tiles_ref.1), custom_call_target="tpu_custom_call" | custom-call | flops 100000000 | bytes 41943040 | tf_op jit(solution)/shard_map/pallas_call | solution.py:49
  21.1 0.5 collective-permute-start.7
  21.6 0.4 collective-permute-start.9
  22.1 0.3 collective-permute-done.6.refs_1_
  22.6 0.3 collective-permute-done.8.refs_5_
  23.1 3.7 %shard_map.146 = (f32[32,256]{1,0:T(8,128)S(1)}, f32[32,256]{1,0:T(8,128)S(1)}, f32[32,256]{1,0:T(8,128)S(1)}, f32[32,256]{1,0:T(8,128)S(1)}) custom-call(s32[2]{0:T(128)S(1)} %pad_add_fusion.1.ids_ref, s32[1]{0:T(128)} %get-tuple-element.85.total_ref, s32[512]{0:T(512)S(1)} %get-tuple-element.86.list_ref, s32[128]{0:T(128)S(1)} %get-tuple-element.87.row_ref, ...), custom_call_target="tpu_custom_call" | custom-call | flops 1000000000 | bytes 16777216 | tf_op jit(solution)/shard_map/pallas_call | solution.py:49
  26.8 0.6 collective-permute-start.10
  27.4 3.8 %collective-permute-start.11 = (f32[32,256]{1,0:T(8,128)S(1)}, f32[32,256]{1,0:T(8,128)S(1)}, u32[]{:S(2)}, u32[]{:S(2)}) collective-permute-start(f32[32,256]{1,0:T(8,128)S(1)} %get-tuple-element.95), channel_id=1, source_target_pairs={{0,2},{1,3},{2,0},{3,1},{4,6},{5,7},{6,4},{7,5},{8,10},{9,11},{10,... | collective-permute-start | bytes 98312 | tf_op jit(solution)/shard_map/ppermute | solution.py:29
  31.2 2.9 %collective-permute-done.11.refs_2_ = f32[32,256]{1,0:T(8,128)S(1)} collective-permute-done((f32[32,256]{1,0:T(8,128)S(1)}, f32[32,256]{1,0:T(8,128)S(1)}, u32[]{:S(2)}, u32[]{:S(2)}) %collective-permute-start.11) | collective-permute-done | bytes 32800 | tf_op jit(solution)/shard_map/ppermute | solution.py:29
  34.1 2.8 %collective-permute-done.12.refs_3_ = f32[32,256]{1,0:T(8,128)S(1)} collective-permute-done((f32[32,256]{1,0:T(8,128)S(1)}, f32[32,256]{1,0:T(8,128)S(1)}, u32[]{:S(2)}, u32[]{:S(2)}) %collective-permute-start.12) | collective-permute-done | bytes 32800 | tf_op jit(solution)/shard_map/ppermute | solution.py:29
  37.0 1.3 %shard_map.147 = (f32[128,256]{1,0:T(8,128)S(1)}, f32[256,256]{1,0:T(8,128)S(1)}, f32[256,256]{1,0:T(8,128)S(1)}, f32[256,172]{1,0:T(8,128)S(1)}, f32[48,256]{1,...) custom-call(s32[2]{0:T(128)S(1)} %pad_add_fusion.1.ids_ref, ...), custom_call_target="tpu_custom_call" | custom-call | flops 100000000 | bytes 2097152 | tf_op jit(solution)/shard_map/pallas_call | solution.py:49
  38.4 1.6 %collective-permute-start.14 = (f32[48,256]{1,0:T(8,128)S(1)}, f32[48,256]{1,0:T(8,128)S(1)}, u32[]{:S(2)}, u32[]{:S(2)}) collective-permute-start(f32[48,256]{1,0:T(8,128)S(1)} %get-tuple-element.103), channel_id=1, source_target_pairs={{0,2},{1,3},{2,0},{3,1},{4,6},{5,7},{6,4},{7,5},{8,10},{9,11},{10,... | collective-permute-start | bytes 147464 | tf_op jit(solution)/shard_map/ppermute | solution.py:29
  39.9 2.8 %collective-permute-start.15 = (f32[48,256]{1,0:T(8,128)S(1)}, f32[48,256]{1,0:T(8,128)S(1)}, u32[]{:S(2)}, u32[]{:S(2)}) collective-permute-start(f32[48,256]{1,0:T(8,128)S(1)} %get-tuple-element.104), channel_id=1, source_target_pairs={{0,3},{1,2},{2,1},{3,0},{4,7},{5,6},{6,5},{7,4},{8,11},{9,10},{10,... | collective-permute-start | bytes 147464 | tf_op jit(solution)/shard_map/ppermute | solution.py:29
  42.8 0.7 collective-permute-done.14.refs_2_
  43.5 2.3 %collective-permute-done.15.refs_3_ = f32[48,256]{1,0:T(8,128)S(1)} collective-permute-done((f32[48,256]{1,0:T(8,128)S(1)}, f32[48,256]{1,0:T(8,128)S(1)}, u32[]{:S(2)}, u32[]{:S(2)}) %collective-permute-start.15) | collective-permute-done | bytes 49184 | tf_op jit(solution)/shard_map/ppermute | solution.py:29
  45.8 3.6 %collective-permute-start.21 = (f32[4,48,256]{2,1,0:T(8,128)S(1)}, f32[4,48,256]{2,1,0:T(8,128)S(1)}, u32[]{:S(2)}, u32[]{:S(2)}) collective-permute-start(f32[4,48,256]{2,1,0:T(8,128)S(1)} %shard_map.148.refs_0_), channel_id=1, source_target_pairs={{0,24},{4,28},{8,16},{12,20},{16,8},{20,12},{24,0},{28,4},{1,25},{... | collective-permute-start | bytes 589832 | tf_op jit(solution)/shard_map/ppermute | solution.py:29
  49.5 1.2 collective-permute-start.19
  50.7 4.1 %collective-permute-done.21.refs_6_ = f32[4,48,256]{2,1,0:T(8,128)S(1)} collective-permute-done((f32[4,48,256]{2,1,0:T(8,128)S(1)}, f32[4,48,256]{2,1,0:T(8,128)S(1)}, u32[]{:S(2)}, u32[]{:S(2)}) %collective-permute-start.21) | collective-permute-done | bytes 196640 | tf_op jit(solution)/shard_map/ppermute | solution.py:29
  54.8 2.6 %collective-permute-done.19.refs_4_ = f32[4,48,256]{2,1,0:T(8,128)S(1)} collective-permute-done((f32[4,48,256]{2,1,0:T(8,128)S(1)}, f32[4,48,256]{2,1,0:T(8,128)S(1)}, u32[]{:S(2)}, u32[]{:S(2)}) %collective-permute-start.19) | collective-permute-done | bytes 196640 | tf_op jit(solution)/shard_map/ppermute | solution.py:29
  57.4 0.5 collective-permute-start.18
  57.9 0.9 collective-permute-done.20.refs_5_
  59.1 4.0 %shard_map.149 = (f32[24,1024]{1,0:T(8,128)S(1)}, f32[24,1024]{1,0:T(8,128)S(1)}, f32[24,128]{1,0:T(8,128)S(1)}) custom-call(s32[2]{0:T(128)S(1)} %pad_add_fusion.1.ids_ref, s32[1]{0:T(128)} %get-tuple-element.85.total_ref, s32[512]{0:T(512)S(1)} %get-tuple-element.86.list_ref, s32[128]{0:T(128)S(1)} %get-tuple-element.87.row_ref, ...), custom_call_target="tpu_custom_call" | custom-call | flops 1000000000 | bytes 16777216 | tf_op jit(solution)/shard_map/pallas_call | solution.py:49
  63.1 2.0 %collective-permute-start.25 = (f32[24,128]{1,0:T(8,128)S(1)}, f32[24,128]{1,0:T(8,128)S(1)}, u32[]{:S(2)}, u32[]{:S(2)}) collective-permute-start(f32[24,128]{1,0:T(8,128)S(1)} %get-tuple-element.107.refs_0_), channel_id=1, source_target_pairs={{0,3},{1,2},{2,1},{3,0},{4,7},{5,6},{6,5},{7,4},{8,11},{9,10},{10,... | collective-permute-start | bytes 36872 | tf_op jit(solution)/shard_map/ppermute | solution.py:29
  65.1 0.5 collective-permute-start.24
  65.6 1.9 %collective-permute-start.23 = (f32[24,128]{1,0:T(8,128)S(1)}, f32[24,128]{1,0:T(8,128)S(1)}, u32[]{:S(2)}, u32[]{:S(2)}) collective-permute-start(f32[24,128]{1,0:T(8,128)S(1)} %get-tuple-element.107.refs_0_), channel_id=1, source_target_pairs={{0,1},{1,0},{2,3},{3,2},{4,5},{5,4},{6,7},{7,6},{8,9},{9,8},{10,11... | collective-permute-start | bytes 36872 | tf_op jit(solution)/shard_map/ppermute | solution.py:29
  67.5 2.0 %collective-permute-start.28 = (f32[24,1024]{1,0:T(8,128)S(1)}, f32[24,1024]{1,0:T(8,128)S(1)}, u32[]{:S(2)}, u32[]{:S(2)}) collective-permute-start(f32[24,1024]{1,0:T(8,128)S(1)} %get-tuple-element.116.upper_ref.refs_0_), channel_id=1, source_target_pairs={{0,3},{1,2},{2,1},{3,0},{4,7},{5,6},{6,5},{7,4},{8,11},{9,10},{10,... | collective-permute-start | bytes 294920 | tf_op jit(solution)/shard_map/ppermute | solution.py:29
  69.5 2.4 %collective-permute-start.26 = (f32[24,1024]{1,0:T(8,128)S(1)}, f32[24,1024]{1,0:T(8,128)S(1)}, u32[]{:S(2)}, u32[]{:S(2)}) collective-permute-start(f32[24,1024]{1,0:T(8,128)S(1)} %get-tuple-element.116.upper_ref.refs_0_), channel_id=1, source_target_pairs={{0,1},{1,0},{2,3},{3,2},{4,5},{5,4},{6,7},{7,6},{8,9},{9,8},{10,11... | collective-permute-start | bytes 294920 | tf_op jit(solution)/shard_map/ppermute | solution.py:29
  71.9 3.1 %shard_map.150 = (f32[48,1024]{1,0:T(8,128)S(1)}, f32[48,1024]{1,0:T(8,128)S(1)}, f32[48,1024]{1,0:T(8,128)S(1)}, f32[48,1024]{1,0:T(8,128)S(1)}, f32[48,1024]{1...) custom-call(s32[2]{0:T(128)S(1)} %pad_add_fusion.1.ids_ref, ...), custom_call_target="tpu_custom_call" | custom-call | flops 1000000000 | bytes 16777216 | tf_op jit(solution)/shard_map/pallas_call | solution.py:49
  75.1 3.4 %collective-permute-done.27.refs_2_ = f32[24,1024]{1,0:T(8,128)S(1)} collective-permute-done((f32[24,1024]{1,0:T(8,128)S(1)}, f32[24,1024]{1,0:T(8,128)S(1)}, u32[]{:S(2)}, u32[]{:S(2)}) %collective-permute-start.27) | collective-permute-done | bytes 98336 | tf_op jit(solution)/shard_map/ppermute | solution.py:29
  78.5 0.5 collective-permute-start.30
  79.0 0.5 collective-permute-start.32
  79.5 0.4 collective-permute-done.29.refs_4_
  79.9 0.3 collective-permute-done.30.refs_5_
  80.4 0.3 collective-permute-done.32.refs_7_
  80.8 2.5 %collective-permute-start.36 = (f32[48,1024]{1,0:T(8,128)S(1)}, f32[48,1024]{1,0:T(8,128)S(1)}, u32[]{:S(2)}, u32[]{:S(2)}) collective-permute-start(f32[48,1024]{1,0:T(8,128)S(1)} %get-tuple-element.134), channel_id=1, source_target_pairs={{0,8},{4,12},{8,0},{12,4},{16,24},{20,28},{24,16},{28,20},{1,9},{5... | collective-permute-start | bytes 589832 | tf_op jit(solution)/shard_map/ppermute | solution.py:29
  83.3 1.5 %collective-permute-start.37 = (f32[48,1024]{1,0:T(8,128)S(1)}, f32[48,1024]{1,0:T(8,128)S(1)}, u32[]{:S(2)}, u32[]{:S(2)}) collective-permute-start(f32[48,1024]{1,0:T(8,128)S(1)} %get-tuple-element.135), channel_id=1, source_target_pairs={{0,16},{4,20},{8,24},{12,28},{16,0},{20,4},{24,8},{28,12},{1,17},{... | collective-permute-start | bytes 589832 | tf_op jit(solution)/shard_map/ppermute | solution.py:29
  84.8 2.2 %collective-permute-start.35 = (f32[24,1024]{1,0:T(8,128)S(1)}, f32[24,1024]{1,0:T(8,128)S(1)}, u32[]{:S(2)}, u32[]{:S(2)}) collective-permute-start(f32[24,1024]{1,0:T(8,128)S(1)} %get-tuple-element.132.lower_ref.refs_4_), channel_id=1, source_target_pairs={{0,3},{1,2},{2,1},{3,0},{4,7},{5,6},{6,5},{7,4},{8,11},{9,10},{10,... | collective-permute-start | bytes 294920 | tf_op jit(solution)/shard_map/ppermute | solution.py:29
  87.0 2.0 %collective-permute-done.36.refs_1_ = f32[48,1024]{1,0:T(8,128)S(1)} collective-permute-done((f32[48,1024]{1,0:T(8,128)S(1)}, f32[48,1024]{1,0:T(8,128)S(1)}, u32[]{:S(2)}, u32[]{:S(2)}) %collective-permute-start.36) | collective-permute-done | bytes 196640 | tf_op jit(solution)/shard_map/ppermute | solution.py:29
  89.2 5.0 %collective-permute-done.37.refs_2_ = f32[48,1024]{1,0:T(8,128)S(1)} collective-permute-done((f32[48,1024]{1,0:T(8,128)S(1)}, f32[48,1024]{1,0:T(8,128)S(1)}, u32[]{:S(2)}, u32[]{:S(2)}) %collective-permute-start.37) | collective-permute-done | bytes 196640 | tf_op jit(solution)/shard_map/ppermute | solution.py:29
  94.3 0.6 shard_map.153
  95.0 2.7 %collective-permute-start.40 = (f32[48,256]{1,0:T(8,128)S(1)}, f32[48,256]{1,0:T(8,128)S(1)}, u32[]{:S(2)}, u32[]{:S(2)}) collective-permute-start(f32[48,256]{1,0:T(8,128)S(1)} %get-tuple-element.139), channel_id=1, source_target_pairs={{0,2},{1,3},{2,0},{3,1},{4,6},{5,7},{6,4},{7,5},{8,10},{9,11},{10,... | collective-permute-start | bytes 147464 | tf_op jit(solution)/shard_map/ppermute | solution.py:29
  97.7 1.7 %collective-permute-start.41 = (f32[48,256]{1,0:T(8,128)S(1)}, f32[48,256]{1,0:T(8,128)S(1)}, u32[]{:S(2)}, u32[]{:S(2)}) collective-permute-start(f32[48,256]{1,0:T(8,128)S(1)} %get-tuple-element.140), channel_id=1, source_target_pairs={{0,3},{1,2},{2,1},{3,0},{4,7},{5,6},{6,5},{7,4},{8,11},{9,10},{10,... | collective-permute-start | bytes 147464 | tf_op jit(solution)/shard_map/ppermute | solution.py:29
  99.3 1.5 %shard_map.152 = f32[172,1024]{1,0:T(8,128)} custom-call(s32[2]{0:T(128)S(1)} %pad_add_fusion.1.ids_ref, f32[24,1024]{1,0:T(8,128)S(1)} %get-tuple-element.116.upper_ref.refs_0_, f32[24,1024]{1,0:T(8,128)S(1)} %collective-permute-done.26.refs_1_, f32[24,1024]{1,0:T(8,128)S(1)} %collective-permute-done.27.refs_2_, ...), custom_call_target="tpu_custom_call" | custom-call | bytes 2097152 | tf_op jit(solution)/shard_map/pallas_call | solution.py:49
  100.9 2.7 %collective-permute-done.41.refs_3_ = f32[48,256]{1,0:T(8,128)S(1)} collective-permute-done((f32[48,256]{1,0:T(8,128)S(1)}, f32[48,256]{1,0:T(8,128)S(1)}, u32[]{:S(2)}, u32[]{:S(2)}) %collective-permute-start.41) | collective-permute-done | bytes 49184 | tf_op jit(solution)/shard_map/ppermute | solution.py:29
  103.6 1.3 %shard_map.154 = (f32[4,40,256]{2,1,0:T(8,128)S(1)}, f32[4,40,256]{2,1,0:T(8,128)S(1)}) custom-call(s32[2]{0:T(128)S(1)} %pad_add_fusion.1.ids_ref, f32[128,256]{1,0:T(8,128)S(1)} %get-tuple-element.142.mixed_ref, f32[256,256]{1,0:T(8,128)S(1)} %get-tuple-element.143.hidden_ref, f32[256,256]{1,0:T(8,128)S(1)} %get-tuple-element.144.slope_ref, ...), custom_call_target="tpu_custom_call" | custom-call | flops 100000000 | bytes 2097152 | tf_op jit(solution)/shard_map/pallas_call | solution.py:49
  105.0 1.4 %collective-permute-done.42 = f32[4,40,256]{2,1,0:T(8,128)S(1)} collective-permute-done((f32[4,40,256]{2,1,0:T(8,128)S(1)}, f32[4,40,256]{2,1,0:T(8,128)S(1)}, u32[]{:S(2)}, u32[]{:S(2)}) %collective-permute-start.42) | collective-permute-done | bytes 163872 | tf_op jit(solution)/shard_map/ppermute | solution.py:29
  106.5 1.7 %collective-permute-start.45 = (f32[40,256]{1,0:T(8,128)S(1)}, f32[40,256]{1,0:T(8,128)S(1)}, u32[]{:S(2)}, u32[]{:S(2)}) collective-permute-start(f32[40,256]{1,0:T(8,128)S(1)} %get-tuple-element.159), channel_id=1, source_target_pairs={{0,3},{1,2},{2,1},{3,0},{4,7},{5,6},{6,5},{7,4},{8,11},{9,10},{10,... | collective-permute-start | bytes 122888 | tf_op jit(solution)/shard_map/ppermute | solution.py:29
  108.2 1.7 %collective-permute-start.44 = (f32[40,256]{1,0:T(8,128)S(1)}, f32[40,256]{1,0:T(8,128)S(1)}, u32[]{:S(2)}, u32[]{:S(2)}) collective-permute-start(f32[40,256]{1,0:T(8,128)S(1)} %get-tuple-element.160), channel_id=1, source_target_pairs={{0,2},{1,3},{2,0},{3,1},{4,6},{5,7},{6,4},{7,5},{8,10},{9,11},{10,... | collective-permute-start | bytes 122888 | tf_op jit(solution)/shard_map/ppermute | solution.py:29
  110.0 0.5 collective-permute-done.43
  110.5 2.2 %collective-permute-done.45 = f32[40,256]{1,0:T(8,128)S(1)} collective-permute-done((f32[40,256]{1,0:T(8,128)S(1)}, f32[40,256]{1,0:T(8,128)S(1)}, u32[]{:S(2)}, u32[]{:S(2)}) %collective-permute-start.45) | collective-permute-done | bytes 40992 | tf_op jit(solution)/shard_map/ppermute | solution.py:29
  112.7 1.5 %collective-permute-done.44 = f32[40,256]{1,0:T(8,128)S(1)} collective-permute-done((f32[40,256]{1,0:T(8,128)S(1)}, f32[40,256]{1,0:T(8,128)S(1)}, u32[]{:S(2)}, u32[]{:S(2)}) %collective-permute-start.44) | collective-permute-done | bytes 40992 | tf_op jit(solution)/shard_map/ppermute | solution.py:29
  114.2 1.2 %collective-permute-start.48 = (f32[40,256]{1,0:T(8,128)S(1)}, f32[40,256]{1,0:T(8,128)S(1)}, u32[]{:S(2)}, u32[]{:S(2)}) collective-permute-start(f32[40,256]{1,0:T(8,128)S(1)} %fusion.2), channel_id=1, source_target_pairs={{0,24},{4,28},{8,16},{12,20},{16,8},{20,12},{24,0},{28,4},{1,25},{... | collective-permute-start | bytes 122888 | tf_op jit(solution)/shard_map/ppermute | solution.py:29
  115.4 1.2 collective-permute-start.47
  116.6 1.1 collective-permute-start.46
  117.7 1.8 %collective-permute-done.48 = f32[40,256]{1,0:T(8,128)S(1)} collective-permute-done((f32[40,256]{1,0:T(8,128)S(1)}, f32[40,256]{1,0:T(8,128)S(1)}, u32[]{:S(2)}, u32[]{:S(2)}) %collective-permute-start.48) | collective-permute-done | bytes 40992 | tf_op jit(solution)/shard_map/ppermute | solution.py:29
  119.7 0.9 collective-permute-done.46
  120.7 1.2 collective-permute-done.49.other_ref
  121.9 1.3 %shard_map.155 = (f32[32,256]{1,0:T(8,128)}, f32[1,64]{1,0:T(1,128)}, f32[64,172]{1,0:T(8,128)}, f32[1,172]{1,0:T(1,128)}, f32[1,1]{1,0:T(1,128)}) custom-call(s32[2]{0:T(128)S(1)} %pad_add_fusion.1.ids_ref, f32[40,256]{1,0:T(8,128)S(1)} %add_add_fusion.mine_ref, f32[40,256]{1,0:T(8,128)S(1)} %collective-permute-done.49.other_ref), custom_call_target="tpu_custom_call" | custom-call | tf_op jit(solution)/shard_map/pallas_call | solution.py:49
  (61 shorter events, 2.3 us)
Async XLA Ops:
  0.6 20.4 %copy-start = (f32[32,1024]{1,0:T(8,128)S(1)}, f32[32,1024]{1,0:T(8,128)}, u32[]{:S(2)}) copy-start(f32[32,1024]{1,0:T(8,128)} %refs_0_) | copy-start | bytes 393220
  1.5 8.6 %collective-permute-start.5 = (f32[104,256]{1,0:T(8,128)S(1)}, f32[104,256]{1,0:T(8,128)S(1)}, u32[]{:S(2)}, u32[]{:S(2)}) collective-permute-start(f32[104,256]{1,0:T(8,128)S(1)} %pad_add_fusion.refs_4_), channel_id=1, source_target_pairs={{0,3},{1,2},{2,1},{3,0},{4,7},{5,6},{6,5},{7,4},{8,11},{9,10},{10,... | collective-permute-start | bytes 319496 | tf_op jit(solution)/shard_map/ppermute | solution.py:29
  6.7 14.3 %collective-permute-start.1 = (f32[32,1024]{1,0:T(8,128)}, f32[32,1024]{1,0:T(8,128)S(1)}, u32[]{:S(2)}, u32[]{:S(2)}) collective-permute-start(f32[32,1024]{1,0:T(8,128)} %refs_0_), channel_id=1, source_target_pairs={{0,16},{4,20},{8,24},{12,28},{16,0},{20,4},{24,8},{28,12},{1,17},{... | collective-permute-start | bytes 393224 | tf_op jit(solution)/shard_map/ppermute | solution.py:29
  8.2 12.8 %collective-permute-start = (f32[32,1024]{1,0:T(8,128)}, f32[32,1024]{1,0:T(8,128)S(1)}, u32[]{:S(2)}, u32[]{:S(2)}) collective-permute-start(f32[32,1024]{1,0:T(8,128)} %refs_0_), channel_id=1, source_target_pairs={{0,8},{4,12},{8,0},{12,4},{16,24},{20,28},{24,16},{28,20},{1,9},{5... | collective-permute-start | bytes 393224 | tf_op jit(solution)/shard_map/ppermute | solution.py:29
  9.7 11.3 %collective-permute-start.2 = (f32[32,1024]{1,0:T(8,128)}, f32[32,1024]{1,0:T(8,128)S(1)}, u32[]{:S(2)}, u32[]{:S(2)}) collective-permute-start(f32[32,1024]{1,0:T(8,128)} %refs_0_), channel_id=1, source_target_pairs={{0,24},{4,28},{8,16},{12,20},{16,8},{20,12},{24,0},{28,4},{1,25},{... | collective-permute-start | bytes 393224 | tf_op jit(solution)/shard_map/ppermute | solution.py:29
  10.1 10.8 %collective-permute-start.4 = (f32[104,256]{1,0:T(8,128)S(1)}, f32[104,256]{1,0:T(8,128)S(1)}, u32[]{:S(2)}, u32[]{:S(2)}) collective-permute-start(f32[104,256]{1,0:T(8,128)S(1)} %pad_add_fusion.refs_4_), channel_id=1, source_target_pairs={{0,2},{1,3},{2,0},{3,1},{4,6},{5,7},{6,4},{7,5},{8,10},{9,11},{10,... | collective-permute-start | bytes 319496 | tf_op jit(solution)/shard_map/ppermute | solution.py:29
  10.2 10.8 %collective-permute-start.3 = (f32[104,256]{1,0:T(8,128)S(1)}, f32[104,256]{1,0:T(8,128)S(1)}, u32[]{:S(2)}, u32[]{:S(2)}) collective-permute-start(f32[104,256]{1,0:T(8,128)S(1)} %pad_add_fusion.refs_4_), channel_id=1, source_target_pairs={{0,1},{1,0},{2,3},{3,2},{4,5},{5,4},{6,7},{7,6},{8,9},{9,8},{10,11... | collective-permute-start | bytes 319496 | tf_op jit(solution)/shard_map/ppermute | solution.py:29
  21.0 1.4 %collective-permute-start.6 = (f32[32,1024]{1,0:T(8,128)S(1)}, f32[32,1024]{1,0:T(8,128)S(1)}, u32[]{:S(2)}, u32[]{:S(2)}) collective-permute-start(f32[32,1024]{1,0:T(8,128)S(1)} %copy-done), channel_id=1, source_target_pairs={{0,4},{4,0},{8,12},{12,8},{16,20},{20,16},{24,28},{28,24},{1,5},{5... | collective-permute-start | bytes 393224 | tf_op jit(solution)/shard_map/ppermute | solution.py:29
  21.1 1.5 %collective-permute-start.7 = (f32[32,1024]{1,0:T(8,128)S(1)}, f32[32,1024]{1,0:T(8,128)S(1)}, u32[]{:S(2)}, u32[]{:S(2)}) collective-permute-start(f32[32,1024]{1,0:T(8,128)S(1)} %collective-permute-done.refs_2_), channel_id=1, source_target_pairs={{0,4},{4,0},{8,12},{12,8},{16,20},{20,16},{24,28},{28,24},{1,5},{5... | collective-permute-start | bytes 393224 | tf_op jit(solution)/shard_map/ppermute | solution.py:29
  21.6 1.3 %collective-permute-start.8 = (f32[32,1024]{1,0:T(8,128)S(1)}, f32[32,1024]{1,0:T(8,128)S(1)}, u32[]{:S(2)}, u32[]{:S(2)}) collective-permute-start(f32[32,1024]{1,0:T(8,128)S(1)} %collective-permute-done.1.refs_4_), channel_id=1, source_target_pairs={{0,4},{4,0},{8,12},{12,8},{16,20},{20,16},{24,28},{28,24},{1,5},{5... | collective-permute-start | bytes 393224 | tf_op jit(solution)/shard_map/ppermute | solution.py:29
  21.6 1.5 %collective-permute-start.9 = (f32[32,1024]{1,0:T(8,128)S(1)}, f32[32,1024]{1,0:T(8,128)S(1)}, u32[]{:S(2)}, u32[]{:S(2)}) collective-permute-start(f32[32,1024]{1,0:T(8,128)S(1)} %collective-permute-done.2.refs_6_), channel_id=1, source_target_pairs={{0,4},{4,0},{8,12},{12,8},{16,20},{20,16},{24,28},{28,24},{1,5},{5... | collective-permute-start | bytes 393224 | tf_op jit(solution)/shard_map/ppermute | solution.py:29
  26.8 4.5 %collective-permute-start.10 = (f32[32,256]{1,0:T(8,128)S(1)}, f32[32,256]{1,0:T(8,128)S(1)}, u32[]{:S(2)}, u32[]{:S(2)}) collective-permute-start(f32[32,256]{1,0:T(8,128)S(1)} %get-tuple-element.94), channel_id=1, source_target_pairs={{0,1},{1,0},{2,3},{3,2},{4,5},{5,4},{6,7},{7,6},{8,9},{9,8},{10,11... | collective-permute-start | bytes 98312 | tf_op jit(solution)/shard_map/ppermute | solution.py:29
  27.4 6.7 %collective-permute-start.11 = (f32[32,256]{1,0:T(8,128)S(1)}, f32[32,256]{1,0:T(8,128)S(1)}, u32[]{:S(2)}, u32[]{:S(2)}) collective-permute-start(f32[32,256]{1,0:T(8,128)S(1)} %get-tuple-element.95), channel_id=1, source_target_pairs={{0,2},{1,3},{2,0},{3,1},{4,6},{5,7},{6,4},{7,5},{8,10},{9,11},{10,... | collective-permute-start | bytes 98312 | tf_op jit(solution)/shard_map/ppermute | solution.py:29
  31.2 5.7 %collective-permute-start.12 = (f32[32,256]{1,0:T(8,128)S(1)}, f32[32,256]{1,0:T(8,128)S(1)}, u32[]{:S(2)}, u32[]{:S(2)}) collective-permute-start(f32[32,256]{1,0:T(8,128)S(1)} %get-tuple-element.96), channel_id=1, source_target_pairs={{0,3},{1,2},{2,1},{3,0},{4,7},{5,6},{6,5},{7,4},{8,11},{9,10},{10,... | collective-permute-start | bytes 98312 | tf_op jit(solution)/shard_map/ppermute | solution.py:29
  37.0 22.1 %copy-start.1 = (s32[1024]{0:T(1024)S(1)}, s32[1024]{0:T(1024)}, u32[]{:S(2)}) copy-start(s32[1024]{0:T(1024)} %param.14) | copy-start | bytes 12292
  37.0 22.1 %copy-start.3 = (f32[172]{0:T(256)S(1)}, f32[172]{0:T(256)}, u32[]{:S(2)}) copy-start(f32[172]{0:T(256)} %param.19) | copy-start | bytes 2068
  38.3 4.5 %collective-permute-start.13 = (f32[48,256]{1,0:T(8,128)S(1)}, f32[48,256]{1,0:T(8,128)S(1)}, u32[]{:S(2)}, u32[]{:S(2)}) collective-permute-start(f32[48,256]{1,0:T(8,128)S(1)} %get-tuple-element.102), channel_id=1, source_target_pairs={{0,1},{1,0},{2,3},{3,2},{4,5},{5,4},{6,7},{7,6},{8,9},{9,8},{10,11... | collective-permute-start | bytes 147464 | tf_op jit(solution)/shard_map/ppermute | solution.py:29
  38.4 5.1 %collective-permute-start.14 = (f32[48,256]{1,0:T(8,128)S(1)}, f32[48,256]{1,0:T(8,128)S(1)}, u32[]{:S(2)}, u32[]{:S(2)}) collective-permute-start(f32[48,256]{1,0:T(8,128)S(1)} %get-tuple-element.103), channel_id=1, source_target_pairs={{0,2},{1,3},{2,0},{3,1},{4,6},{5,7},{6,4},{7,5},{8,10},{9,11},{10,... | collective-permute-start | bytes 147464 | tf_op jit(solution)/shard_map/ppermute | solution.py:29
  39.9 5.9 %collective-permute-start.15 = (f32[48,256]{1,0:T(8,128)S(1)}, f32[48,256]{1,0:T(8,128)S(1)}, u32[]{:S(2)}, u32[]{:S(2)}) collective-permute-start(f32[48,256]{1,0:T(8,128)S(1)} %get-tuple-element.104), channel_id=1, source_target_pairs={{0,3},{1,2},{2,1},{3,0},{4,7},{5,6},{6,5},{7,4},{8,11},{9,10},{10,... | collective-permute-start | bytes 147464 | tf_op jit(solution)/shard_map/ppermute | solution.py:29
  45.8 26.1 %copy-start.2 = (s32[1024]{0:T(1024)S(1)}, s32[1024]{0:T(1024)}, u32[]{:S(2)}) copy-start(s32[1024]{0:T(1024)} %param.15) | copy-start | bytes 12292
  45.8 8.9 %collective-permute-start.21 = (f32[4,48,256]{2,1,0:T(8,128)S(1)}, f32[4,48,256]{2,1,0:T(8,128)S(1)}, u32[]{:S(2)}, u32[]{:S(2)}) collective-permute-start(f32[4,48,256]{2,1,0:T(8,128)S(1)} %shard_map.148.refs_0_), channel_id=1, source_target_pairs={{0,24},{4,28},{8,16},{12,20},{16,8},{20,12},{24,0},{28,4},{1,25},{... | collective-permute-start | bytes 589832 | tf_op jit(solution)/shard_map/ppermute | solution.py:29
  49.5 7.9 %collective-permute-start.19 = (f32[4,48,256]{2,1,0:T(8,128)S(1)}, f32[4,48,256]{2,1,0:T(8,128)S(1)}, u32[]{:S(2)}, u32[]{:S(2)}) collective-permute-start(f32[4,48,256]{2,1,0:T(8,128)S(1)} %shard_map.148.refs_0_), channel_id=1, source_target_pairs={{0,16},{4,20},{8,24},{12,28},{16,0},{20,4},{24,8},{28,12},{1,17},{... | collective-permute-start | bytes 589832 | tf_op jit(solution)/shard_map/ppermute | solution.py:29
  50.7 6.7 %collective-permute-start.17 = (f32[4,48,256]{2,1,0:T(8,128)S(1)}, f32[4,48,256]{2,1,0:T(8,128)S(1)}, u32[]{:S(2)}, u32[]{:S(2)}) collective-permute-start(f32[4,48,256]{2,1,0:T(8,128)S(1)} %shard_map.148.refs_0_), channel_id=1, source_target_pairs={{0,8},{4,12},{8,0},{12,4},{16,24},{20,28},{24,16},{28,20},{1,9},{5... | collective-permute-start | bytes 589832 | tf_op jit(solution)/shard_map/ppermute | solution.py:29
  50.7 7.2 %collective-permute-start.16 = (f32[4,48,256]{2,1,0:T(8,128)S(1)}, f32[4,48,256]{2,1,0:T(8,128)S(1)}, u32[]{:S(2)}, u32[]{:S(2)}) collective-permute-start(f32[4,48,256]{2,1,0:T(8,128)S(1)} %shard_map.148.refs_0_), channel_id=1, source_target_pairs={{0,4},{4,0},{8,12},{12,8},{16,20},{20,16},{24,28},{28,24},{1,5},{5... | collective-permute-start | bytes 589832 | tf_op jit(solution)/shard_map/ppermute | solution.py:29
  54.8 3.1 %collective-permute-start.22 = (f32[4,48,256]{2,1,0:T(8,128)S(1)}, f32[4,48,256]{2,1,0:T(8,128)S(1)}, u32[]{:S(2)}, u32[]{:S(2)}) collective-permute-start(f32[4,48,256]{2,1,0:T(8,128)S(1)} %collective-permute-done.21.refs_6_), channel_id=1, source_target_pairs={{0,4},{4,0},{8,12},{12,8},{16,20},{20,16},{24,28},{28,24},{1,5},{5... | collective-permute-start | bytes 589832 | tf_op jit(solution)/shard_map/ppermute | solution.py:29
  57.4 1.4 %collective-permute-start.20 = (f32[4,48,256]{2,1,0:T(8,128)S(1)}, f32[4,48,256]{2,1,0:T(8,128)S(1)}, u32[]{:S(2)}, u32[]{:S(2)}) collective-permute-start(f32[4,48,256]{2,1,0:T(8,128)S(1)} %collective-permute-done.19.refs_4_), channel_id=1, source_target_pairs={{0,4},{4,0},{8,12},{12,8},{16,20},{20,16},{24,28},{28,24},{1,5},{5... | collective-permute-start | bytes 589832 | tf_op jit(solution)/shard_map/ppermute | solution.py:29
  57.4 1.7 %collective-permute-start.18 = (f32[4,48,256]{2,1,0:T(8,128)S(1)}, f32[4,48,256]{2,1,0:T(8,128)S(1)}, u32[]{:S(2)}, u32[]{:S(2)}) collective-permute-start(f32[4,48,256]{2,1,0:T(8,128)S(1)} %collective-permute-done.17.refs_2_), channel_id=1, source_target_pairs={{0,4},{4,0},{8,12},{12,8},{16,20},{20,16},{24,28},{28,24},{1,5},{5... | collective-permute-start | bytes 589832 | tf_op jit(solution)/shard_map/ppermute | solution.py:29
  63.1 6.4 %collective-permute-start.25 = (f32[24,128]{1,0:T(8,128)S(1)}, f32[24,128]{1,0:T(8,128)S(1)}, u32[]{:S(2)}, u32[]{:S(2)}) collective-permute-start(f32[24,128]{1,0:T(8,128)S(1)} %get-tuple-element.107.refs_0_), channel_id=1, source_target_pairs={{0,3},{1,2},{2,1},{3,0},{4,7},{5,6},{6,5},{7,4},{8,11},{9,10},{10,... | collective-permute-start | bytes 36872 | tf_op jit(solution)/shard_map/ppermute | solution.py:29
  65.1 6.8 %collective-permute-start.24 = (f32[24,128]{1,0:T(8,128)S(1)}, f32[24,128]{1,0:T(8,128)S(1)}, u32[]{:S(2)}, u32[]{:S(2)}) collective-permute-start(f32[24,128]{1,0:T(8,128)S(1)} %get-tuple-element.107.refs_0_), channel_id=1, source_target_pairs={{0,2},{1,3},{2,0},{3,1},{4,6},{5,7},{6,4},{7,5},{8,10},{9,11},{10,... | collective-permute-start | bytes 36872 | tf_op jit(solution)/shard_map/ppermute | solution.py:29
  65.6 6.3 %collective-permute-start.23 = (f32[24,128]{1,0:T(8,128)S(1)}, f32[24,128]{1,0:T(8,128)S(1)}, u32[]{:S(2)}, u32[]{:S(2)}) collective-permute-start(f32[24,128]{1,0:T(8,128)S(1)} %get-tuple-element.107.refs_0_), channel_id=1, source_target_pairs={{0,1},{1,0},{2,3},{3,2},{4,5},{5,4},{6,7},{7,6},{8,9},{9,8},{10,11... | collective-permute-start | bytes 36872 | tf_op jit(solution)/shard_map/ppermute | solution.py:29
  67.5 7.5 %collective-permute-start.28 = (f32[24,1024]{1,0:T(8,128)S(1)}, f32[24,1024]{1,0:T(8,128)S(1)}, u32[]{:S(2)}, u32[]{:S(2)}) collective-permute-start(f32[24,1024]{1,0:T(8,128)S(1)} %get-tuple-element.116.upper_ref.refs_0_), channel_id=1, source_target_pairs={{0,3},{1,2},{2,1},{3,0},{4,7},{5,6},{6,5},{7,4},{8,11},{9,10},{10,... | collective-permute-start | bytes 294920 | tf_op jit(solution)/shard_map/ppermute | solution.py:29
  69.5 8.9 %collective-permute-start.27 = (f32[24,1024]{1,0:T(8,128)S(1)}, f32[24,1024]{1,0:T(8,128)S(1)}, u32[]{:S(2)}, u32[]{:S(2)}) collective-permute-start(f32[24,1024]{1,0:T(8,128)S(1)} %get-tuple-element.116.upper_ref.refs_0_), channel_id=1, source_target_pairs={{0,2},{1,3},{2,0},{3,1},{4,6},{5,7},{6,4},{7,5},{8,10},{9,11},{10,... | collective-permute-start | bytes 294920 | tf_op jit(solution)/shard_map/ppermute | solution.py:29
  69.5 8.9 %collective-permute-start.26 = (f32[24,1024]{1,0:T(8,128)S(1)}, f32[24,1024]{1,0:T(8,128)S(1)}, u32[]{:S(2)}, u32[]{:S(2)}) collective-permute-start(f32[24,1024]{1,0:T(8,128)S(1)} %get-tuple-element.116.upper_ref.refs_0_), channel_id=1, source_target_pairs={{0,1},{1,0},{2,3},{3,2},{4,5},{5,4},{6,7},{7,6},{8,9},{9,8},{10,11... | collective-permute-start | bytes 294920 | tf_op jit(solution)/shard_map/ppermute | solution.py:29
  78.4 1.4 %collective-permute-start.29 = (f32[48,1024]{1,0:T(8,128)S(1)}, f32[48,1024]{1,0:T(8,128)S(1)}, u32[]{:S(2)}, u32[]{:S(2)}) collective-permute-start(f32[48,1024]{1,0:T(8,128)S(1)} %get-tuple-element.124), channel_id=1, source_target_pairs={{0,4},{4,0},{8,12},{12,8},{16,20},{20,16},{24,28},{28,24},{1,5},{5... | collective-permute-start | bytes 589832 | tf_op jit(solution)/shard_map/ppermute | solution.py:29
  78.5 1.7 %collective-permute-start.30 = (f32[48,1024]{1,0:T(8,128)S(1)}, f32[48,1024]{1,0:T(8,128)S(1)}, u32[]{:S(2)}, u32[]{:S(2)}) collective-permute-start(f32[48,1024]{1,0:T(8,128)S(1)} %get-tuple-element.125), channel_id=1, source_target_pairs={{0,4},{4,0},{8,12},{12,8},{16,20},{20,16},{24,28},{28,24},{1,5},{5... | collective-permute-start | bytes 589832 | tf_op jit(solution)/shard_map/ppermute | solution.py:29
  78.9 1.5 %collective-permute-start.31 = (f32[48,1024]{1,0:T(8,128)S(1)}, f32[48,1024]{1,0:T(8,128)S(1)}, u32[]{:S(2)}, u32[]{:S(2)}) collective-permute-start(f32[48,1024]{1,0:T(8,128)S(1)} %get-tuple-element.126), channel_id=1, source_target_pairs={{0,4},{4,0},{8,12},{12,8},{16,20},{20,16},{24,28},{28,24},{1,5},{5... | collective-permute-start | bytes 589832 | tf_op jit(solution)/shard_map/ppermute | solution.py:29
  79.0 1.7 %collective-permute-start.32 = (f32[48,1024]{1,0:T(8,128)S(1)}, f32[48,1024]{1,0:T(8,128)S(1)}, u32[]{:S(2)}, u32[]{:S(2)}) collective-permute-start(f32[48,1024]{1,0:T(8,128)S(1)} %get-tuple-element.127), channel_id=1, source_target_pairs={{0,4},{4,0},{8,12},{12,8},{16,20},{20,16},{24,28},{28,24},{1,5},{5... | collective-permute-start | bytes 589832 | tf_op jit(solution)/shard_map/ppermute | solution.py:29
  80.8 8.2 %collective-permute-start.36 = (f32[48,1024]{1,0:T(8,128)S(1)}, f32[48,1024]{1,0:T(8,128)S(1)}, u32[]{:S(2)}, u32[]{:S(2)}) collective-permute-start(f32[48,1024]{1,0:T(8,128)S(1)} %get-tuple-element.134), channel_id=1, source_target_pairs={{0,8},{4,12},{8,0},{12,4},{16,24},{20,28},{24,16},{28,20},{1,9},{5... | collective-permute-start | bytes 589832 | tf_op jit(solution)/shard_map/ppermute | solution.py:29
  83.3 11.0 %collective-permute-start.37 = (f32[48,1024]{1,0:T(8,128)S(1)}, f32[48,1024]{1,0:T(8,128)S(1)}, u32[]{:S(2)}, u32[]{:S(2)}) collective-permute-start(f32[48,1024]{1,0:T(8,128)S(1)} %get-tuple-element.135), channel_id=1, source_target_pairs={{0,16},{4,20},{8,24},{12,28},{16,0},{20,4},{24,8},{28,12},{1,17},{... | collective-permute-start | bytes 589832 | tf_op jit(solution)/shard_map/ppermute | solution.py:29
  84.8 9.4 %collective-permute-start.38 = (f32[48,1024]{1,0:T(8,128)S(1)}, f32[48,1024]{1,0:T(8,128)S(1)}, u32[]{:S(2)}, u32[]{:S(2)}) collective-permute-start(f32[48,1024]{1,0:T(8,128)S(1)} %get-tuple-element.136), channel_id=1, source_target_pairs={{0,24},{4,28},{8,16},{12,20},{16,8},{20,12},{24,0},{28,4},{1,25},{... | collective-permute-start | bytes 589832 | tf_op jit(solution)/shard_map/ppermute | solution.py:29
  84.8 12.8 %collective-permute-start.35 = (f32[24,1024]{1,0:T(8,128)S(1)}, f32[24,1024]{1,0:T(8,128)S(1)}, u32[]{:S(2)}, u32[]{:S(2)}) collective-permute-start(f32[24,1024]{1,0:T(8,128)S(1)} %get-tuple-element.132.lower_ref.refs_4_), channel_id=1, source_target_pairs={{0,3},{1,2},{2,1},{3,0},{4,7},{5,6},{6,5},{7,4},{8,11},{9,10},{10,... | collective-permute-start | bytes 294920 | tf_op jit(solution)/shard_map/ppermute | solution.py:29
  87.0 12.3 %collective-permute-start.34 = (f32[24,1024]{1,0:T(8,128)S(1)}, f32[24,1024]{1,0:T(8,128)S(1)}, u32[]{:S(2)}, u32[]{:S(2)}) collective-permute-start(f32[24,1024]{1,0:T(8,128)S(1)} %get-tuple-element.132.lower_ref.refs_4_), channel_id=1, source_target_pairs={{0,2},{1,3},{2,0},{3,1},{4,6},{5,7},{6,4},{7,5},{8,10},{9,11},{10,... | collective-permute-start | bytes 294920 | tf_op jit(solution)/shard_map/ppermute | solution.py:29
  89.0 10.4 %collective-permute-start.33 = (f32[24,1024]{1,0:T(8,128)S(1)}, f32[24,1024]{1,0:T(8,128)S(1)}, u32[]{:S(2)}, u32[]{:S(2)}) collective-permute-start(f32[24,1024]{1,0:T(8,128)S(1)} %get-tuple-element.132.lower_ref.refs_4_), channel_id=1, source_target_pairs={{0,1},{1,0},{2,3},{3,2},{4,5},{5,4},{6,7},{7,6},{8,9},{9,8},{10,11... | collective-permute-start | bytes 294920 | tf_op jit(solution)/shard_map/ppermute | solution.py:29
  94.9 6.0 %collective-permute-start.39 = (f32[48,256]{1,0:T(8,128)S(1)}, f32[48,256]{1,0:T(8,128)S(1)}, u32[]{:S(2)}, u32[]{:S(2)}) collective-permute-start(f32[48,256]{1,0:T(8,128)S(1)} %get-tuple-element.138), channel_id=1, source_target_pairs={{0,1},{1,0},{2,3},{3,2},{4,5},{5,4},{6,7},{7,6},{8,9},{9,8},{10,11... | collective-permute-start | bytes 147464 | tf_op jit(solution)/shard_map/ppermute | solution.py:29
  95.0 5.9 %collective-permute-start.40 = (f32[48,256]{1,0:T(8,128)S(1)}, f32[48,256]{1,0:T(8,128)S(1)}, u32[]{:S(2)}, u32[]{:S(2)}) collective-permute-start(f32[48,256]{1,0:T(8,128)S(1)} %get-tuple-element.139), channel_id=1, source_target_pairs={{0,2},{1,3},{2,0},{3,1},{4,6},{5,7},{6,4},{7,5},{8,10},{9,11},{10,... | collective-permute-start | bytes 147464 | tf_op jit(solution)/shard_map/ppermute | solution.py:29
  97.7 5.9 %collective-permute-start.41 = (f32[48,256]{1,0:T(8,128)S(1)}, f32[48,256]{1,0:T(8,128)S(1)}, u32[]{:S(2)}, u32[]{:S(2)}) collective-permute-start(f32[48,256]{1,0:T(8,128)S(1)} %get-tuple-element.140), channel_id=1, source_target_pairs={{0,3},{1,2},{2,1},{3,0},{4,7},{5,6},{6,5},{7,4},{8,11},{9,10},{10,... | collective-permute-start | bytes 147464 | tf_op jit(solution)/shard_map/ppermute | solution.py:29
  104.9 1.5 %collective-permute-start.42 = (f32[4,40,256]{2,1,0:T(8,128)S(1)}, f32[4,40,256]{2,1,0:T(8,128)S(1)}, u32[]{:S(2)}, u32[]{:S(2)}) collective-permute-start(f32[4,40,256]{2,1,0:T(8,128)S(1)} %get-tuple-element.152), channel_id=1, source_target_pairs={{0,4},{4,0},{8,12},{12,8},{16,20},{20,16},{24,28},{28,24},{1,5},{5... | collective-permute-start | bytes 491528 | tf_op jit(solution)/shard_map/ppermute | solution.py:29
  106.4 4.1 %collective-permute-start.43 = (f32[40,256]{1,0:T(8,128)S(1)}, f32[40,256]{1,0:T(8,128)S(1)}, u32[]{:S(2)}, u32[]{:S(2)}) collective-permute-start(f32[40,256]{1,0:T(8,128)S(1)} %get-tuple-element.158), channel_id=1, source_target_pairs={{0,1},{1,0},{2,3},{3,2},{4,5},{5,4},{6,7},{7,6},{8,9},{9,8},{10,11... | collective-permute-start | bytes 122888 | tf_op jit(solution)/shard_map/ppermute | solution.py:29
  106.5 6.2 %collective-permute-start.45 = (f32[40,256]{1,0:T(8,128)S(1)}, f32[40,256]{1,0:T(8,128)S(1)}, u32[]{:S(2)}, u32[]{:S(2)}) collective-permute-start(f32[40,256]{1,0:T(8,128)S(1)} %get-tuple-element.159), channel_id=1, source_target_pairs={{0,3},{1,2},{2,1},{3,0},{4,7},{5,6},{6,5},{7,4},{8,11},{9,10},{10,... | collective-permute-start | bytes 122888 | tf_op jit(solution)/shard_map/ppermute | solution.py:29
  108.2 5.9 %collective-permute-start.44 = (f32[40,256]{1,0:T(8,128)S(1)}, f32[40,256]{1,0:T(8,128)S(1)}, u32[]{:S(2)}, u32[]{:S(2)}) collective-permute-start(f32[40,256]{1,0:T(8,128)S(1)} %get-tuple-element.160), channel_id=1, source_target_pairs={{0,2},{1,3},{2,0},{3,1},{4,6},{5,7},{6,4},{7,5},{8,10},{9,11},{10,... | collective-permute-start | bytes 122888 | tf_op jit(solution)/shard_map/ppermute | solution.py:29
  114.2 5.3 %collective-permute-start.48 = (f32[40,256]{1,0:T(8,128)S(1)}, f32[40,256]{1,0:T(8,128)S(1)}, u32[]{:S(2)}, u32[]{:S(2)}) collective-permute-start(f32[40,256]{1,0:T(8,128)S(1)} %fusion.2), channel_id=1, source_target_pairs={{0,24},{4,28},{8,16},{12,20},{16,8},{20,12},{24,0},{28,4},{1,25},{... | collective-permute-start | bytes 122888 | tf_op jit(solution)/shard_map/ppermute | solution.py:29
  115.4 4.3 %collective-permute-start.47 = (f32[40,256]{1,0:T(8,128)S(1)}, f32[40,256]{1,0:T(8,128)S(1)}, u32[]{:S(2)}, u32[]{:S(2)}) collective-permute-start(f32[40,256]{1,0:T(8,128)S(1)} %fusion.2), channel_id=1, source_target_pairs={{0,16},{4,20},{8,24},{12,28},{16,0},{20,4},{24,8},{28,12},{1,17},{... | collective-permute-start | bytes 122888 | tf_op jit(solution)/shard_map/ppermute | solution.py:29
  116.6 4.0 %collective-permute-start.46 = (f32[40,256]{1,0:T(8,128)S(1)}, f32[40,256]{1,0:T(8,128)S(1)}, u32[]{:S(2)}, u32[]{:S(2)}) collective-permute-start(f32[40,256]{1,0:T(8,128)S(1)} %fusion.2), channel_id=1, source_target_pairs={{0,8},{4,12},{8,0},{12,4},{16,24},{20,28},{24,16},{28,20},{1,9},{5... | collective-permute-start | bytes 122888 | tf_op jit(solution)/shard_map/ppermute | solution.py:29
  120.6 1.3 %collective-permute-start.49 = (f32[40,256]{1,0:T(8,128)S(1)}, f32[40,256]{1,0:T(8,128)S(1)}, u32[]{:S(2)}, u32[]{:S(2)}) collective-permute-start(f32[40,256]{1,0:T(8,128)S(1)} %add_add_fusion.mine_ref), channel_id=1, source_target_pairs={{0,4},{4,0},{8,12},{12,8},{16,20},{20,16},{24,28},{28,24},{1,5},{5... | collective-permute-start | bytes 122888 | tf_op jit(solution)/shard_map/ppermute | solution.py:29
